TPU v7x, 512 devices: a whole 4x4x16 slice. The times are simulated.
512 devices in a mesh: dp: 64 (over x, z_hi, y, core), fsdp: 8 (over z_lo).
Axes of the slice: x: 4, y: 4, z: 16 (z_hi: 2, z_lo: 8; z = z_hi * 8 + z_lo), core: 2. Of those that a mesh axis runs over, the one named last changes fastest.
Arguments:
- image_features: bfloat16 [196608, 1152], P(('dp', 'fsdp')), may hold values from -24 to 24
- head_weight: bfloat16 [1152, 1152], P('fsdp'), may hold values from -0.0048828125 to 0.0048828125
- text_embeds: bfloat16 [196608, 1152], P(('dp', 'fsdp')), may hold values from -0.17675781 to 0.17675781
- partner: int32 [196608], P(('dp', 'fsdp')), may hold values from 0 to 196607, as said below
- logit_scale: float32 [1], replicated, may hold values from 1.5 to 2.5
- logit_bias: float32 [1], replicated, may hold values from -4 to -1
Outputs:
- text_grad: bfloat16 [196608, 1152], P(('dp', 'fsdp'))
- head_grad: float32 [1152, 1152], P('fsdp')
Inputs may be any that keep to these rules, and one draw needn't show every extreme that they name: The partner of an image in block (p, q) is a text of block ((p + k) mod 64, q) for some k from 0 to 3.
All inputs are finite; a program needn't handle non-finite values.
Results may differ from a plain program's by a relative error of at most 0.015.
Values may be sent and summed in bfloat16 or wider, within the bound.
No kernel may reach another device: no remote copies, remote signals or barrier semaphores. Data moves between devices by JAX's collectives and lax.ppermute only.
A program may use at most 64 MiB of HBM per device.

v0:
```python
import jax
import jax.numpy as jnp
from jax import lax
from jax.sharding import PartitionSpec as P

STEPS = 4


def passed_along(block, axis, distance):
    devices = range(lax.axis_size(axis))
    route = [((i - distance) % len(devices), i) for i in devices]
    return lax.ppermute(block, axis, route)


def on_device(image_features, head_weight, text_embeds, partner, logit_scale, logit_bias):
    rows = image_features.shape[0]
    columns = image_features
    projected = jnp.dot(
        columns,
        lax.all_gather(head_weight, "fsdp", axis=0, tiled=True),
        preferred_element_type=jnp.float32,
    )
    img_norm = jnp.sqrt(jnp.sum(projected * projected, axis=1, keepdims=True) + 1e-06)
    unit_f = projected / img_norm
    unit_img = unit_f.astype(jnp.bfloat16)
    text_f = text_embeds.astype(jnp.float32)
    txt_norm = jnp.sqrt(jnp.sum(text_f * text_f, axis=1, keepdims=True) + 1e-06)
    unit_t = text_f / txt_norm
    unit_txt = unit_t.astype(jnp.bfloat16)
    scale = jnp.exp(logit_scale[0])
    bias = logit_bias[0]
    width_dp = lax.axis_size("dp")
    width_fsdp = lax.axis_size("fsdp")
    place = lax.axis_index("dp")
    lane = lax.axis_index("fsdp")
    offsets = lax.iota(jnp.int32, rows)

    def pair_terms(visitor, ahead):
        owner_ids = ((place + ahead) % width_dp * width_fsdp + lane) * rows + offsets
        logits = (
            scale * jnp.einsum("ie,je->ij", unit_img, visitor, preferred_element_type=jnp.float32)
            + bias
        )
        sign = jnp.where(partner[:, None] == owner_ids[None, :], 1.0, -1.0)
        weights = (-sign * jax.nn.sigmoid(-sign * logits)).astype(jnp.bfloat16)
        grad_img = scale * jnp.dot(weights, visitor, preferred_element_type=jnp.float32)
        grad_txt = scale * jnp.einsum(
            "ij,ie->je", weights, unit_img, preferred_element_type=jnp.float32
        )
        return (grad_img, grad_txt)

    img_grad, txt_grad = pair_terms(unit_txt, 0)
    visitor = unit_txt
    carried = txt_grad
    for ahead in range(1, STEPS):
        visitor = passed_along(visitor, "dp", -1)
        grad_img, grad_txt = pair_terms(visitor, ahead)
        img_grad = img_grad + grad_img
        if ahead == 1:
            carried = grad_txt
        else:
            carried = (
                passed_along(carried.astype(jnp.bfloat16), "dp", -1).astype(carried.dtype)
                + grad_txt
            )
    txt_grad = txt_grad + passed_along(carried.astype(jnp.bfloat16), "dp", STEPS - 1).astype(
        carried.dtype
    )
    proj_grad = (
        (img_grad - unit_f * jnp.sum(unit_f * img_grad, axis=1, keepdims=True)) / img_norm
    ).astype(jnp.bfloat16)
    text_grad = (
        (txt_grad - unit_t * jnp.sum(unit_t * txt_grad, axis=1, keepdims=True)) / txt_norm
    ).astype(jnp.bfloat16)
    columns = image_features
    share = lax.psum_scatter(
        jnp.einsum("rd,re->de", columns, proj_grad, preferred_element_type=jnp.float32).astype(
            jnp.bfloat16
        ),
        "fsdp",
        scatter_dimension=0,
        tiled=True,
    ).astype(jnp.float32)
    head_grad = lax.psum(share, "dp")
    return (text_grad, head_grad)


def solution(mesh):
    in_specs = (
        P(("dp", "fsdp"), None),
        P("fsdp", None),
        P(("dp", "fsdp"), None),
        P(("dp", "fsdp")),
        P(),
        P(),
    )
    out_specs = (P(("dp", "fsdp"), None), P("fsdp", None))
    return jax.shard_map(
        on_device, mesh=mesh, in_specs=in_specs, out_specs=out_specs, check_vma=False
    )
```

profile of v0, /device:TPU:32, one launch (start us, length us, event | category | flops | bytes accessed | tf_op | source)
XLA Modules:
  0.0 960.9 jit_solution(17579871105465727845)
XLA Ops:
  7.2 0.0 copy-start
  7.2 0.0 copy-start.1
  7.2 0.0 all-gather.2.cloned.1.call-start
  7.2 0.7 all-gather.2.cloned.1.call-update
  7.9 0.0 reduce-scatter.4.cloned.1.call-start
  8.0 1.4 fusion.3
  9.4 0.0 copy-done.1
  9.4 0.3 fusion.38
  9.7 18.9 %collective-permute-start = (bf16[384,1152]{1,0:T(8,128)(2,1)S(1)}, bf16[384,1152]{1,0:T(8,128)(2,1)S(1)}, u32[]{:S(2)}, u32[]{:S(2)}) collective-permute-start(bf16[384,1152]{1,0:T(8,128)(2,1)S(1)} %fusion.38), channel_id=1, source_target_pairs={{8,0},{16,8},{24,16},{32,24},{40,32},{48,40},{56,48},{64,56},{72,6... | collective-permute-start | bytes 2654216 | tf_op jit(solution)/shard_map/ppermute | solution.py:12
  28.6 83.4 %collective-permute-done = bf16[384,1152]{1,0:T(8,128)(2,1)S(1)} collective-permute-done((bf16[384,1152]{1,0:T(8,128)(2,1)S(1)}, bf16[384,1152]{1,0:T(8,128)(2,1)S(1)}, u32[]{:S(2)}, u32[]{:S(2)}) %collective-permute-start) | collective-permute-done | bytes 884768 | tf_op jit(solution)/shard_map/ppermute | solution.py:12
  112.0 17.5 %collective-permute-start.2 = (bf16[384,1152]{1,0:T(8,128)(2,1)S(1)}, bf16[384,1152]{1,0:T(8,128)(2,1)}, u32[]{:S(2)}, u32[]{:S(2)}) collective-permute-start(bf16[384,1152]{1,0:T(8,128)(2,1)S(1)} %collective-permute-done), channel_id=1, source_target_pairs={{8,0},{16,8},{24,16},{32,24},{40,32},{48,40},{56,48},{64,56},{72,6... | collective-permute-start | bytes 2654216 | tf_op jit(solution)/shard_map/ppermute | solution.py:12
  130.9 0.6 iota_add_fusion.1
  131.5 52.6 %collective-permute-done.2 = bf16[384,1152]{1,0:T(8,128)(2,1)} collective-permute-done((bf16[384,1152]{1,0:T(8,128)(2,1)S(1)}, bf16[384,1152]{1,0:T(8,128)(2,1)}, u32[]{:S(2)}, u32[]{:S(2)}) %collective-permute-start.2) | collective-permute-done | bytes 884768 | tf_op jit(solution)/shard_map/ppermute | solution.py:12
  184.1 16.9 %collective-permute-start.4 = (bf16[384,1152]{1,0:T(8,128)(2,1)}, bf16[384,1152]{1,0:T(8,128)(2,1)}, u32[]{:S(2)}, u32[]{:S(2)}) collective-permute-start(bf16[384,1152]{1,0:T(8,128)(2,1)} %collective-permute-done.2), channel_id=1, source_target_pairs={{8,0},{16,8},{24,16},{32,24},{40,32},{48,40},{56,48},{64,56},{72,6... | collective-permute-start | bytes 2654216 | tf_op jit(solution)/shard_map/ppermute | solution.py:12
  201.1 0.0 all-gather.2.cloned.1.call-done
  201.1 0.0 copy-done
  201.1 3.3 multiply_reduce_fusion.2
  204.4 0.0 copy-done.2
  204.4 0.0 copy-start.13
  204.4 0.2 fusion.39
  204.7 0.4 copy-done.13
  205.1 0.8 fusion.32
  205.9 0.0 copy-start.4
  205.9 0.4 copy-done.3
  206.3 0.8 fusion.33
  207.1 0.0 copy-start.10
  207.1 0.0 copy-done.12
  207.1 2.1 fusion.34
  209.1 0.0 copy-done.4
  209.1 0.0 copy-start.6
  209.2 0.6 fusion.40
  209.8 0.0 copy-done.10
  209.8 0.6 convolution_add_fusion.2
  210.5 0.0 copy-done.6
  210.5 1.8 convolution_add_fusion.1
  212.3 35.4 %collective-permute-done.4 = bf16[384,1152]{1,0:T(8,128)(2,1)} collective-permute-done((bf16[384,1152]{1,0:T(8,128)(2,1)}, bf16[384,1152]{1,0:T(8,128)(2,1)}, u32[]{:S(2)}, u32[]{:S(2)}) %collective-permute-start.4) | collective-permute-done | bytes 884768 | tf_op jit(solution)/shard_map/ppermute | solution.py:12
  247.7 1.9 fusion.35
  249.6 0.0 copy-start.8
  249.6 2.1 multiply_reduce_fusion
  251.8 0.0 copy-done.8
  251.8 3.5 fusion
  255.3 5.2 copy.10
  260.5 0.0 reduce-scatter.4.cloned.1.call-update
  260.5 0.9 copy-done.11
  261.5 0.7 fusion.2
  262.2 0.0 copy-start.9
  262.2 17.1 %collective-permute-start.1 = (bf16[384,1152]{1,0:T(8,128)(2,1)S(1)}, bf16[384,1152]{1,0:T(8,128)(2,1)S(1)}, u32[]{:S(2)}, u32[]{:S(2)}) collective-permute-start(bf16[384,1152]{1,0:T(8,128)(2,1)S(1)} %fusion.2), channel_id=1, source_target_pairs={{8,0},{16,8},{24,16},{32,24},{40,32},{48,40},{56,48},{64,56},{72,6... | collective-permute-start | bytes 2654216 | tf_op jit(solution)/shard_map/ppermute | solution.py:12
  279.3 25.6 %collective-permute-done.1 = bf16[384,1152]{1,0:T(8,128)(2,1)S(1)} collective-permute-done((bf16[384,1152]{1,0:T(8,128)(2,1)S(1)}, bf16[384,1152]{1,0:T(8,128)(2,1)S(1)}, u32[]{:S(2)}, u32[]{:S(2)}) %collective-permute-start.1) | collective-permute-done | bytes 884768 | tf_op jit(solution)/shard_map/ppermute | solution.py:12
  304.8 0.0 copy-done.7
  304.8 0.7 add_convert_fusion.1
  305.5 17.3 %collective-permute-start.3 = (bf16[384,1152]{1,0:T(8,128)(2,1)S(1)}, bf16[384,1152]{1,0:T(8,128)(2,1)S(1)}, u32[]{:S(2)}, u32[]{:S(2)}) collective-permute-start(bf16[384,1152]{1,0:T(8,128)(2,1)S(1)} %add_convert_fusion.1), channel_id=1, source_target_pairs={{8,0},{16,8},{24,16},{32,24},{40,32},{48,40},{56,48},{64,56},{72,6... | collective-permute-start | bytes 2654216 | tf_op jit(solution)/shard_map/ppermute | solution.py:12
  322.9 0.0 copy-done.9
  322.9 0.7 convolution_multiply_fusion
  323.5 0.0 copy-start.5
  323.6 26.9 %collective-permute-done.3 = bf16[384,1152]{1,0:T(8,128)(2,1)S(1)} collective-permute-done((bf16[384,1152]{1,0:T(8,128)(2,1)S(1)}, bf16[384,1152]{1,0:T(8,128)(2,1)S(1)}, u32[]{:S(2)}, u32[]{:S(2)}) %collective-permute-start.3) | collective-permute-done | bytes 884768 | tf_op jit(solution)/shard_map/ppermute | solution.py:12
  350.4 0.2 add_convert_fusion
  350.6 2.1 collective-permute-start.5
  352.7 26.4 %collective-permute-done.5 = bf16[384,1152]{1,0:T(8,128)(2,1)S(1)} collective-permute-done((bf16[384,1152]{1,0:T(8,128)(2,1)S(1)}, bf16[384,1152]{1,0:T(8,128)(2,1)S(1)}, u32[]{:S(2)}, u32[]{:S(2)}) %collective-permute-start.5) | collective-permute-done | bytes 884768 | tf_op jit(solution)/shard_map/ppermute | solution.py:12
  379.1 0.0 copy-done.5
  379.1 1.0 multiply_reduce_fusion.1
  380.1 1.5 divide_convert_fusion.1
  381.6 1.2 copy.11
  382.8 570.0 %all-reduce.1 = f32[144,1152]{0,1:T(8,128)S(1)} all-reduce(bf16[144,1152]{0,1:T(8,128)(2,1)S(1)} %copy.11), channel_id=1, replica_groups=mesh['dp'=64,'fsdp'=8] {'dp'}, use_global_device_ids=true, to_apply=%region_5.6 | all-reduce | flops 165888 | bytes 995328 | tf_op jit(solution)/shard_map/psum | solution.py:84
  952.8 1.2 copy.9
  (11 shorter events, 0.0 us)
Async XLA Ops:
  7.2 194.0 %copy-start = (bf16[384,1152]{1,0:T(8,128)(2,1)S(1)}, bf16[384,1152]{1,0:T(8,128)(2,1)}, u32[]{:S(2)}) copy-start(bf16[384,1152]{1,0:T(8,128)(2,1)} %param.6) | copy-start | bytes 2654212
  7.2 2.2 copy-start.1
  7.2 193.9 %all-gather.2.cloned.1.call-start = ((), (), s32[]{:S(2)}) async-start(), calls=%async_computation.1 | async-start | bytes 2985984 | tf_op jit(solution)/shard_map/all_gather | solution.py:20
  7.9 373.7 %reduce-scatter.4.cloned.1.call-start = ((), (), s32[]{:S(2)}) async-start(), calls=%async_computation.2 | async-start | bytes 2985984
  9.7 102.3 %collective-permute-start = (bf16[384,1152]{1,0:T(8,128)(2,1)S(1)}, bf16[384,1152]{1,0:T(8,128)(2,1)S(1)}, u32[]{:S(2)}, u32[]{:S(2)}) collective-permute-start(bf16[384,1152]{1,0:T(8,128)(2,1)S(1)} %fusion.38), channel_id=1, source_target_pairs={{8,0},{16,8},{24,16},{32,24},{40,32},{48,40},{56,48},{64,56},{72,6... | collective-permute-start | bytes 2654216 | tf_op jit(solution)/shard_map/ppermute | solution.py:12
  112.0 92.4 %copy-start.2 = (bf16[384,1152]{1,0:T(8,128)(2,1)}, bf16[384,1152]{1,0:T(8,128)(2,1)S(1)}, u32[]{:S(2)}) copy-start(bf16[384,1152]{1,0:T(8,128)(2,1)S(1)} %collective-permute-done) | copy-start | bytes 2654212
  112.0 72.1 %collective-permute-start.2 = (bf16[384,1152]{1,0:T(8,128)(2,1)S(1)}, bf16[384,1152]{1,0:T(8,128)(2,1)}, u32[]{:S(2)}, u32[]{:S(2)}) collective-permute-start(bf16[384,1152]{1,0:T(8,128)(2,1)S(1)} %collective-permute-done), channel_id=1, source_target_pairs={{8,0},{16,8},{24,16},{32,24},{40,32},{48,40},{56,48},{64,56},{72,6... | collective-permute-start | bytes 2654216 | tf_op jit(solution)/shard_map/ppermute | solution.py:12
  184.1 63.5 %collective-permute-start.4 = (bf16[384,1152]{1,0:T(8,128)(2,1)}, bf16[384,1152]{1,0:T(8,128)(2,1)}, u32[]{:S(2)}, u32[]{:S(2)}) collective-permute-start(bf16[384,1152]{1,0:T(8,128)(2,1)} %collective-permute-done.2), channel_id=1, source_target_pairs={{8,0},{16,8},{24,16},{32,24},{40,32},{48,40},{56,48},{64,56},{72,6... | collective-permute-start | bytes 2654216 | tf_op jit(solution)/shard_map/ppermute | solution.py:12
  204.4 0.7 copy-start.13
  205.1 1.2 copy-start.3
  205.9 3.2 copy-start.4
  206.3 0.8 copy-start.12
  207.1 2.7 copy-start.10
  209.1 1.3 copy-start.6
  249.6 2.2 copy-start.8
  260.5 1.0 copy-start.11
  261.5 43.3 %copy-start.7 = (bf16[384,384]{1,0:T(8,128)(2,1)S(1)}, bf16[384,384]{1,0:T(8,128)(2,1)}, u32[]{:S(2)}) copy-start(bf16[384,384]{1,0:T(8,128)(2,1)} %copy-done.6) | copy-start | bytes 884740
  262.2 60.7 %copy-start.9 = (bf16[384,384]{1,0:T(8,128)(2,1)S(1)}, bf16[384,384]{1,0:T(8,128)(2,1)}, u32[]{:S(2)}) copy-start(bf16[384,384]{1,0:T(8,128)(2,1)} %copy-done.8) | copy-start | bytes 884740
  262.2 42.7 %collective-permute-start.1 = (bf16[384,1152]{1,0:T(8,128)(2,1)S(1)}, bf16[384,1152]{1,0:T(8,128)(2,1)S(1)}, u32[]{:S(2)}, u32[]{:S(2)}) collective-permute-start(bf16[384,1152]{1,0:T(8,128)(2,1)S(1)} %fusion.2), channel_id=1, source_target_pairs={{8,0},{16,8},{24,16},{32,24},{40,32},{48,40},{56,48},{64,56},{72,6... | collective-permute-start | bytes 2654216 | tf_op jit(solution)/shard_map/ppermute | solution.py:12
  305.5 44.9 %collective-permute-start.3 = (bf16[384,1152]{1,0:T(8,128)(2,1)S(1)}, bf16[384,1152]{1,0:T(8,128)(2,1)S(1)}, u32[]{:S(2)}, u32[]{:S(2)}) collective-permute-start(bf16[384,1152]{1,0:T(8,128)(2,1)S(1)} %add_convert_fusion.1), channel_id=1, source_target_pairs={{8,0},{16,8},{24,16},{32,24},{40,32},{48,40},{56,48},{64,56},{72,6... | collective-permute-start | bytes 2654216 | tf_op jit(solution)/shard_map/ppermute | solution.py:12
  323.5 55.6 %copy-start.5 = (bf16[384,384]{1,0:T(8,128)(2,1)S(1)}, bf16[384,384]{1,0:T(8,128)(2,1)}, u32[]{:S(2)}) copy-start(bf16[384,384]{1,0:T(8,128)(2,1)} %copy-done.4) | copy-start | bytes 884740
  350.6 28.5 %collective-permute-start.5 = (bf16[384,1152]{1,0:T(8,128)(2,1)S(1)}, bf16[384,1152]{1,0:T(8,128)(2,1)S(1)}, u32[]{:S(2)}, u32[]{:S(2)}) collective-permute-start(bf16[384,1152]{1,0:T(8,128)(2,1)S(1)} %add_convert_fusion), channel_id=1, source_target_pairs={{488,0},{496,8},{504,16},{0,24},{8,32},{16,40},{24,48},{32,56},{40... | collective-permute-start | bytes 2654216 | tf_op jit(solution)/shard_map/ppermute | solution.py:12
Sparse Core Ops, SparseCore 0:
  10.1 122.9 all-gather.1
  260.7 83.5 reduce-scatter.3
where the time goes:
time: 962 us; the launch traced here: 961 us
  blocking collectives  570 us (59%)
  waiting for transfers between devices  251 us (26%)
  starting transfers between devices  90 us (9%)
  matrix products  20.6 us (2%)
  between operations  15.7 us (2%)
    psum x1, blocking collectives, on_device(): head_grad = lax.psum(share, 'dp')  570 us
    ppermute x6, waiting for transfers between devices, passed_along(): return lax.ppermute(block, axis, route)  250 us
    ppermute x6, starting transfers between devices, passed_along(): return lax.ppermute(block, axis, route)  89.9 us
  transfers between devices with their start and end apart: 8, of which 6 were waited for; matrix products, arithmetic and copies ran while one was open for 2% of the time, Pallas kernels for 0%

commit v1 on v0

v1 whole, which is shorter than its diff:
```python
import jax
import jax.numpy as jnp
from jax import lax
from jax.sharding import PartitionSpec as P

STEPS = 4
SIDE = 4
CORES = 2
GROUP = SIDE * CORES
AXES = ("dp", "fsdp")


def along_chain(block, width, lanes, moves):
    groups = width // GROUP
    route = [
        ((g * GROUP + s) * lanes + q, ((g + dg) % groups * GROUP + t) * lanes + q)
        for g in range(groups)
        for q in range(lanes)
        for s, dg, t in moves
    ]
    return lax.ppermute(block, AXES, route)


def by_coords(block, width, lanes, target):
    route = []
    for p in range(width):
        for q in range(lanes):
            x, hi, y, core = p // 16, p // 8 % 2, p // 2 % 4, p % 2
            x2, hi2, y2, core2, q2 = target(x, hi, y, core, q)
            route.append((p * lanes + q, (((x2 * 2 + hi2) * 4 + y2) * 2 + core2) * lanes + q2))
    return lax.ppermute(block, AXES, route)


def on_device(image_features, head_weight, text_embeds, partner, logit_scale, logit_bias):
    bf16, f32 = jnp.bfloat16, jnp.float32
    rows = image_features.shape[0]
    depth = image_features.shape[1]
    width_dp = lax.axis_size("dp")
    lanes = lax.axis_size("fsdp")
    place = lax.axis_index("dp")
    lane = lax.axis_index("fsdp")
    slot = place % GROUP
    core = place % CORES
    at_y = place // CORES % SIDE
    at_x = place // (2 * GROUP)
    first, last = slot == 0, slot == GROUP - 1

    def chain(block, moves):
        return along_chain(block, width_dp, lanes, moves)

    def coords(block, target):
        return by_coords(block, width_dp, lanes, target)

    def core_swap(block):
        return coords(block, lambda x, hi, y, c, q: (x, hi, y, 1 - c, q))

    def x_shift(block, d):
        return coords(block, lambda x, hi, y, c, q: ((x + d) % SIDE, hi, y, c, q))

    def y_shift(block, d):
        return coords(block, lambda x, hi, y, c, q: (x, hi, (y + d) % SIDE, c, q))

    def z_flip(block, bit):
        return coords(block, lambda x, hi, y, c, q: (x, hi, y, c, q ^ bit))

    def hi_flip(block):
        return coords(block, lambda x, hi, y, c, q: (x, 1 - hi, y, c, q))

    held = head_weight.shape[0]
    half = held // CORES
    step = (half // SIDE) // 8 * 8
    window = half - (SIDE - 1) * step

    def weight():
        mine = lax.dynamic_slice_in_dim(head_weight, core * half + at_x * step, window, 0)
        mine = lax.all_gather(mine, "fsdp", axis=0, tiled=False)
        others = [x_shift(mine, d) for d in range(1, SIDE)]
        ours = jnp.zeros((lanes, half, head_weight.shape[1]), bf16)
        for d, piece in enumerate([mine] + others):
            at = (at_x - d) % SIDE * step
            ours = lax.dynamic_update_slice_in_dim(ours, piece, at, 1)
        theirs = core_swap(ours)
        low = jnp.where(core == 0, ours, theirs)
        high = jnp.where(core == 0, theirs, ours)
        return jnp.concatenate([low, high], axis=1).reshape(lanes * held, -1)

    text_f = text_embeds.astype(f32)
    txt_norm = jnp.sqrt(jnp.sum(text_f * text_f, axis=1, keepdims=True) + 1e-06)
    unit_t = text_f / txt_norm
    unit_txt = unit_t.astype(bf16)
    down = [(s, 0, s - 1) for s in range(1, GROUP)]
    up = [(s, 0, s + 1) for s in range(GROUP - 1)]

    far = chain(unit_txt, [(0, -1, 0), (2, -1, 2), (1, 0, 7)])
    full_weight = weight()
    far_2 = chain(far, [(7, -1, 7), (2, 0, 0)])
    text_1 = chain(jnp.where(first, far, unit_txt), down + [(0, 0, 7)])
    got_2 = chain(jnp.where(first, far_2, text_1), down + [(0, 0, 7)])
    text_2 = jnp.where(last, far_2, got_2)
    got_3 = chain(text_2, down)
    text_3 = jnp.where(last, got_2, got_3)
    texts = [unit_txt, text_1, text_2, text_3]

    projected = jnp.dot(image_features, full_weight, preferred_element_type=f32)
    img_norm = jnp.sqrt(jnp.sum(projected * projected, axis=1, keepdims=True) + 1e-06)
    unit_f = projected / img_norm
    unit_img = unit_f.astype(bf16)

    offset = partner % rows
    ahead = (partner // (rows * lanes) - place) % width_dp
    code = jnp.concatenate([ahead, offset // 128, offset % 128]).astype(bf16)
    code = jnp.pad(code, (0, unit_img.shape[1] - code.shape[0]))
    code = jnp.pad(code[None, :], ((0, 7), (0, 0)))
    parcel = jnp.concatenate([unit_img, code], axis=0)

    back = chain(parcel, [(7, 1, 7), (5, 1, 5), (6, 0, 0)])
    back_2 = chain(back, [(0, 1, 0), (5, 0, 7)])
    image_1 = chain(jnp.where(last, back, parcel), up + [(7, 0, 0)])
    come_2 = chain(jnp.where(last, back_2, image_1), up + [(7, 0, 0)])
    image_2 = jnp.where(first, back_2, come_2)
    come_3 = chain(image_2, up)
    image_3 = jnp.where(first, come_2, come_3)

    scale = jnp.exp(logit_scale[0])
    bias = logit_bias[0]
    offsets = lax.iota(jnp.int32, rows)

    def pair_weight(logits, match):
        sign = jnp.where(match, 1.0, -1.0)
        return (-sign * jax.nn.sigmoid(-sign * logits)).astype(bf16)

    img_grad = 0.0
    for k, text in enumerate(texts):
        logits = scale * jnp.einsum("ie,je->ij", unit_img, text, preferred_element_type=f32) + bias
        met = jnp.where(ahead == k, offset, -1)
        weights = pair_weight(logits, met[:, None] == offsets[None, :])
        img_grad = img_grad + scale * jnp.dot(weights, text, preferred_element_type=f32)
    proj_grad = (
        (img_grad - unit_f * jnp.sum(unit_f * img_grad, axis=1, keepdims=True)) / img_norm
    ).astype(bf16)

    term = jnp.einsum(
        "rd,re->de", image_features, proj_grad, preferred_element_type=f32
    ).astype(bf16)
    cols = term.shape[1]
    term = term.reshape(lanes, CORES, half, cols)
    ours = lax.dynamic_index_in_dim(term, core, 1, keepdims=False)
    theirs = lax.dynamic_index_in_dim(term, 1 - core, 1, keepdims=False)
    total = ours.astype(f32) + core_swap(theirs).astype(f32)

    def cut_x(d):
        return lax.dynamic_slice_in_dim(total, (at_x + d) % SIDE * step, window, 1)

    sent = [x_shift(cut_x(d).astype(bf16), d) for d in range(1, SIDE)]
    total_x = cut_x(0)
    for piece in sent:
        total_x = total_x + piece.astype(f32)
    step_y = (cols // SIDE) // 128 * 128
    window_y = cols - (SIDE - 1) * step_y

    def cut_y(d):
        return lax.dynamic_slice_in_dim(total_x, (at_y + d) % SIDE * step_y, window_y, 2)

    sent = [y_shift(cut_y(d).astype(bf16), d) for d in range(1, SIDE)]
    total_z = cut_y(0)
    for piece in sent:
        total_z = total_z + piece.astype(f32)
    bit = lanes // 2
    while bit:
        halves = total_z.reshape(2, bit, window, window_y)
        side = lane // bit % 2
        keep = lax.dynamic_index_in_dim(halves, side, 0, keepdims=False)
        give = lax.dynamic_index_in_dim(halves, 1 - side, 0, keepdims=False)
        total_z = keep + z_flip(give.astype(bf16), bit).astype(f32)
        bit //= 2
    total_z = total_z.reshape(window, window_y)
    total_z = (total_z + hi_flip(total_z)).astype(bf16)

    pieces = [total_z] + [y_shift(total_z, d) for d in range(1, SIDE)]
    strip = jnp.zeros((window, cols), bf16)
    for d, piece in enumerate(pieces):
        strip = lax.dynamic_update_slice_in_dim(strip, piece, (at_y - d) % SIDE * step_y, 1)
    pieces = [strip] + [x_shift(strip, d) for d in range(1, SIDE)]
    ours = jnp.zeros((half, cols), bf16)
    for d, piece in enumerate(pieces):
        ours = lax.dynamic_update_slice_in_dim(ours, piece, (at_x - d) % SIDE * step, 0)
    theirs = core_swap(ours)
    low = jnp.where(core == 0, ours, theirs)
    high = jnp.where(core == 0, theirs, ours)
    head_grad = jnp.concatenate([low, high], axis=0).astype(f32)

    txt_grad = 0.0
    for k, image in enumerate([parcel, image_1, image_2, image_3]):
        unit, marks = image[:rows], image[rows].astype(f32).astype(jnp.int32)
        met = marks[rows : 2 * rows] * 128 + marks[2 * rows : 3 * rows]
        met = jnp.where(marks[:rows] == k, met, -1)
        logits = scale * jnp.einsum("je,ie->ji", unit_txt, unit, preferred_element_type=f32) + bias
        weights = pair_weight(logits, met[None, :] == offsets[:, None])
        txt_grad = txt_grad + scale * jnp.dot(weights, unit, preferred_element_type=f32)
    text_grad = (
        (txt_grad - unit_t * jnp.sum(unit_t * txt_grad, axis=1, keepdims=True)) / txt_norm
    ).astype(bf16)
    return (text_grad, head_grad)


def solution(mesh):
    in_specs = (
        P(("dp", "fsdp"), None),
        P("fsdp", None),
        P(("dp", "fsdp"), None),
        P(("dp", "fsdp")),
        P(),
        P(),
    )
    out_specs = (P(("dp", "fsdp"), None), P("fsdp", None))
    return jax.shard_map(
        on_device, mesh=mesh, in_specs=in_specs, out_specs=out_specs, check_vma=False
    )
```

time: 962 us -> 327 us (0.34)
  the two profiles are of different devices: /device:TPU:32 before, /device:TPU:1 now
where the time goes in v1:
time: 327 us; the launch traced here: 325 us
  starting transfers between devices  165 us (50%)
  blocking collectives  45.7 us (14%)
  matrix products  41.4 us (13%)
  waiting for transfers between devices  40.2 us (12%)
  other arithmetic  21.2 us (6%)
  local copies, waits for them, and re-layouts  9.42 us (3%)
    ppermute x22, starting transfers between devices, by_coords(): return lax.ppermute(block, AXES, route)  108 us
    ppermute x10, starting transfers between devices, along_chain(): return lax.ppermute(block, AXES, route)  56.8 us
    all_gather x1, blocking collectives, weight(): mine = lax.all_gather(mine, 'fsdp', axis=0, tiled=False)  45.7 us
    ppermute x22, waiting for transfers between devices, by_coords(): return lax.ppermute(block, AXES, route)  28.7 us
    dot_general x4, matrix products, on_device(): jnp.dot(weights, text, preferred_element_type=f32)  18.7 us
    dot_general x4, matrix products, on_device(): jnp.dot(weights, unit, preferred_element_type=f32)  17.3 us
    ppermute x10, waiting for transfers between devices, along_chain(): return lax.ppermute(block, AXES, route)  11.5 us
  transfers between devices with their start and end apart: 32, of which 11 were waited for; matrix products, arithmetic and copies ran while one was open for 21% of the time, Pallas kernels for 0%

profile of v1, /device:TPU:1, one launch (start us, length us, event | category | flops | bytes accessed | tf_op | source)
XLA Modules:
  0.0 325.4 jit_solution(1678372777390022505)
XLA Ops:
  1.6 45.7 %all-gather = bf16[192,1152]{1,0:T(8,128)(2,1)S(1)} all-gather(bf16[24,1152]{1,0:T(8,128)(2,1)S(1)} %constant_dynamic-slice_fusion), channel_id=2, replica_groups=mesh['dp'=64,'fsdp'=8] {'fsdp'}, dimensions={0}, use_global_device_ids=true | all-gather | bytes 497664 | tf_op jit(solution)/shard_map/all_gather | solution.py:76
  47.3 3.0 collective-permute-start
  50.4 4.4 %collective-permute-start.1 = (bf16[8,24,1152]{2,1,0:T(8,128)(2,1)S(1)}, bf16[8,24,1152]{2,1,0:T(8,128)(2,1)}, u32[]{:S(2)}, u32[]{:S(2)}) collective-permute-start(bf16[8,24,1152]{2,1,0:T(8,128)(2,1)S(1)} %bitcast.68), channel_id=1, source_target_pairs={{0,256},{1,257},{2,258},{3,259},{4,260},{5,261},{6,262},{7,263},{8... | collective-permute-start | bytes 1327112 | tf_op jit(solution)/shard_map/ppermute | solution.py:31
  54.7 3.1 collective-permute-start.2
  57.8 1.4 fusion.4
  59.2 1.2 fusion.182
  60.4 5.6 %collective-permute-start.9 = (bf16[384,1152]{1,0:T(8,128)(2,1)}, bf16[384,1152]{1,0:T(8,128)(2,1)}, u32[]{:S(2)}, u32[]{:S(2)}) collective-permute-start(bf16[384,1152]{1,0:T(8,128)(2,1)} %fusion.182), channel_id=1, source_target_pairs={{0,448},{16,464},{8,56},{1,449},{17,465},{9,57},{2,450},{18,466},{... | collective-permute-start | bytes 2654216 | tf_op jit(solution)/shard_map/ppermute | solution.py:21
  67.5 1.1 constant_dynamic-update-slice_fusion.10
  68.6 1.1 constant_dynamic-update-slice_fusion.9
  69.7 1.1 constant_dynamic-update-slice_fusion.8
  70.7 16.3 %collective-permute-start.3 = (bf16[8,72,1152]{2,1,0:T(8,128)(2,1)S(1)}, bf16[8,72,1152]{2,1,0:T(8,128)(2,1)}, u32[]{:S(2)}, u32[]{:S(2)}) collective-permute-start(bf16[8,72,1152]{2,1,0:T(8,128)(2,1)S(1)} %constant_dynamic-update-slice_fusion.8), channel_id=1, source_target_pairs={{0,8},{1,9},{2,10},{3,11},{4,12},{5,13},{6,14},{7,15},{8,0},{9,1},... | collective-permute-start | bytes 3981320 | tf_op jit(solution)/shard_map/ppermute | solution.py:31
  88.3 31.0 %collective-permute-start.10 = (bf16[384,1152]{1,0:T(8,128)(2,1)S(1)}, bf16[384,1152]{1,0:T(8,128)(2,1)S(1)}, u32[]{:S(2)}, u32[]{:S(2)}) collective-permute-start(bf16[384,1152]{1,0:T(8,128)(2,1)S(1)} %broadcast_select_fusion.8), channel_id=1, source_target_pairs={{8,0},{16,8},{24,16},{32,24},{40,32},{48,40},{56,48},{0,56},{9,1},... | collective-permute-start | bytes 2654216 | tf_op jit(solution)/shard_map/ppermute | solution.py:21
  120.0 1.6 broadcast_select_fusion.1
  121.8 1.5 multiply_reduce_fusion.1
  123.3 6.7 %collective-permute-done.10 = bf16[384,1152]{1,0:T(8,128)(2,1)S(1)} collective-permute-done((bf16[384,1152]{1,0:T(8,128)(2,1)S(1)}, bf16[384,1152]{1,0:T(8,128)(2,1)S(1)}, u32[]{:S(2)}, u32[]{:S(2)}) %collective-permute-start.10) | collective-permute-done | bytes 884768 | tf_op jit(solution)/shard_map/ppermute | solution.py:21
  130.0 1.1 broadcast_select_fusion.7
  131.1 10.2 %collective-permute-start.12 = (bf16[384,1152]{1,0:T(8,128)(2,1)}, bf16[384,1152]{1,0:T(8,128)(2,1)}, u32[]{:S(2)}, u32[]{:S(2)}) collective-permute-start(bf16[384,1152]{1,0:T(8,128)(2,1)} %broadcast_select_fusion.7), channel_id=1, source_target_pairs={{8,0},{16,8},{24,16},{32,24},{40,32},{48,40},{56,48},{0,56},{9,1},... | collective-permute-start | bytes 2654216 | tf_op jit(solution)/shard_map/ppermute | solution.py:21
  142.5 1.7 collective-permute-start.4
  144.2 4.1 %fusion.74 = f32[384,1152]{1,0:T(8,128)} fusion(bf16[384,1152]{1,0:T(8,128)(2,1)} %fusion.182, bf16[384,1152]{1,0:T(8,128)(2,1)S(1)} %bitcast_convert_fusion, s32[384]{0:T(512)S(1)} %get-tuple-element.18, f32[]{:T(128)} %bitcast.60, f32[]{:T(128)} %bitcast), kind=kOutput, calls=%fused_computation.100 | convolution fusion | flops 681099264 | bytes 3540488 | tf_op jit(solution)/shard_map/dot_general | solution.py:137
  148.3 4.7 %convolution_add_fusion.1 = f32[384,1152]{1,0:T(8,128)} fusion(f32[384,1152]{1,0:T(8,128)} %fusion.74, bf16[384,1152]{1,0:T(8,128)(2,1)} %copy-done.7, bf16[384,1152]{1,0:T(8,128)(2,1)S(1)} %bitcast_convert_fusion, s32[384]{0:T(512)} %get-tuple-element.16, f32[]{:T(128)} %bitcast.59, f32[]{:T(128)} %bitcast), kind=kOutput, calls=%fused_computation.4 | convolution fusion | flops 681541632 | bytes 5309960 | tf_op jit(solution)/shard_map/dot_general | solution.py:137
  153.0 2.2 broadcast_select_fusion.6
  155.2 1.9 collective-permute-start.13
  157.1 3.8 %fusion.76 = f32[384,1152]{1,0:T(8,128)} fusion(bf16[384,1152]{1,0:T(8,128)(2,1)S(1)} %bitcast_convert_fusion, bf16[384,1152]{1,0:T(8,128)(2,1)} %fusion.182, f32[]{:T(128)} %bitcast.56, f32[]{:T(128)} %bitcast, s32[384]{0:T(512)S(1)} %fusion.160), kind=kOutput, calls=%fused_computation.102 | convolution fusion | flops 681099264 | bytes 3540488 | tf_op jit(solution)/shard_map/dot_general | solution.py:199
  160.9 1.1 broadcast_select_fusion.5
  162.0 1.7 collective-permute-start.5
  163.7 1.6 collective-permute-start.6
  165.3 4.8 %collective-permute-done.13 = bf16[384,1152]{1,0:T(8,128)(2,1)} collective-permute-done((bf16[384,1152]{1,0:T(8,128)(2,1)}, bf16[384,1152]{1,0:T(8,128)(2,1)}, u32[]{:S(2)}, u32[]{:S(2)}) %collective-permute-start.13) | collective-permute-done | bytes 884768 | tf_op jit(solution)/shard_map/ppermute | solution.py:21
  170.1 4.2 %fusion.73 = f32[384,1152]{1,0:T(8,128)} fusion(bf16[384,1152]{1,0:T(8,128)(2,1)S(1)} %bitcast_convert_fusion, bf16[384,1152]{1,0:T(8,128)(2,1)} %collective-permute-done.12, bf16[384,1152]{1,0:T(8,128)(2,1)} %collective-permute-done.13, pred[]{:T(512)S(6)} %eq.185, s32[384]{0:T(512)S(1)} %copy-done.12, f32[]{:T(128)} %bitcast.57, f32[]{:T(128)} %bitcast), kind=kOutput, calls=%fused_computation.99 | convolution fusion | flops 681984000 | bytes 4425225 | tf_op jit(solution)/shard_map/dot_general | solution.py:137
  174.3 5.8 %fusion.5 = (f32[384]{0:T(512)S(1)}, f32[384,1152]{1,0:T(8,128)}) fusion(f32[1152,384]{0,1:T(8,128)} %copy-done.5, f32[384]{0:T(512)S(1)} %add_sqrt_fusion, f32[]{:T(128)} %bitcast, f32[384,1152]{1,0:T(8,128)} %fusion.73, f32[384,1152]{1,0:T(8,128)} %convolution_add_fusion.1, bf16[384,1152]{1,0:T(8,128)(2,1)} %broadcast_select_fusion.6, ...), kind=kOutput, calls=%fused_computation.17 | convolution fusion | flops 683753088 | bytes 8851976 | tf_op jit(solution)/shard_map/dot_general | solution.py:137
  180.1 3.8 %convolution_convert_fusion = bf16[1152,1152]{0,1:T(8,128)(2,1)S(1)} fusion(bf16[384,1152]{1,0:T(8,128)(2,1)S(1)} %copy-done, f32[384,1152]{1,0:T(8,128)} %get-tuple-element.27, f32[384]{0:T(512)S(1)} %add_sqrt_fusion, f32[384]{0:T(512)S(1)} %get-tuple-element.26, f32[1152,384]{0,1:T(8,128)} %copy-done.5), kind=kOutput, calls=%fused_computation | convolution fusion | flops 1022754816 | bytes 7080960 | tf_op jit(solution)/shard_map/rd,re->de/dot_general | solution.py:142
  183.9 1.3 dynamic-slice_bitcast_fusion
  185.2 1.9 collective-permute-start.14
  187.1 2.3 broadcast_select_fusion.4
  190.1 4.9 %convolution_add_fusion.3 = f32[384,1152]{1,0:T(8,128)} fusion(f32[384,1152]{1,0:T(8,128)} %fusion.76, bf16[384,1152]{1,0:T(8,128)(2,1)} %fusion.182, bf16[392,1152]{1,0:T(8,128)(2,1)} %collective-permute-done.5, s32[384]{0:T(512)S(1)} %fusion.163, f32[]{:T(128)} %bitcast.63, f32[]{:T(128)} %bitcast), kind=kOutput, calls=%fused_computation.8 | convolution fusion | flops 681541632 | bytes 6195712 | tf_op jit(solution)/shard_map/dot_general | solution.py:199
  195.0 2.0 convert_add_fusion
  197.2 2.5 collective-permute-start.15
  199.8 2.5 collective-permute-start.16
  202.2 3.7 %collective-permute-start.17 = (bf16[8,24,1152]{2,1,0:T(8,128)(2,1)S(1)}, bf16[8,24,1152]{2,1,0:T(8,128)(2,1)S(1)}, u32[]{:S(2)}, u32[]{:S(2)}) collective-permute-start(bf16[8,24,1152]{2,1,0:T(8,128)(2,1)S(1)} %get-tuple-element.7), channel_id=1, source_target_pairs={{0,384},{1,385},{2,386},{3,387},{4,388},{5,389},{6,390},{7,391},{8... | collective-permute-start | bytes 1327112 | tf_op jit(solution)/shard_map/ppermute | solution.py:31
  206.1 2.5 collective-permute-start.8
  208.7 6.9 %collective-permute-done.16 = bf16[8,24,1152]{2,1,0:T(8,128)(2,1)S(1)} collective-permute-done((bf16[8,24,1152]{2,1,0:T(8,128)(2,1)S(1)}, bf16[8,24,1152]{2,1,0:T(8,128)(2,1)S(1)}, u32[]{:S(2)}, u32[]{:S(2)}) %collective-permute-start.16) | collective-permute-done | bytes 442400 | tf_op jit(solution)/shard_map/ppermute | solution.py:31
  215.8 11.5 %collective-permute-start.18 = (bf16[8,24,384]{2,1,0:T(8,128)(2,1)S(1)}, bf16[8,24,384]{2,1,0:T(8,128)(2,1)S(1)}, u32[]{:S(2)}, u32[]{:S(2)}) collective-permute-start(bf16[8,24,384]{2,1,0:T(8,128)(2,1)S(1)} %get-tuple-element.11), channel_id=1, source_target_pairs={{0,16},{1,17},{2,18},{3,19},{4,20},{5,21},{6,22},{7,23},{8,24},{9,... | collective-permute-start | bytes 442376 | tf_op jit(solution)/shard_map/ppermute | solution.py:31
  227.3 7.1 %collective-permute-start.19 = (bf16[8,24,384]{2,1,0:T(8,128)(2,1)S(1)}, bf16[8,24,384]{2,1,0:T(8,128)(2,1)S(1)}, u32[]{:S(2)}, u32[]{:S(2)}) collective-permute-start(bf16[8,24,384]{2,1,0:T(8,128)(2,1)S(1)} %get-tuple-element.13), channel_id=1, source_target_pairs={{0,32},{1,33},{2,34},{3,35},{4,36},{5,37},{6,38},{7,39},{8,40},{9,... | collective-permute-start | bytes 442376 | tf_op jit(solution)/shard_map/ppermute | solution.py:31
  234.4 1.9 collective-permute-start.20
  236.4 1.4 collective-permute-done.19
  237.8 4.2 %collective-permute-done.20 = bf16[8,24,384]{2,1,0:T(8,128)(2,1)S(1)} collective-permute-done((bf16[8,24,384]{2,1,0:T(8,128)(2,1)S(1)}, bf16[8,24,384]{2,1,0:T(8,128)(2,1)S(1)}, u32[]{:S(2)}, u32[]{:S(2)}) %collective-permute-start.20) | collective-permute-done | bytes 147488 | tf_op jit(solution)/shard_map/ppermute | solution.py:31
  242.0 14.4 %collective-permute-start.21 = (bf16[4,24,384]{2,1,0:T(8,128)(2,1)S(1)}, bf16[4,24,384]{2,1,0:T(8,128)(2,1)S(1)}, u32[]{:S(2)}, u32[]{:S(2)}) collective-permute-start(bf16[4,24,384]{2,1,0:T(8,128)(2,1)S(1)} %fusion.146), channel_id=1, source_target_pairs={{0,4},{1,5},{2,6},{3,7},{4,0},{5,1},{6,2},{7,3},{8,12},{9,13},{10,... | collective-permute-start | bytes 221192 | tf_op jit(solution)/shard_map/ppermute | solution.py:31
  257.5 1.2 collective-permute-done.21
  258.8 1.9 collective-permute-start.22
  261.5 2.9 collective-permute-done.22
  264.5 1.9 collective-permute-start.23
  266.4 2.6 collective-permute-done.23
  269.0 1.9 collective-permute-start.24
  270.9 4.4 %fusion.75 = f32[384,1152]{1,0:T(8,128)} fusion(bf16[384,1152]{1,0:T(8,128)(2,1)} %fusion.182, bf16[392,1152]{1,0:T(8,128)(2,1)} %broadcast_select_fusion.2, s32[384]{0:T(512)S(1)} %fusion.165, f32[]{:T(128)} %bitcast.61, f32[]{:T(128)} %bitcast), kind=kOutput, calls=%fused_computation.101 | convolution fusion | flops 681099264 | bytes 4426240 | tf_op jit(solution)/shard_map/dot_general | solution.py:199
  275.2 8.1 %collective-permute-done.24 = f32[24,384]{1,0:T(8,128)S(1)} collective-permute-done((f32[24,384]{1,0:T(8,128)S(1)}, f32[24,384]{1,0:T(8,128)S(1)}, u32[]{:S(2)}, u32[]{:S(2)}) %collective-permute-start.24) | collective-permute-done | bytes 36896 | tf_op jit(solution)/shard_map/ppermute | solution.py:31
  283.9 1.9 collective-permute-start.25
  285.9 4.3 %multiply_reduce_fusion = (f32[384]{0:T(512)S(1)}, f32[384,1152]{1,0:T(8,128)S(1)}) fusion(f32[384]{0:T(512)S(1)} %add_sqrt_fusion.1, bf16[384,1152]{1,0:T(8,128)(2,1)S(1)} %copy-done.1, f32[]{:T(128)} %bitcast, f32[384,1152]{1,0:T(8,128)} %fusion.75, f32[384,1152]{1,0:T(8,128)} %convolution_add_fusion.3, bf16[392,1152]{1,0:T(8,128)(2,1)} %copy-done.6, ...), kind=kOutput, calls=%fused_computation.22 | convolution fusion | flops 684195456 | bytes 8853504 | tf_op jit(solution)/shard_map/dot_general | solution.py:199
  290.2 4.8 %collective-permute-start.26 = (bf16[24,384]{1,0:T(8,128)(2,1)}, bf16[24,384]{1,0:T(8,128)(2,1)S(1)}, u32[]{:S(2)}, u32[]{:S(2)}) collective-permute-start(bf16[24,384]{1,0:T(8,128)(2,1)} %get-tuple-element.3), channel_id=1, source_target_pairs={{0,32},{1,33},{2,34},{3,35},{4,36},{5,37},{6,38},{7,39},{8,40},{9,... | collective-permute-start | bytes 55304 | tf_op jit(solution)/shard_map/ppermute | solution.py:31
  295.0 1.9 collective-permute-start.27
  296.9 1.3 constant_dynamic-update-slice_fusion.6
  300.3 4.5 %collective-permute-start.28 = (bf16[24,1152]{1,0:T(8,128)(2,1)}, bf16[24,1152]{1,0:T(8,128)(2,1)S(1)}, u32[]{:S(2)}, u32[]{:S(2)}) collective-permute-start(bf16[24,1152]{1,0:T(8,128)(2,1)} %constant_dynamic-update-slice_fusion.4), channel_id=1, source_target_pairs={{0,128},{1,129},{2,130},{3,131},{4,132},{5,133},{6,134},{7,135},{8... | collective-permute-start | bytes 165896 | tf_op jit(solution)/shard_map/ppermute | solution.py:31
  304.8 3.5 %collective-permute-start.29 = (bf16[24,1152]{1,0:T(8,128)(2,1)}, bf16[24,1152]{1,0:T(8,128)(2,1)S(1)}, u32[]{:S(2)}, u32[]{:S(2)}) collective-permute-start(bf16[24,1152]{1,0:T(8,128)(2,1)} %constant_dynamic-update-slice_fusion.4), channel_id=1, source_target_pairs={{0,256},{1,257},{2,258},{3,259},{4,260},{5,261},{6,262},{7,263},{8... | collective-permute-start | bytes 165896 | tf_op jit(solution)/shard_map/ppermute | solution.py:31
  308.3 4.0 %collective-permute-start.30 = (bf16[24,1152]{1,0:T(8,128)(2,1)}, bf16[24,1152]{1,0:T(8,128)(2,1)S(1)}, u32[]{:S(2)}, u32[]{:S(2)}) collective-permute-start(bf16[24,1152]{1,0:T(8,128)(2,1)} %constant_dynamic-update-slice_fusion.4), channel_id=1, source_target_pairs={{0,384},{1,385},{2,386},{3,387},{4,388},{5,389},{6,390},{7,391},{8... | collective-permute-start | bytes 165896 | tf_op jit(solution)/shard_map/ppermute | solution.py:31
  313.8 9.3 %collective-permute-start.31 = (bf16[72,1152]{1,0:T(8,128)(2,1)S(1)}, bf16[72,1152]{1,0:T(8,128)(2,1)S(1)}, u32[]{:S(2)}, u32[]{:S(2)}) collective-permute-start(bf16[72,1152]{1,0:T(8,128)(2,1)S(1)} %constant_dynamic-update-slice_fusion), channel_id=1, source_target_pairs={{0,8},{1,9},{2,10},{3,11},{4,12},{5,13},{6,14},{7,15},{8,0},{9,1},... | collective-permute-start | bytes 497672 | tf_op jit(solution)/shard_map/ppermute | solution.py:31
  323.1 1.3 divide_convert_fusion
  (96 shorter events, 12.8 us)
Async XLA Ops:
  0.6 121.1 %copy-start = (bf16[384,1152]{1,0:T(8,128)(2,1)S(1)}, bf16[384,1152]{1,0:T(8,128)(2,1)}, u32[]{:S(2)}) copy-start(bf16[384,1152]{1,0:T(8,128)(2,1)} %param.6) | copy-start | bytes 2654212
  0.6 58.6 %copy-start.1 = (bf16[384,1152]{1,0:T(8,128)(2,1)S(1)}, bf16[384,1152]{1,0:T(8,128)(2,1)}, u32[]{:S(2)}) copy-start(bf16[384,1152]{1,0:T(8,128)(2,1)} %param.8) | copy-start | bytes 2654212
  47.3 20.2 %collective-permute-start = (bf16[8,24,1152]{2,1,0:T(8,128)(2,1)S(1)}, bf16[8,24,1152]{2,1,0:T(8,128)(2,1)}, u32[]{:S(2)}, u32[]{:S(2)}) collective-permute-start(bf16[8,24,1152]{2,1,0:T(8,128)(2,1)S(1)} %bitcast.67), channel_id=1, source_target_pairs={{0,128},{1,129},{2,130},{3,131},{4,132},{5,133},{6,134},{7,135},{8... | collective-permute-start | bytes 1327112 | tf_op jit(solution)/shard_map/ppermute | solution.py:31
  50.4 18.2 %collective-permute-start.1 = (bf16[8,24,1152]{2,1,0:T(8,128)(2,1)S(1)}, bf16[8,24,1152]{2,1,0:T(8,128)(2,1)}, u32[]{:S(2)}, u32[]{:S(2)}) collective-permute-start(bf16[8,24,1152]{2,1,0:T(8,128)(2,1)S(1)} %bitcast.68), channel_id=1, source_target_pairs={{0,256},{1,257},{2,258},{3,259},{4,260},{5,261},{6,262},{7,263},{8... | collective-permute-start | bytes 1327112 | tf_op jit(solution)/shard_map/ppermute | solution.py:31
  54.7 15.0 %collective-permute-start.2 = (bf16[8,24,1152]{2,1,0:T(8,128)(2,1)S(1)}, bf16[8,24,1152]{2,1,0:T(8,128)(2,1)}, u32[]{:S(2)}, u32[]{:S(2)}) collective-permute-start(bf16[8,24,1152]{2,1,0:T(8,128)(2,1)S(1)} %bitcast.69), channel_id=1, source_target_pairs={{0,384},{1,385},{2,386},{3,387},{4,388},{5,389},{6,390},{7,391},{8... | collective-permute-start | bytes 1327112 | tf_op jit(solution)/shard_map/ppermute | solution.py:31
  60.4 27.5 %collective-permute-start.9 = (bf16[384,1152]{1,0:T(8,128)(2,1)}, bf16[384,1152]{1,0:T(8,128)(2,1)}, u32[]{:S(2)}, u32[]{:S(2)}) collective-permute-start(bf16[384,1152]{1,0:T(8,128)(2,1)} %fusion.182), channel_id=1, source_target_pairs={{0,448},{16,464},{8,56},{1,449},{17,465},{9,57},{2,450},{18,466},{... | collective-permute-start | bytes 2654216 | tf_op jit(solution)/shard_map/ppermute | solution.py:21
  67.4 19.6 %copy-start.11 = (s32[384]{0:T(512)S(1)}, s32[384]{0:T(512)}, u32[]{:S(2)}) copy-start(s32[384]{0:T(512)} %param.9) | copy-start | bytes 4612
  70.7 49.2 %collective-permute-start.3 = (bf16[8,72,1152]{2,1,0:T(8,128)(2,1)S(1)}, bf16[8,72,1152]{2,1,0:T(8,128)(2,1)}, u32[]{:S(2)}, u32[]{:S(2)}) collective-permute-start(bf16[8,72,1152]{2,1,0:T(8,128)(2,1)S(1)} %constant_dynamic-update-slice_fusion.8), channel_id=1, source_target_pairs={{0,8},{1,9},{2,10},{3,11},{4,12},{5,13},{6,14},{7,15},{8,0},{9,1},... | collective-permute-start | bytes 3981320 | tf_op jit(solution)/shard_map/ppermute | solution.py:31
  87.9 53.6 %copy-start.9 = (bf16[8,1152]{1,0:T(8,128)(2,1)}, bf16[8,1152]{1,0:T(8,128)(2,1)S(1)}, u32[]{:S(2)}) copy-start(bf16[8,1152]{1,0:T(8,128)(2,1)S(1)} %fusion.152) | copy-start | bytes 55300
  88.3 41.7 %collective-permute-start.10 = (bf16[384,1152]{1,0:T(8,128)(2,1)S(1)}, bf16[384,1152]{1,0:T(8,128)(2,1)S(1)}, u32[]{:S(2)}, u32[]{:S(2)}) collective-permute-start(bf16[384,1152]{1,0:T(8,128)(2,1)S(1)} %broadcast_select_fusion.8), channel_id=1, source_target_pairs={{8,0},{16,8},{24,16},{32,24},{40,32},{48,40},{56,48},{0,56},{9,1},... | collective-permute-start | bytes 2654216 | tf_op jit(solution)/shard_map/ppermute | solution.py:21
  119.3 10.8 %collective-permute-start.11 = (bf16[384,1152]{1,0:T(8,128)(2,1)}, bf16[384,1152]{1,0:T(8,128)(2,1)S(1)}, u32[]{:S(2)}, u32[]{:S(2)}) collective-permute-start(bf16[384,1152]{1,0:T(8,128)(2,1)} %collective-permute-done.9), channel_id=1, source_target_pairs={{56,504},{16,0},{57,505},{17,1},{58,506},{18,2},{59,507},{19,3},{6... | collective-permute-start | bytes 2654216 | tf_op jit(solution)/shard_map/ppermute | solution.py:21
  123.3 19.2 %copy-start.5 = (f32[1152,384]{0,1:T(8,128)}, f32[1152,384]{0,1:T(8,128)S(1)}, u32[]{:S(2)}) copy-start(f32[1152,384]{0,1:T(8,128)S(1)} %get-tuple-element.23) | copy-start | bytes 5308420
  130.0 11.5 %copy-start.7 = (bf16[384,1152]{1,0:T(8,128)(2,1)}, bf16[384,1152]{1,0:T(8,128)(2,1)S(1)}, u32[]{:S(2)}) copy-start(bf16[384,1152]{1,0:T(8,128)(2,1)S(1)} %collective-permute-done.10) | copy-start | bytes 2654212
  130.0 11.5 %copy-start.2 = (bf16[384,1152]{1,0:T(8,128)(2,1)}, bf16[384,1152]{1,0:T(8,128)(2,1)S(1)}, u32[]{:S(2)}) copy-start(bf16[384,1152]{1,0:T(8,128)(2,1)S(1)} %collective-permute-done.11) | copy-start | bytes 2654212
  131.1 21.8 %collective-permute-start.12 = (bf16[384,1152]{1,0:T(8,128)(2,1)}, bf16[384,1152]{1,0:T(8,128)(2,1)}, u32[]{:S(2)}, u32[]{:S(2)}) collective-permute-start(bf16[384,1152]{1,0:T(8,128)(2,1)} %broadcast_select_fusion.7), channel_id=1, source_target_pairs={{8,0},{16,8},{24,16},{32,24},{40,32},{48,40},{56,48},{0,56},{9,1},... | collective-permute-start | bytes 2654216 | tf_op jit(solution)/shard_map/ppermute | solution.py:21
  142.5 18.4 %collective-permute-start.4 = (bf16[392,1152]{1,0:T(8,128)(2,1)}, bf16[392,1152]{1,0:T(8,128)(2,1)}, u32[]{:S(2)}, u32[]{:S(2)}) collective-permute-start(bf16[392,1152]{1,0:T(8,128)(2,1)} %pad_maximum_fusion.1), channel_id=1, source_target_pairs={{56,120},{40,104},{48,0},{57,121},{41,105},{49,1},{58,122},{42,106... | collective-permute-start | bytes 2709512 | tf_op jit(solution)/shard_map/ppermute | solution.py:21
  148.3 4.7 %copy-start.3 = (bf16[384,1152]{1,0:T(8,128)(2,1)S(1)}, bf16[384,1152]{1,0:T(8,128)(2,1)}, u32[]{:S(2)}) copy-start(bf16[384,1152]{1,0:T(8,128)(2,1)} %copy-done.2) | copy-start | bytes 2654212
  155.2 15.0 %collective-permute-start.13 = (bf16[384,1152]{1,0:T(8,128)(2,1)}, bf16[384,1152]{1,0:T(8,128)(2,1)}, u32[]{:S(2)}, u32[]{:S(2)}) collective-permute-start(bf16[384,1152]{1,0:T(8,128)(2,1)} %broadcast_select_fusion.6), channel_id=1, source_target_pairs={{8,0},{16,8},{24,16},{32,24},{40,32},{48,40},{56,48},{9,1},{17,9},... | collective-permute-start | bytes 2654216 | tf_op jit(solution)/shard_map/ppermute | solution.py:21
  157.1 3.8 %copy-start.10 = (bf16[8,1152]{1,0:T(8,128)(2,1)S(1)}, bf16[8,1152]{1,0:T(8,128)(2,1)}, u32[]{:S(2)}) copy-start(bf16[8,1152]{1,0:T(8,128)(2,1)} %copy-done.9) | copy-start | bytes 55300
  160.9 9.3 %copy-start.12 = (s32[384]{0:T(512)S(1)}, s32[384]{0:T(512)}, u32[]{:S(2)}) copy-start(s32[384]{0:T(512)} %get-tuple-element.17) | copy-start | bytes 4612
  162.0 25.1 %collective-permute-start.5 = (bf16[392,1152]{1,0:T(8,128)(2,1)}, bf16[392,1152]{1,0:T(8,128)(2,1)}, u32[]{:S(2)}, u32[]{:S(2)}) collective-permute-start(bf16[392,1152]{1,0:T(8,128)(2,1)} %broadcast_select_fusion.5), channel_id=1, source_target_pairs={{0,8},{8,16},{16,24},{24,32},{32,40},{40,48},{48,56},{56,0},{1,9},... | collective-permute-start | bytes 2709512 | tf_op jit(solution)/shard_map/ppermute | solution.py:21
  163.7 23.4 %collective-permute-start.6 = (bf16[392,1152]{1,0:T(8,128)(2,1)}, bf16[392,1152]{1,0:T(8,128)(2,1)}, u32[]{:S(2)}, u32[]{:S(2)}) collective-permute-start(bf16[392,1152]{1,0:T(8,128)(2,1)} %collective-permute-done.4), channel_id=1, source_target_pairs={{0,64},{40,56},{1,65},{41,57},{2,66},{42,58},{3,67},{43,59},{4,68}... | collective-permute-start | bytes 2709512 | tf_op jit(solution)/shard_map/ppermute | solution.py:21
  183.9 5.5 %copy-start.4 = (bf16[1152,1152]{0,1:T(8,128)(2,1)}, bf16[1152,1152]{0,1:T(8,128)(2,1)S(1)}, u32[]{:S(2)}) copy-start(bf16[1152,1152]{0,1:T(8,128)(2,1)S(1)} %convolution_convert_fusion) | copy-start | bytes 7962628
  185.2 9.8 %collective-permute-start.14 = (bf16[8,72,1152]{2,1,0:T(8,128)(2,1)}, bf16[8,72,1152]{2,1,0:T(8,128)(2,1)}, u32[]{:S(2)}, u32[]{:S(2)}) collective-permute-start(bf16[8,72,1152]{2,1,0:T(8,128)(2,1)} %dynamic-slice_bitcast_fusion), channel_id=1, source_target_pairs={{0,8},{1,9},{2,10},{3,11},{4,12},{5,13},{6,14},{7,15},{8,0},{9,1},... | collective-permute-start | bytes 3981320 | tf_op jit(solution)/shard_map/ppermute | solution.py:31
  189.4 16.6 %collective-permute-start.7 = (bf16[392,1152]{1,0:T(8,128)(2,1)}, bf16[392,1152]{1,0:T(8,128)(2,1)S(1)}, u32[]{:S(2)}, u32[]{:S(2)}) collective-permute-start(bf16[392,1152]{1,0:T(8,128)(2,1)} %broadcast_select_fusion.4), channel_id=1, source_target_pairs={{0,8},{8,16},{16,24},{24,32},{32,40},{40,48},{48,56},{56,0},{1,9},... | collective-permute-start | bytes 2709512 | tf_op jit(solution)/shard_map/ppermute | solution.py:21
  197.2 11.4 %collective-permute-start.15 = (bf16[8,24,1152]{2,1,0:T(8,128)(2,1)S(1)}, bf16[8,24,1152]{2,1,0:T(8,128)(2,1)S(1)}, u32[]{:S(2)}, u32[]{:S(2)}) collective-permute-start(bf16[8,24,1152]{2,1,0:T(8,128)(2,1)S(1)} %get-tuple-element.6), channel_id=1, source_target_pairs={{0,128},{1,129},{2,130},{3,131},{4,132},{5,133},{6,134},{7,135},{8... | collective-permute-start | bytes 1327112 | tf_op jit(solution)/shard_map/ppermute | solution.py:31
  199.8 15.8 %collective-permute-start.16 = (bf16[8,24,1152]{2,1,0:T(8,128)(2,1)S(1)}, bf16[8,24,1152]{2,1,0:T(8,128)(2,1)S(1)}, u32[]{:S(2)}, u32[]{:S(2)}) collective-permute-start(bf16[8,24,1152]{2,1,0:T(8,128)(2,1)S(1)} %get-tuple-element.8), channel_id=1, source_target_pairs={{0,256},{1,257},{2,258},{3,259},{4,260},{5,261},{6,262},{7,263},{8... | collective-permute-start | bytes 1327112 | tf_op jit(solution)/shard_map/ppermute | solution.py:31
  202.2 13.3 %collective-permute-start.17 = (bf16[8,24,1152]{2,1,0:T(8,128)(2,1)S(1)}, bf16[8,24,1152]{2,1,0:T(8,128)(2,1)S(1)}, u32[]{:S(2)}, u32[]{:S(2)}) collective-permute-start(bf16[8,24,1152]{2,1,0:T(8,128)(2,1)S(1)} %get-tuple-element.7), channel_id=1, source_target_pairs={{0,384},{1,385},{2,386},{3,387},{4,388},{5,389},{6,390},{7,391},{8... | collective-permute-start | bytes 1327112 | tf_op jit(solution)/shard_map/ppermute | solution.py:31
  206.1 51.4 %copy-start.6 = (bf16[392,1152]{1,0:T(8,128)(2,1)}, bf16[392,1152]{1,0:T(8,128)(2,1)S(1)}, u32[]{:S(2)}) copy-start(bf16[392,1152]{1,0:T(8,128)(2,1)S(1)} %broadcast_select_fusion.3) | copy-start | bytes 2709508
  206.1 50.3 %collective-permute-start.8 = (bf16[392,1152]{1,0:T(8,128)(2,1)S(1)}, bf16[392,1152]{1,0:T(8,128)(2,1)S(1)}, u32[]{:S(2)}, u32[]{:S(2)}) collective-permute-start(bf16[392,1152]{1,0:T(8,128)(2,1)S(1)} %broadcast_select_fusion.3), channel_id=1, source_target_pairs={{0,8},{8,16},{16,24},{24,32},{32,40},{40,48},{48,56},{1,9},{9,17},... | collective-permute-start | bytes 2709512 | tf_op jit(solution)/shard_map/ppermute | solution.py:21
  215.8 20.6 %collective-permute-start.18 = (bf16[8,24,384]{2,1,0:T(8,128)(2,1)S(1)}, bf16[8,24,384]{2,1,0:T(8,128)(2,1)S(1)}, u32[]{:S(2)}, u32[]{:S(2)}) collective-permute-start(bf16[8,24,384]{2,1,0:T(8,128)(2,1)S(1)} %get-tuple-element.11), channel_id=1, source_target_pairs={{0,16},{1,17},{2,18},{3,19},{4,20},{5,21},{6,22},{7,23},{8,24},{9,... | collective-permute-start | bytes 442376 | tf_op jit(solution)/shard_map/ppermute | solution.py:31
  227.3 10.4 %collective-permute-start.19 = (bf16[8,24,384]{2,1,0:T(8,128)(2,1)S(1)}, bf16[8,24,384]{2,1,0:T(8,128)(2,1)S(1)}, u32[]{:S(2)}, u32[]{:S(2)}) collective-permute-start(bf16[8,24,384]{2,1,0:T(8,128)(2,1)S(1)} %get-tuple-element.13), channel_id=1, source_target_pairs={{0,32},{1,33},{2,34},{3,35},{4,36},{5,37},{6,38},{7,39},{8,40},{9,... | collective-permute-start | bytes 442376 | tf_op jit(solution)/shard_map/ppermute | solution.py:31
  234.4 7.5 %collective-permute-start.20 = (bf16[8,24,384]{2,1,0:T(8,128)(2,1)S(1)}, bf16[8,24,384]{2,1,0:T(8,128)(2,1)S(1)}, u32[]{:S(2)}, u32[]{:S(2)}) collective-permute-start(bf16[8,24,384]{2,1,0:T(8,128)(2,1)S(1)} %get-tuple-element.12), channel_id=1, source_target_pairs={{0,48},{1,49},{2,50},{3,51},{4,52},{5,53},{6,54},{7,55},{8,56},{9,... | collective-permute-start | bytes 442376 | tf_op jit(solution)/shard_map/ppermute | solution.py:31
  242.0 16.7 %collective-permute-start.21 = (bf16[4,24,384]{2,1,0:T(8,128)(2,1)S(1)}, bf16[4,24,384]{2,1,0:T(8,128)(2,1)S(1)}, u32[]{:S(2)}, u32[]{:S(2)}) collective-permute-start(bf16[4,24,384]{2,1,0:T(8,128)(2,1)S(1)} %fusion.146), channel_id=1, source_target_pairs={{0,4},{1,5},{2,6},{3,7},{4,0},{5,1},{6,2},{7,3},{8,12},{9,13},{10,... | collective-permute-start | bytes 221192 | tf_op jit(solution)/shard_map/ppermute | solution.py:31
  258.8 5.6 %collective-permute-start.22 = (bf16[2,24,384]{2,1,0:T(8,128)(2,1)S(1)}, bf16[2,24,384]{2,1,0:T(8,128)(2,1)S(1)}, u32[]{:S(2)}, u32[]{:S(2)}) collective-permute-start(bf16[2,24,384]{2,1,0:T(8,128)(2,1)S(1)} %fusion.147), channel_id=1, source_target_pairs={{0,2},{1,3},{2,0},{3,1},{4,6},{5,7},{6,4},{7,5},{8,10},{9,11},{10,... | collective-permute-start | bytes 110600 | tf_op jit(solution)/shard_map/ppermute | solution.py:31
  264.5 4.5 %collective-permute-start.23 = (bf16[1,24,384]{2,1,0:T(8,128)(2,1)S(1)}, bf16[1,24,384]{2,1,0:T(8,128)(2,1)S(1)}, u32[]{:S(2)}, u32[]{:S(2)}) collective-permute-start(bf16[1,24,384]{2,1,0:T(8,128)(2,1)S(1)} %dynamic-slice_convert_fusion.8), channel_id=1, source_target_pairs={{0,1},{1,0},{2,3},{3,2},{4,5},{5,4},{6,7},{7,6},{8,9},{9,8},{10,11... | collective-permute-start | bytes 55304 | tf_op jit(solution)/shard_map/ppermute | solution.py:31
  269.0 14.3 %collective-permute-start.24 = (f32[24,384]{1,0:T(8,128)S(1)}, f32[24,384]{1,0:T(8,128)S(1)}, u32[]{:S(2)}, u32[]{:S(2)}) collective-permute-start(f32[24,384]{1,0:T(8,128)S(1)} %add_bitcast_fusion), channel_id=1, source_target_pairs={{0,64},{1,65},{2,66},{3,67},{4,68},{5,69},{6,70},{7,71},{8,72},{9,... | collective-permute-start | bytes 110600 | tf_op jit(solution)/shard_map/ppermute | solution.py:31
  283.9 1.9 copy-start.8
  283.9 13.0 %collective-permute-start.25 = (bf16[24,384]{1,0:T(8,128)(2,1)}, bf16[24,384]{1,0:T(8,128)(2,1)}, u32[]{:S(2)}, u32[]{:S(2)}) collective-permute-start(bf16[24,384]{1,0:T(8,128)(2,1)} %get-tuple-element.3), channel_id=1, source_target_pairs={{0,16},{1,17},{2,18},{3,19},{4,20},{5,21},{6,22},{7,23},{8,24},{9,... | collective-permute-start | bytes 55304 | tf_op jit(solution)/shard_map/ppermute | solution.py:31
  290.2 8.0 %collective-permute-start.26 = (bf16[24,384]{1,0:T(8,128)(2,1)}, bf16[24,384]{1,0:T(8,128)(2,1)S(1)}, u32[]{:S(2)}, u32[]{:S(2)}) collective-permute-start(bf16[24,384]{1,0:T(8,128)(2,1)} %get-tuple-element.3), channel_id=1, source_target_pairs={{0,32},{1,33},{2,34},{3,35},{4,36},{5,37},{6,38},{7,39},{8,40},{9,... | collective-permute-start | bytes 55304 | tf_op jit(solution)/shard_map/ppermute | solution.py:31
  295.0 4.7 %collective-permute-start.27 = (bf16[24,384]{1,0:T(8,128)(2,1)}, bf16[24,384]{1,0:T(8,128)(2,1)S(1)}, u32[]{:S(2)}, u32[]{:S(2)}) collective-permute-start(bf16[24,384]{1,0:T(8,128)(2,1)} %get-tuple-element.3), channel_id=1, source_target_pairs={{0,48},{1,49},{2,50},{3,51},{4,52},{5,53},{6,54},{7,55},{8,56},{9,... | collective-permute-start | bytes 55304 | tf_op jit(solution)/shard_map/ppermute | solution.py:31
  300.3 12.8 %collective-permute-start.28 = (bf16[24,1152]{1,0:T(8,128)(2,1)}, bf16[24,1152]{1,0:T(8,128)(2,1)S(1)}, u32[]{:S(2)}, u32[]{:S(2)}) collective-permute-start(bf16[24,1152]{1,0:T(8,128)(2,1)} %constant_dynamic-update-slice_fusion.4), channel_id=1, source_target_pairs={{0,128},{1,129},{2,130},{3,131},{4,132},{5,133},{6,134},{7,135},{8... | collective-permute-start | bytes 165896 | tf_op jit(solution)/shard_map/ppermute | solution.py:31
  304.8 8.3 %collective-permute-start.29 = (bf16[24,1152]{1,0:T(8,128)(2,1)}, bf16[24,1152]{1,0:T(8,128)(2,1)S(1)}, u32[]{:S(2)}, u32[]{:S(2)}) collective-permute-start(bf16[24,1152]{1,0:T(8,128)(2,1)} %constant_dynamic-update-slice_fusion.4), channel_id=1, source_target_pairs={{0,256},{1,257},{2,258},{3,259},{4,260},{5,261},{6,262},{7,263},{8... | collective-permute-start | bytes 165896 | tf_op jit(solution)/shard_map/ppermute | solution.py:31
  308.3 5.5 %collective-permute-start.30 = (bf16[24,1152]{1,0:T(8,128)(2,1)}, bf16[24,1152]{1,0:T(8,128)(2,1)S(1)}, u32[]{:S(2)}, u32[]{:S(2)}) collective-permute-start(bf16[24,1152]{1,0:T(8,128)(2,1)} %constant_dynamic-update-slice_fusion.4), channel_id=1, source_target_pairs={{0,384},{1,385},{2,386},{3,387},{4,388},{5,389},{6,390},{7,391},{8... | collective-permute-start | bytes 165896 | tf_op jit(solution)/shard_map/ppermute | solution.py:31
  313.8 10.7 %collective-permute-start.31 = (bf16[72,1152]{1,0:T(8,128)(2,1)S(1)}, bf16[72,1152]{1,0:T(8,128)(2,1)S(1)}, u32[]{:S(2)}, u32[]{:S(2)}) collective-permute-start(bf16[72,1152]{1,0:T(8,128)(2,1)S(1)} %constant_dynamic-update-slice_fusion), channel_id=1, source_target_pairs={{0,8},{1,9},{2,10},{3,11},{4,12},{5,13},{6,14},{7,15},{8,0},{9,1},... | collective-permute-start | bytes 497672 | tf_op jit(solution)/shard_map/ppermute | solution.py:31

commit v2 on v1

v2 whole, which is shorter than its diff:
```python
import jax
import jax.numpy as jnp
from jax import lax
from jax.sharding import PartitionSpec as P

STEPS = 4
SIDE = 4
CORES = 2
GROUP = SIDE * CORES
AXES = ("dp", "fsdp")


def along_chain(block, width, lanes, moves):
    groups = width // GROUP
    route = [
        ((g * GROUP + s) * lanes + q, ((g + dg) % groups * GROUP + t) * lanes + q)
        for g in range(groups)
        for q in range(lanes)
        for s, dg, t in moves
    ]
    return lax.ppermute(block, AXES, route)


def by_coords(block, width, lanes, target):
    route = []
    for p in range(width):
        for q in range(lanes):
            x, hi, y, core = p // 16, p // 8 % 2, p // 2 % 4, p % 2
            x2, hi2, y2, core2, q2 = target(x, hi, y, core, q)
            route.append((p * lanes + q, (((x2 * 2 + hi2) * 4 + y2) * 2 + core2) * lanes + q2))
    return lax.ppermute(block, AXES, route)


def on_device(image_features, head_weight, text_embeds, partner, logit_scale, logit_bias):
    bf16, f32 = jnp.bfloat16, jnp.float32
    rows = image_features.shape[0]
    depth = image_features.shape[1]
    width_dp = lax.axis_size("dp")
    lanes = lax.axis_size("fsdp")
    place = lax.axis_index("dp")
    lane = lax.axis_index("fsdp")
    slot = place % GROUP
    core = place % CORES
    at_y = place // CORES % SIDE
    at_x = place // (2 * GROUP)
    first, last = slot == 0, slot == GROUP - 1

    def chain(block, moves):
        return along_chain(block, width_dp, lanes, moves)

    def coords(block, target):
        return by_coords(block, width_dp, lanes, target)

    def core_swap(block):
        return coords(block, lambda x, hi, y, c, q: (x, hi, y, 1 - c, q))

    def x_shift(block, d):
        return coords(block, lambda x, hi, y, c, q: ((x + d) % SIDE, hi, y, c, q))

    def y_shift(block, d):
        return coords(block, lambda x, hi, y, c, q: (x, hi, (y + d) % SIDE, c, q))

    def x_flip(block, bit):
        return coords(block, lambda x, hi, y, c, q: (x ^ bit, hi, y, c, q))

    def y_flip(block, bit):
        return coords(block, lambda x, hi, y, c, q: (x, hi, y ^ bit, c, q))

    def z_flip(block, bit):
        return coords(block, lambda x, hi, y, c, q: (x, hi, y, c, q ^ bit))

    def hi_flip(block):
        return coords(block, lambda x, hi, y, c, q: (x, 1 - hi, y, c, q))

    held, cols = head_weight.shape
    half = held // CORES
    step = (half // SIDE) // 8 * 8
    window = half - (SIDE - 1) * step
    step_y = (cols // SIDE) // 128 * 128
    window_y = cols - (SIDE - 1) * step_y

    def in_order(mine, theirs, bit, axis):
        low = jnp.where(bit == 0, mine, theirs)
        high = jnp.where(bit == 0, theirs, mine)
        return jnp.concatenate([low, high], axis=axis)

    scale = jnp.exp(logit_scale[0])
    bias = logit_bias[0]

    def one_step(stage, *blocks):
        def unused(*_):
            return jax.tree.map(lambda r: jnp.zeros(r.shape, r.dtype), jax.eval_shape(stage, *blocks))

        return lax.cond(scale > 0.0, stage, unused, *blocks)

    def gather_z(mine):
        bit = 1
        while bit < lanes:
            mine = in_order(mine, z_flip(mine, bit), lane // bit % 2, 0)
            bit *= 2
        return mine

    def gather_rest(mine):
        pieces = [mine] + [y_shift(mine, d) for d in range(1, SIDE)]
        strip = jnp.zeros((lanes, window, cols), bf16)
        for d, piece in enumerate(pieces):
            strip = lax.dynamic_update_slice_in_dim(strip, piece, (at_y - d) % SIDE * step_y, 2)
        pieces = [strip] + [x_shift(strip, d) for d in range(1, SIDE)]
        ours = jnp.zeros((lanes, half, cols), bf16)
        for d, piece in enumerate(pieces):
            ours = lax.dynamic_update_slice_in_dim(ours, piece, (at_x - d) % SIDE * step, 1)
        return in_order(ours, core_swap(ours), core, 1).reshape(lanes * held, cols)

    def sum_xy(total):
        def cut_x(d):
            return lax.dynamic_slice_in_dim(total, (at_x + d) % SIDE * step, window, 1)

        sent = [x_shift(cut_x(d).astype(bf16), d) for d in range(1, SIDE)]
        total_x = cut_x(0)
        for piece in sent:
            total_x = total_x + piece.astype(f32)

        def cut_y(d):
            return lax.dynamic_slice_in_dim(total_x, (at_y + d) % SIDE * step_y, window_y, 2)

        sent = [y_shift(cut_y(d).astype(bf16), d) for d in range(1, SIDE)]
        total_y = cut_y(0)
        for piece in sent:
            total_y = total_y + piece.astype(f32)
        return total_y

    text_f = text_embeds.astype(f32)
    txt_norm = jnp.sqrt(jnp.sum(text_f * text_f, axis=1, keepdims=True) + 1e-06)
    unit_t = text_f / txt_norm
    unit_txt = unit_t.astype(bf16)
    down = [(s, 0, s - 1) for s in range(1, GROUP)]
    up = [(s, 0, s + 1) for s in range(GROUP - 1)]

    far = chain(unit_txt, [(0, -1, 7), (2, -1, 2)])
    ready, _ = lax.optimization_barrier((head_weight, unit_txt))
    mine = lax.dynamic_slice(
        ready, (core * half + at_x * step, at_y * step_y), (window, window_y)
    )[None]

    def gather(mine):
        mine, moved, near = one_step(
            lambda m: (gather_z(m), chain(unit_txt, [(1, 0, 6)]), chain(unit_txt, down)), mine
        )
        far_1 = chain(moved, [(6, -1, 6)])
        whole = one_step(gather_rest, mine)
        return *lax.optimization_barrier((whole, far_1)), near

    full_weight, far_1, near = one_step(gather, mine)
    full_weight, far = lax.optimization_barrier((full_weight, far))

    projected = jnp.dot(image_features, full_weight, preferred_element_type=f32)
    img_norm = jnp.sqrt(jnp.sum(projected * projected, axis=1, keepdims=True) + 1e-06)
    unit_f = projected / img_norm
    unit_img = unit_f.astype(bf16)

    offset = partner % rows
    ahead = (partner // (rows * lanes) - place) % width_dp
    code = jnp.concatenate([ahead, offset // 128, offset % 128]).astype(bf16)
    code = jnp.pad(code, (0, unit_img.shape[1] - code.shape[0]))
    code = jnp.pad(code[None, :], ((0, 7), (0, 0)))
    parcel = jnp.concatenate([unit_img, code], axis=0)

    back = chain(parcel, [(7, 1, 0), (5, 1, 5)])

    offsets = lax.iota(jnp.int32, rows)

    def pair_weight(logits, match):
        sign = jnp.where(match, 1.0, -1.0)
        weights = (-sign * jax.nn.sigmoid(-sign * logits)).astype(bf16)
        return lax.optimization_barrier(weights)

    def met_grad(text, k):
        logits = jnp.einsum("ie,je->ij", unit_img, text, preferred_element_type=f32)
        met = jnp.where(ahead == k, offset, -1)
        weights = pair_weight(scale * logits + bias, met[:, None] == offsets[None, :])
        return scale * jnp.dot(weights, text, preferred_element_type=f32)

    def meet_texts(far, near, far_1):
        far_2 = chain(far, [(2, 0, 7)])
        text_1 = jnp.where(last, far, near)
        text_2 = chain(text_1, down)
        text_3 = chain(text_2, down)
        far_3 = chain(far_1, [(6, 0, 7)])
        text_2 = jnp.where(last, far_2, text_2)
        text_3 = jnp.where(last, far_3, jnp.where(slot == GROUP - 2, far_1, text_3))
        texts = [
            (unit_txt, 0),
            (text_1, 1),
            (text_2, jnp.where(last, 3, 2)),
            (text_3, jnp.where(last, 2, 3)),
        ]
        img_grad = 0.0
        for text, k in texts[:-1]:
            img_grad = img_grad + met_grad(text, k)
        back_0 = chain(parcel, [(6, 0, 1)])
        return img_grad, text_3, back_0, chain(parcel, up)

    def head_terms(img_grad, text):
        img_grad = img_grad + met_grad(text, jnp.where(last, 2, 3))
        proj_grad = (
            (img_grad - unit_f * jnp.sum(unit_f * img_grad, axis=1, keepdims=True)) / img_norm
        ).astype(bf16)
        term = jnp.einsum(
            "rd,re->de", image_features, proj_grad, preferred_element_type=f32
        ).astype(bf16)
        term = term.reshape(lanes, CORES, half, cols)
        ours = lax.dynamic_index_in_dim(term, core, 1, keepdims=False)
        theirs = lax.dynamic_index_in_dim(term, 1 - core, 1, keepdims=False)
        return ours.astype(f32) + core_swap(theirs).astype(f32)

    def sum_z(total):
        bit = lanes // 2
        while bit:
            halves = total.reshape(2, bit, window, window_y)
            side = lane // bit % 2
            keep = lax.dynamic_index_in_dim(halves, side, 0, keepdims=False)
            give = lax.dynamic_index_in_dim(halves, 1 - side, 0, keepdims=False)
            total = keep + z_flip(give.astype(bf16), bit).astype(f32)
            bit //= 2
        total = total.reshape(window, window_y)
        return (total + hi_flip(total)).astype(bf16)

    img_grad, text, back_0, beside = one_step(meet_texts, far, near, far_1)
    back_1 = chain(back_0, [(1, 1, 1)])
    total = one_step(lambda *blocks: sum_xy(head_terms(*blocks)), img_grad, text)
    total, back, back_1 = lax.optimization_barrier((total, back, back_1))
    back_2 = chain(back, [(5, 0, 0)])
    image_1 = jnp.where(first, back, beside)
    image_2 = chain(image_1, up)
    total_z = one_step(sum_z, total)
    total_z, back_2, image_2, parcel, image_1 = lax.optimization_barrier(
        (total_z, back_2, image_2, parcel, image_1)
    )
    image_3 = chain(image_2, up)
    back_3 = chain(back_1, [(1, 0, 0)])
    image_2 = jnp.where(first, back_2, image_2)
    image_3 = jnp.where(first, back_3, jnp.where(slot == 1, back_1, image_3))

    strips = total_z[None]
    for bit in (1, 2):
        strips = in_order(strips, y_flip(strips, bit), at_y // bit % 2, 0)
    strip = jnp.concatenate(
        [strips[j, :, :step_y] for j in range(SIDE - 1)] + [strips[SIDE - 1]], axis=1
    )[None]
    for bit in (1, 2):
        strip = in_order(strip, x_flip(strip, bit), at_x // bit % 2, 0)
    ours = jnp.concatenate(
        [strip[j, :step] for j in range(SIDE - 1)] + [strip[SIDE - 1]], axis=0
    )
    head_grad = in_order(ours, core_swap(ours), core, 0).astype(f32)

    images = [
        (parcel, 0),
        (image_1, 1),
        (image_2, jnp.where(first, 3, 2)),
        (image_3, jnp.where(first, 2, 3)),
    ]

    txt_grad = 0.0
    for image, k in images:
        unit, marks = image[:rows], image[rows].astype(f32).astype(jnp.int32)
        met = marks[rows : 2 * rows] * 128 + marks[2 * rows : 3 * rows]
        met = jnp.where(marks[:rows] == k, met, -1)
        logits = scale * jnp.einsum("je,ie->ji", unit_txt, unit, preferred_element_type=f32) + bias
        weights = pair_weight(logits, met[None, :] == offsets[:, None])
        txt_grad = txt_grad + scale * jnp.dot(weights, unit, preferred_element_type=f32)
    text_grad = (
        (txt_grad - unit_t * jnp.sum(unit_t * txt_grad, axis=1, keepdims=True)) / txt_norm
    ).astype(bf16)
    return (text_grad, head_grad)


def solution(mesh):
    in_specs = (
        P(("dp", "fsdp"), None),
        P("fsdp", None),
        P(("dp", "fsdp"), None),
        P(("dp", "fsdp")),
        P(),
        P(),
    )
    out_specs = (P(("dp", "fsdp"), None), P("fsdp", None))
    return jax.shard_map(
        on_device, mesh=mesh, in_specs=in_specs, out_specs=out_specs, check_vma=False
    )
```

time: 327 us -> 350 us (1.070)
  waiting for transfers between devices: 40.2 us -> 134 us
  blocking collectives: 45.7 us -> 0 us
  starting transfers between devices: 165 us -> 145 us
  matrix products: 41.4 us -> 31.5 us
    ppermute x22 -> x26, waiting for transfers between devices: 28.7 us -> 120 us  [by_coords(): return lax.ppermute(block, AXES, route)]
    all_gather x1 -> x0, blocking collectives: 45.7 us -> none  [weight(): mine = lax.all_gather(mine, 'fsdp', axis=0, tiled=False)]
    ppermute x22 -> x26, starting transfers between devices: 108 us -> 89.1 us  [by_coords(): return lax.ppermute(block, AXES, route)]
    dot_general x4, matrix products: 17.3 us -> 3.94 us  [on_device(): jnp.dot(weights, unit, preferred_element_type=f32)]
    dynamic_update_slice x11 -> x8, local copies, waits for them, and re-layouts: 6.7 us -> 0.29 us  [the longest x4 0.18 us: gather_rest(): lax.dynamic_update_slice_in_dim(ours, piece, (at_x - d) % SIDE * step, 1)]
    ppermute x10 -> x16, waiting for transfers between devices: 11.5 us -> 14.1 us  [along_chain(): return lax.ppermute(block, AXES, route)]
    select_n x11 -> x16, other arithmetic: 10.5 us -> 8.02 us  [the longest x1 2.21 us: meet_texts(): text_3 = jnp.where(last, far_3, jnp.where(slot == GROUP - 2, far_1, text_3))]
    dot_general x5 -> x13, matrix products: 22.5 us -> 24 us  [the longest x4 10.7 us: met_grad(): logits = jnp.einsum('ie,je->ij', unit_img, text, preferred_element_type=f32)]
  transfers between devices with their start and end apart: 32 -> 42, of which waited for: 11 -> 24; matrix products, arithmetic and copies ran while one was open for 21% -> 14% of each run, Pallas kernels for 0% -> 0%
where the time goes in v2:
time: 350 us; the launch traced here: 348 us
  starting transfers between devices  145 us (41%)
  waiting for transfers between devices  134 us (38%)
  matrix products  31.5 us (9%)
  other arithmetic  23.9 us (7%)
  local copies, waits for them, and re-layouts  10.1 us (3%)
    ppermute x26, waiting for transfers between devices, by_coords(): return lax.ppermute(block, AXES, route)  120 us
    ppermute x26, starting transfers between devices, by_coords(): return lax.ppermute(block, AXES, route)  89.1 us
    ppermute x16, starting transfers between devices, along_chain(): return lax.ppermute(block, AXES, route)  55.7 us
    ppermute x16, waiting for transfers between devices, along_chain(): return lax.ppermute(block, AXES, route)  14.1 us
    dot_general x4, matrix products, met_grad(): logits = jnp.einsum('ie,je->ij', unit_img, text, preferred_element_type=f32)  10.7 us
    dot_general x4, matrix products, met_grad(): return scale * jnp.dot(weights, text, preferred_element_type=f32)  7.08 us
  transfers between devices with their start and end apart: 42, of which 24 were waited for; matrix products, arithmetic and copies ran while one was open for 14% of the time, Pallas kernels for 0%

profile of v2, /device:TPU:1, one launch (start us, length us, event | category | flops | bytes accessed | tf_op | source)
XLA Modules:
  0.0 347.9 jit_solution(6972519385334470307)
XLA Ops:
  7.1 119.0 %conditional.6 = (bf16[1152,1152]{1,0:T(8,128)(2,1)}, bf16[384,1152]{1,0:T(8,128)(2,1)}, bf16[384,1152]{1,0:T(8,128)(2,1)}) conditional(s32[]{:T(128)} %convert_element_type.174, () %tuple.79, (f32[]{:T(128)}, s32[]{:T(128)}, s32[]{:T(128)}, s32[]{:T(128)}, s32[]{:T(128)}, /*index=5*/bf16[144,1152]{1,0:T(8,128)(2,1)}, ...), branch_computations={%region_1.2_spmd, %region_2.7_spmd} | conditional | flops 6949057 | bytes 41695880 | solution.py:94
  7.1 65.8 %conditional = (bf16[8,24,384]{2,1,0:T(8,128)(2,1)S(1)}, bf16[384,1152]{1,0:T(8,128)(2,1)}, bf16[384,1152]{1,0:T(8,128)(2,1)}) conditional(s32[]{:T(128)} %convert_element_type.124, () %tuple.56, (s32[]{:T(128)}, s32[]{:T(128)}, s32[]{:T(128)}, s32[]{:T(128)}, bf16[144,1152]{1,0:T(8,128)(2,1)}, /*index=5*/bf16[384,1152]{1,0:T(8,128)(2,1)S(1)}) %tuple.57), branch_computations={%region_3.3_spmd, %region_4.4_spmd} | conditional | flops 313408 | bytes 8663934 | solution.py:94
  7.8 4.4 %collective-permute-start = (bf16[1,24,384]{2,1,0:T(8,128)(2,1)S(1)}, bf16[1,24,384]{2,1,0:T(8,128)(2,1)S(1)}, u32[]{:S(2)}, u32[]{:S(2)}) collective-permute-start(bf16[1,24,384]{2,1,0:T(8,128)(2,1)S(1)} %dynamic-slice_bitcast_fusion), channel_id=1, source_target_pairs={{0,1},{1,0},{2,3},{3,2},{4,5},{5,4},{6,7},{7,6},{8,9},{9,8},{10,11... | collective-permute-start | bytes 55304 | tf_op jit(solution)/shard_map/cond/branch_1_fun/cond/branch_1_fun/ppermute | solution.py:31
  12.2 6.4 %collective-permute-start.3 = (bf16[384,1152]{1,0:T(8,128)(2,1)S(1)}, bf16[384,1152]{1,0:T(8,128)(2,1)}, u32[]{:S(2)}, u32[]{:S(2)}) collective-permute-start(bf16[384,1152]{1,0:T(8,128)(2,1)S(1)} %get-tuple-element.164), channel_id=1, source_target_pairs={{8,48},{9,49},{10,50},{11,51},{12,52},{13,53},{14,54},{15,55},{72,... | collective-permute-start | bytes 2654216 | tf_op jit(solution)/shard_map/cond/branch_1_fun/cond/branch_1_fun/ppermute | solution.py:21
  18.6 16.3 %collective-permute-start.4 = (bf16[384,1152]{1,0:T(8,128)(2,1)S(1)}, bf16[384,1152]{1,0:T(8,128)(2,1)}, u32[]{:S(2)}, u32[]{:S(2)}) collective-permute-start(bf16[384,1152]{1,0:T(8,128)(2,1)S(1)} %get-tuple-element.164), channel_id=1, source_target_pairs={{8,0},{16,8},{24,16},{32,24},{40,32},{48,40},{56,48},{9,1},{17,9},... | collective-permute-start | bytes 2654216 | tf_op jit(solution)/shard_map/cond/branch_1_fun/cond/branch_1_fun/ppermute | solution.py:21
  35.6 3.1 collective-permute-start.1
  38.8 24.9 %collective-permute-done.1 = bf16[2,24,384]{2,1,0:T(8,128)(2,1)S(1)} collective-permute-done((bf16[2,24,384]{2,1,0:T(8,128)(2,1)S(1)}, bf16[2,24,384]{2,1,0:T(8,128)(2,1)S(1)}, u32[]{:S(2)}, u32[]{:S(2)}) %collective-permute-start.1) | collective-permute-done | bytes 36896 | tf_op jit(solution)/shard_map/cond/branch_1_fun/cond/branch_1_fun/ppermute | solution.py:31
  63.7 1.9 collective-permute-start.2
  65.6 7.1 %collective-permute-done.2 = bf16[4,24,384]{2,1,0:T(8,128)(2,1)S(1)} collective-permute-done((bf16[4,24,384]{2,1,0:T(8,128)(2,1)S(1)}, bf16[4,24,384]{2,1,0:T(8,128)(2,1)S(1)}, u32[]{:S(2)}, u32[]{:S(2)}) %collective-permute-start.2) | collective-permute-done | bytes 73760 | tf_op jit(solution)/shard_map/cond/branch_1_fun/cond/branch_1_fun/ppermute | solution.py:31
  74.4 51.6 %conditional.1 = (bf16[1152,1152]{1,0:T(8,128)(2,1)}) conditional(s32[]{:T(128)} %convert_element_type.124, () %tuple.55, (s32[]{:T(128)}, s32[]{:T(128)}, bf16[8,24,384]{2,1,0:T(8,128)(2,1)S(1)}, s32[]{:T(128)}) %tuple.58), branch_computations={%region_5.5_spmd, %region_6.6_spmd} | conditional | flops 6635647 | bytes 29492844 | solution.py:94
  74.4 3.8 %collective-permute-start.5 = (bf16[8,24,384]{2,1,0:T(8,128)(2,1)S(1)}, bf16[8,24,384]{2,1,0:T(8,128)(2,1)S(1)}, u32[]{:S(2)}, u32[]{:S(2)}) collective-permute-start(bf16[8,24,384]{2,1,0:T(8,128)(2,1)S(1)} %get-tuple-element.166), channel_id=1, source_target_pairs={{0,16},{1,17},{2,18},{3,19},{4,20},{5,21},{6,22},{7,23},{8,24},{9,... | collective-permute-start | bytes 442376 | tf_op jit(solution)/shard_map/cond/branch_1_fun/cond/branch_1_fun/ppermute | solution.py:31
  78.3 1.9 collective-permute-start.6
  80.2 4.3 %collective-permute-start.7 = (bf16[8,24,384]{2,1,0:T(8,128)(2,1)S(1)}, bf16[8,24,384]{2,1,0:T(8,128)(2,1)S(1)}, u32[]{:S(2)}, u32[]{:S(2)}) collective-permute-start(bf16[8,24,384]{2,1,0:T(8,128)(2,1)S(1)} %get-tuple-element.166), channel_id=1, source_target_pairs={{0,48},{1,49},{2,50},{3,51},{4,52},{5,53},{6,54},{7,55},{8,56},{9,... | collective-permute-start | bytes 442376 | tf_op jit(solution)/shard_map/cond/branch_1_fun/cond/branch_1_fun/ppermute | solution.py:31
  86.6 1.9 collective-permute-start.8
  88.6 4.6 %collective-permute-start.9 = (bf16[8,24,1152]{2,1,0:T(8,128)(2,1)S(1)}, bf16[8,24,1152]{2,1,0:T(8,128)(2,1)S(1)}, u32[]{:S(2)}, u32[]{:S(2)}) collective-permute-start(bf16[8,24,1152]{2,1,0:T(8,128)(2,1)S(1)} %constant_dynamic-update-slice_fusion.4), channel_id=1, source_target_pairs={{0,256},{1,257},{2,258},{3,259},{4,260},{5,261},{6,262},{7,263},{8... | collective-permute-start | bytes 1327112 | tf_op jit(solution)/shard_map/cond/branch_1_fun/cond/branch_1_fun/ppermute | solution.py:31
  93.3 2.7 collective-permute-start.10
  97.2 4.5 %collective-permute-done.9 = bf16[8,24,1152]{2,1,0:T(8,128)(2,1)S(1)} collective-permute-done((bf16[8,24,1152]{2,1,0:T(8,128)(2,1)S(1)}, bf16[8,24,1152]{2,1,0:T(8,128)(2,1)S(1)}, u32[]{:S(2)}, u32[]{:S(2)}) %collective-permute-start.9) | collective-permute-done | bytes 442400 | tf_op jit(solution)/shard_map/cond/branch_1_fun/cond/branch_1_fun/ppermute | solution.py:31
  101.7 2.5 collective-permute-done.10
  104.3 17.1 %collective-permute-start.11 = (bf16[8,72,1152]{2,1,0:T(8,128)(2,1)S(1)}, bf16[8,72,1152]{2,1,0:T(8,128)(2,1)S(1)}, u32[]{:S(2)}, u32[]{:S(2)}) collective-permute-start(bf16[8,72,1152]{2,1,0:T(8,128)(2,1)S(1)} %constant_dynamic-update-slice_fusion), channel_id=1, source_target_pairs={{0,8},{1,9},{2,10},{3,11},{4,12},{5,13},{6,14},{7,15},{8,0},{9,1},... | collective-permute-start | bytes 3981320 | tf_op jit(solution)/shard_map/cond/branch_1_fun/cond/branch_1_fun/ppermute | solution.py:31
  121.4 2.7 collective-permute-done.11
  126.8 3.6 %multiply_reduce_fusion.2 = (f32[384]{0:T(512)S(1)}, f32[1152,384]{0,1:T(8,128)S(1)}) fusion(bf16[384,1152]{1,0:T(8,128)(2,1)} %param.18, bf16[1152,1152]{1,0:T(8,128)(2,1)} %get-tuple-element.235), kind=kOutput, calls=%fused_computation.104 | convolution fusion | flops 1020100224 | bytes 5309952 | tf_op jit(solution)/shard_map/dot_general | solution.py:156
  133.5 45.1 %conditional.7 = (f32[384,1152]{1,0:T(8,128)}, bf16[384,1152]{1,0:T(8,128)(2,1)}, bf16[392,1152]{1,0:T(8,128)(2,1)}, bf16[392,1152]{1,0:T(8,128)(2,1)}) conditional(s32[]{:T(128)} %convert_element_type.174, () %tuple.83, (f32[]{:T(128)}, s32[384]{0:T(512)S(1)}, s32[384]{0:T(512)S(1)}, s32[384]{0:T(512)S(1)}, s32[384]{0:T(512)S(1)}, ...), branch_computations={%region_8.9_spmd, %region_9.10_spmd} | conditional | flops 2047281408 | bytes 59740032 | solution.py:94
  134.7 4.2 %collective-permute-start.22 = (bf16[392,1152]{1,0:T(8,128)(2,1)}, bf16[392,1152]{1,0:T(8,128)(2,1)}, u32[]{:S(2)}, u32[]{:S(2)}) collective-permute-start(bf16[392,1152]{1,0:T(8,128)(2,1)} %get-tuple-element.195), channel_id=1, source_target_pairs={{0,8},{8,16},{16,24},{24,32},{32,40},{40,48},{48,56},{1,9},{9,17},... | collective-permute-start | bytes 2709512 | tf_op jit(solution)/shard_map/cond/branch_1_fun/ppermute | solution.py:21
  141.8 1.9 collective-permute-start.18
  147.1 3.2 fusion.6
  153.9 7.8 %collective-permute-done.18 = bf16[384,1152]{1,0:T(8,128)(2,1)} collective-permute-done((bf16[384,1152]{1,0:T(8,128)(2,1)S(1)}, bf16[384,1152]{1,0:T(8,128)(2,1)}, u32[]{:S(2)}, u32[]{:S(2)}) %collective-permute-start.18) | collective-permute-done | bytes 884768 | tf_op jit(solution)/shard_map/cond/branch_1_fun/ppermute | solution.py:21
  164.3 2.6 fusion.21
  166.9 3.1 fusion
  170.1 6.3 %collective-permute-done.20 = bf16[384,1152]{1,0:T(8,128)(2,1)} collective-permute-done((bf16[384,1152]{1,0:T(8,128)(2,1)}, bf16[384,1152]{1,0:T(8,128)(2,1)}, u32[]{:S(2)}, u32[]{:S(2)}) %collective-permute-start.20) | collective-permute-done | bytes 884768 | tf_op jit(solution)/shard_map/cond/branch_1_fun/ppermute | solution.py:21
  176.4 2.2 select_select_fusion
  180.2 3.8 %collective-permute-start.32 = (bf16[392,1152]{1,0:T(8,128)(2,1)}, bf16[392,1152]{1,0:T(8,128)(2,1)}, u32[]{:S(2)}, u32[]{:S(2)}) collective-permute-start(bf16[392,1152]{1,0:T(8,128)(2,1)} %get-tuple-element.241), channel_id=1, source_target_pairs={{8,72},{9,73},{10,74},{11,75},{12,76},{13,77},{14,78},{15,79},{72,... | collective-permute-start | bytes 2709512 | tf_op jit(solution)/shard_map/ppermute | solution.py:21
  184.5 74.2 %conditional.8 = (f32[8,24,384]{2,1,0:T(8,128)S(1)}) conditional(s32[]{:T(128)} %convert_element_type.174, () %tuple.78, (f32[]{:T(128)}, pred[]{:T(512)}, s32[384]{0:T(512)S(1)}, s32[384]{0:T(512)S(1)}, s32[384]{0:T(512)}, /*index=5*/bf16[384,1152]{1,0:T(8,128)(2,1)S(1)}, bf16[384,1152]{1,0:T(8,128)(2,1)}, f32[]{:T(128)}, f32[384,1152]{1,0:T(8,128)}, ...), branch_computations={%region_10.11_spmd, %region_11.13_spmd} | conditional | flops 1708942080 | bytes 68442920 | solution.py:94
  184.5 3.4 fusion.31
  188.0 2.7 multiply_reduce_fusion
  194.2 1.9 collective-permute-start.23
  196.2 3.1 collective-permute-done.23
  199.3 2.0 convert_add_fusion
  202.5 4.2 %collective-permute-start.26 = (bf16[8,24,1152]{2,1,0:T(8,128)(2,1)}, bf16[8,24,1152]{2,1,0:T(8,128)(2,1)}, u32[]{:S(2)}, u32[]{:S(2)}) collective-permute-start(bf16[8,24,1152]{2,1,0:T(8,128)(2,1)} %get-tuple-element.267), channel_id=1, source_target_pairs={{0,384},{1,385},{2,386},{3,387},{4,388},{5,389},{6,390},{7,391},{8... | collective-permute-start | bytes 1327112 | tf_op jit(solution)/shard_map/cond/branch_1_fun/ppermute | solution.py:31
  206.7 1.9 collective-permute-start.25
  208.6 2.5 collective-permute-start.24
  211.2 14.6 %collective-permute-done.26 = bf16[8,24,1152]{2,1,0:T(8,128)(2,1)} collective-permute-done((bf16[8,24,1152]{2,1,0:T(8,128)(2,1)}, bf16[8,24,1152]{2,1,0:T(8,128)(2,1)}, u32[]{:S(2)}, u32[]{:S(2)}) %collective-permute-start.26) | collective-permute-done | bytes 442400 | tf_op jit(solution)/shard_map/cond/branch_1_fun/ppermute | solution.py:31
  225.7 15.8 %collective-permute-done.24 = bf16[8,24,1152]{2,1,0:T(8,128)(2,1)} collective-permute-done((bf16[8,24,1152]{2,1,0:T(8,128)(2,1)}, bf16[8,24,1152]{2,1,0:T(8,128)(2,1)}, u32[]{:S(2)}, u32[]{:S(2)}) %collective-permute-start.24) | collective-permute-done | bytes 442400 | tf_op jit(solution)/shard_map/cond/branch_1_fun/ppermute | solution.py:31
  244.0 1.9 collective-permute-start.29
  245.9 1.9 collective-permute-start.28
  247.9 3.4 collective-permute-start.27
  251.3 3.0 collective-permute-done.28
  254.3 3.2 collective-permute-done.27
  261.6 1.9 collective-permute-start.34
  264.3 3.4 collective-permute-start.35
  267.8 34.2 %conditional.9 = (bf16[24,384]{1,0:T(8,128)(2,1)S(1)}) conditional(s32[]{:T(128)} %convert_element_type.174, () %tuple.77, (f32[8,24,384]{2,1,0:T(8,128)S(1)}, s32[]{:T(128)}) %tuple.130), branch_computations={%region_13.14_spmd, %region_14.15_spmd} | conditional | flops 147528 | bytes 1659820 | solution.py:94
  267.8 1.9 collective-permute-start.13
  269.7 8.4 %collective-permute-done.13 = bf16[4,24,384]{2,1,0:T(8,128)(2,1)S(1)} collective-permute-done((bf16[4,24,384]{2,1,0:T(8,128)(2,1)S(1)}, bf16[4,24,384]{2,1,0:T(8,128)(2,1)S(1)}, u32[]{:S(2)}, u32[]{:S(2)}) %collective-permute-start.13) | collective-permute-done | bytes 73760 | tf_op jit(solution)/shard_map/cond/branch_1_fun/ppermute | solution.py:31
  280.1 3.9 %collective-permute-done.14 = bf16[2,24,384]{2,1,0:T(8,128)(2,1)S(1)} collective-permute-done((bf16[2,24,384]{2,1,0:T(8,128)(2,1)S(1)}, bf16[2,24,384]{2,1,0:T(8,128)(2,1)S(1)}, u32[]{:S(2)}, u32[]{:S(2)}) %collective-permute-start.14) | collective-permute-done | bytes 36896 | tf_op jit(solution)/shard_map/cond/branch_1_fun/ppermute | solution.py:31
  284.1 1.9 collective-permute-start.15
  286.0 2.6 collective-permute-done.15
  288.6 2.1 collective-permute-start.16
  290.6 11.3 %collective-permute-done.16 = f32[24,384]{1,0:T(8,128)S(1)} collective-permute-done((f32[24,384]{1,0:T(8,128)S(1)}, f32[24,384]{1,0:T(8,128)S(1)}, u32[]{:S(2)}, u32[]{:S(2)}) %collective-permute-start.16) | collective-permute-done | bytes 36896 | tf_op jit(solution)/shard_map/cond/branch_1_fun/ppermute | solution.py:31
  303.6 5.0 %collective-permute-start.36 = (bf16[392,1152]{1,0:T(8,128)(2,1)S(1)}, bf16[392,1152]{1,0:T(8,128)(2,1)S(1)}, u32[]{:S(2)}, u32[]{:S(2)}) collective-permute-start(bf16[392,1152]{1,0:T(8,128)(2,1)S(1)} %collective-permute-done.34), channel_id=1, source_target_pairs={{0,8},{8,16},{16,24},{24,32},{32,40},{40,48},{48,56},{1,9},{9,17},... | collective-permute-start | bytes 2709512 | tf_op jit(solution)/shard_map/ppermute | solution.py:21
  308.8 7.0 %collective-permute-start.37 = (bf16[1,24,384]{2,1,0:T(8,128)(2,1)S(1)}, bf16[1,24,384]{2,1,0:T(8,128)(2,1)S(1)}, u32[]{:S(2)}, u32[]{:S(2)}) collective-permute-start(bf16[1,24,384]{2,1,0:T(8,128)(2,1)S(1)} %bitcast.124), channel_id=1, source_target_pairs={{0,16},{1,17},{2,18},{3,19},{4,20},{5,21},{6,22},{7,23},{8,24},{9,... | collective-permute-start | bytes 55304 | tf_op jit(solution)/shard_map/ppermute | solution.py:31
  315.7 2.0 fusion.66
  319.2 4.3 %collective-permute-start.38 = (bf16[2,24,384]{2,1,0:T(8,128)(2,1)S(1)}, bf16[2,24,384]{2,1,0:T(8,128)(2,1)S(1)}, u32[]{:S(2)}, u32[]{:S(2)}) collective-permute-start(bf16[2,24,384]{2,1,0:T(8,128)(2,1)S(1)} %pad_maximum_fusion.7), channel_id=1, source_target_pairs={{0,32},{1,33},{2,34},{3,35},{4,36},{5,37},{6,38},{7,39},{8,40},{9,... | collective-permute-start | bytes 110600 | tf_op jit(solution)/shard_map/ppermute | solution.py:31
  327.4 2.9 collective-permute-done.39
  333.1 5.4 %collective-permute-done.40 = bf16[2,24,1152]{2,1,0:T(8,128)(2,1)S(1)} collective-permute-done((bf16[2,24,1152]{2,1,0:T(8,128)(2,1)S(1)}, bf16[2,24,1152]{2,1,0:T(8,128)(2,1)S(1)}, u32[]{:S(2)}, u32[]{:S(2)}) %collective-permute-start.40) | collective-permute-done | bytes 110624 | tf_op jit(solution)/shard_map/ppermute | solution.py:31
  338.7 2.6 collective-permute-start.41
  (148 shorter events, 63.4 us)
Async XLA Ops:
  0.6 5.2 %copy-start.10 = (s32[384]{0:T(512)S(1)}, s32[384]{0:T(512)}, u32[]{:S(2)}) copy-start(s32[384]{0:T(512)} %param.21) | copy-start | bytes 4612
  3.5 123.2 %collective-permute-start.30 = (bf16[384,1152]{1,0:T(8,128)(2,1)S(1)}, bf16[384,1152]{1,0:T(8,128)(2,1)}, u32[]{:S(2)}, u32[]{:S(2)}) collective-permute-start(bf16[384,1152]{1,0:T(8,128)(2,1)S(1)} %fusion.95), channel_id=1, source_target_pairs={{0,504},{16,464},{1,505},{17,465},{2,506},{18,466},{3,507},{19,467... | collective-permute-start | bytes 2654216 | tf_op jit(solution)/shard_map/ppermute | solution.py:21
  7.8 27.1 %collective-permute-start = (bf16[1,24,384]{2,1,0:T(8,128)(2,1)S(1)}, bf16[1,24,384]{2,1,0:T(8,128)(2,1)S(1)}, u32[]{:S(2)}, u32[]{:S(2)}) collective-permute-start(bf16[1,24,384]{2,1,0:T(8,128)(2,1)S(1)} %dynamic-slice_bitcast_fusion), channel_id=1, source_target_pairs={{0,1},{1,0},{2,3},{3,2},{4,5},{5,4},{6,7},{7,6},{8,9},{9,8},{10,11... | collective-permute-start | bytes 55304 | tf_op jit(solution)/shard_map/cond/branch_1_fun/cond/branch_1_fun/ppermute | solution.py:31
  12.2 60.6 %collective-permute-start.3 = (bf16[384,1152]{1,0:T(8,128)(2,1)S(1)}, bf16[384,1152]{1,0:T(8,128)(2,1)}, u32[]{:S(2)}, u32[]{:S(2)}) collective-permute-start(bf16[384,1152]{1,0:T(8,128)(2,1)S(1)} %get-tuple-element.164), channel_id=1, source_target_pairs={{8,48},{9,49},{10,50},{11,51},{12,52},{13,53},{14,54},{15,55},{72,... | collective-permute-start | bytes 2654216 | tf_op jit(solution)/shard_map/cond/branch_1_fun/cond/branch_1_fun/ppermute | solution.py:21
  18.6 54.2 %collective-permute-start.4 = (bf16[384,1152]{1,0:T(8,128)(2,1)S(1)}, bf16[384,1152]{1,0:T(8,128)(2,1)}, u32[]{:S(2)}, u32[]{:S(2)}) collective-permute-start(bf16[384,1152]{1,0:T(8,128)(2,1)S(1)} %get-tuple-element.164), channel_id=1, source_target_pairs={{8,0},{16,8},{24,16},{32,24},{40,32},{48,40},{56,48},{9,1},{17,9},... | collective-permute-start | bytes 2654216 | tf_op jit(solution)/shard_map/cond/branch_1_fun/cond/branch_1_fun/ppermute | solution.py:21
  35.6 28.0 %collective-permute-start.1 = (bf16[2,24,384]{2,1,0:T(8,128)(2,1)S(1)}, bf16[2,24,384]{2,1,0:T(8,128)(2,1)S(1)}, u32[]{:S(2)}, u32[]{:S(2)}) collective-permute-start(bf16[2,24,384]{2,1,0:T(8,128)(2,1)S(1)} %pad_maximum_fusion.2), channel_id=1, source_target_pairs={{0,2},{1,3},{2,0},{3,1},{4,6},{5,7},{6,4},{7,5},{8,10},{9,11},{10,... | collective-permute-start | bytes 110600 | tf_op jit(solution)/shard_map/cond/branch_1_fun/cond/branch_1_fun/ppermute | solution.py:31
  63.7 9.1 %collective-permute-start.2 = (bf16[4,24,384]{2,1,0:T(8,128)(2,1)S(1)}, bf16[4,24,384]{2,1,0:T(8,128)(2,1)S(1)}, u32[]{:S(2)}, u32[]{:S(2)}) collective-permute-start(bf16[4,24,384]{2,1,0:T(8,128)(2,1)S(1)} %pad_maximum_fusion.1), channel_id=1, source_target_pairs={{0,4},{1,5},{2,6},{3,7},{4,0},{5,1},{6,2},{7,3},{8,12},{9,13},{10,... | collective-permute-start | bytes 221192 | tf_op jit(solution)/shard_map/cond/branch_1_fun/cond/branch_1_fun/ppermute | solution.py:31
  72.8 53.2 %collective-permute-start.12 = (bf16[384,1152]{1,0:T(8,128)(2,1)}, bf16[384,1152]{1,0:T(8,128)(2,1)}, u32[]{:S(2)}, u32[]{:S(2)}) collective-permute-start(bf16[384,1152]{1,0:T(8,128)(2,1)} %get-tuple-element.177), channel_id=1, source_target_pairs={{48,496},{49,497},{50,498},{51,499},{52,500},{53,501},{54,502},{55... | collective-permute-start | bytes 2654216 | tf_op jit(solution)/shard_map/cond/branch_1_fun/ppermute | solution.py:21
  74.4 10.3 %collective-permute-start.5 = (bf16[8,24,384]{2,1,0:T(8,128)(2,1)S(1)}, bf16[8,24,384]{2,1,0:T(8,128)(2,1)S(1)}, u32[]{:S(2)}, u32[]{:S(2)}) collective-permute-start(bf16[8,24,384]{2,1,0:T(8,128)(2,1)S(1)} %get-tuple-element.166), channel_id=1, source_target_pairs={{0,16},{1,17},{2,18},{3,19},{4,20},{5,21},{6,22},{7,23},{8,24},{9,... | collective-permute-start | bytes 442376 | tf_op jit(solution)/shard_map/cond/branch_1_fun/cond/branch_1_fun/ppermute | solution.py:31
  78.3 7.4 %collective-permute-start.6 = (bf16[8,24,384]{2,1,0:T(8,128)(2,1)S(1)}, bf16[8,24,384]{2,1,0:T(8,128)(2,1)S(1)}, u32[]{:S(2)}, u32[]{:S(2)}) collective-permute-start(bf16[8,24,384]{2,1,0:T(8,128)(2,1)S(1)} %get-tuple-element.166), channel_id=1, source_target_pairs={{0,32},{1,33},{2,34},{3,35},{4,36},{5,37},{6,38},{7,39},{8,40},{9,... | collective-permute-start | bytes 442376 | tf_op jit(solution)/shard_map/cond/branch_1_fun/cond/branch_1_fun/ppermute | solution.py:31
  80.2 6.4 %collective-permute-start.7 = (bf16[8,24,384]{2,1,0:T(8,128)(2,1)S(1)}, bf16[8,24,384]{2,1,0:T(8,128)(2,1)S(1)}, u32[]{:S(2)}, u32[]{:S(2)}) collective-permute-start(bf16[8,24,384]{2,1,0:T(8,128)(2,1)S(1)} %get-tuple-element.166), channel_id=1, source_target_pairs={{0,48},{1,49},{2,50},{3,51},{4,52},{5,53},{6,54},{7,55},{8,56},{9,... | collective-permute-start | bytes 442376 | tf_op jit(solution)/shard_map/cond/branch_1_fun/cond/branch_1_fun/ppermute | solution.py:31
  86.6 10.6 %collective-permute-start.8 = (bf16[8,24,1152]{2,1,0:T(8,128)(2,1)S(1)}, bf16[8,24,1152]{2,1,0:T(8,128)(2,1)S(1)}, u32[]{:S(2)}, u32[]{:S(2)}) collective-permute-start(bf16[8,24,1152]{2,1,0:T(8,128)(2,1)S(1)} %constant_dynamic-update-slice_fusion.4), channel_id=1, source_target_pairs={{0,128},{1,129},{2,130},{3,131},{4,132},{5,133},{6,134},{7,135},{8... | collective-permute-start | bytes 1327112 | tf_op jit(solution)/shard_map/cond/branch_1_fun/cond/branch_1_fun/ppermute | solution.py:31
  88.6 13.0 %collective-permute-start.9 = (bf16[8,24,1152]{2,1,0:T(8,128)(2,1)S(1)}, bf16[8,24,1152]{2,1,0:T(8,128)(2,1)S(1)}, u32[]{:S(2)}, u32[]{:S(2)}) collective-permute-start(bf16[8,24,1152]{2,1,0:T(8,128)(2,1)S(1)} %constant_dynamic-update-slice_fusion.4), channel_id=1, source_target_pairs={{0,256},{1,257},{2,258},{3,259},{4,260},{5,261},{6,262},{7,263},{8... | collective-permute-start | bytes 1327112 | tf_op jit(solution)/shard_map/cond/branch_1_fun/cond/branch_1_fun/ppermute | solution.py:31
  93.3 11.0 %collective-permute-start.10 = (bf16[8,24,1152]{2,1,0:T(8,128)(2,1)S(1)}, bf16[8,24,1152]{2,1,0:T(8,128)(2,1)S(1)}, u32[]{:S(2)}, u32[]{:S(2)}) collective-permute-start(bf16[8,24,1152]{2,1,0:T(8,128)(2,1)S(1)} %constant_dynamic-update-slice_fusion.4), channel_id=1, source_target_pairs={{0,384},{1,385},{2,386},{3,387},{4,388},{5,389},{6,390},{7,391},{8... | collective-permute-start | bytes 1327112 | tf_op jit(solution)/shard_map/cond/branch_1_fun/cond/branch_1_fun/ppermute | solution.py:31
  104.3 19.8 %collective-permute-start.11 = (bf16[8,72,1152]{2,1,0:T(8,128)(2,1)S(1)}, bf16[8,72,1152]{2,1,0:T(8,128)(2,1)S(1)}, u32[]{:S(2)}, u32[]{:S(2)}) collective-permute-start(bf16[8,72,1152]{2,1,0:T(8,128)(2,1)S(1)} %constant_dynamic-update-slice_fusion), channel_id=1, source_target_pairs={{0,8},{1,9},{2,10},{3,11},{4,12},{5,13},{6,14},{7,15},{8,0},{9,1},... | collective-permute-start | bytes 3981320 | tf_op jit(solution)/shard_map/cond/branch_1_fun/cond/branch_1_fun/ppermute | solution.py:31
  130.3 0.6 copy-start.8
  133.5 45.1 %collective-permute-start.21 = (bf16[392,1152]{1,0:T(8,128)(2,1)}, bf16[392,1152]{1,0:T(8,128)(2,1)}, u32[]{:S(2)}, u32[]{:S(2)}) collective-permute-start(bf16[392,1152]{1,0:T(8,128)(2,1)} %get-tuple-element.195), channel_id=1, source_target_pairs={{48,8},{49,9},{50,10},{51,11},{52,12},{53,13},{54,14},{55,15},{112... | collective-permute-start | bytes 2709512 | tf_op jit(solution)/shard_map/cond/branch_1_fun/ppermute | solution.py:21
  134.7 43.8 %collective-permute-start.22 = (bf16[392,1152]{1,0:T(8,128)(2,1)}, bf16[392,1152]{1,0:T(8,128)(2,1)}, u32[]{:S(2)}, u32[]{:S(2)}) collective-permute-start(bf16[392,1152]{1,0:T(8,128)(2,1)} %get-tuple-element.195), channel_id=1, source_target_pairs={{0,8},{8,16},{16,24},{24,32},{32,40},{40,48},{48,56},{1,9},{9,17},... | collective-permute-start | bytes 2709512 | tf_op jit(solution)/shard_map/cond/branch_1_fun/ppermute | solution.py:21
  138.9 25.3 %collective-permute-start.17 = (bf16[384,1152]{1,0:T(8,128)(2,1)}, bf16[384,1152]{1,0:T(8,128)(2,1)}, u32[]{:S(2)}, u32[]{:S(2)}) collective-permute-start(bf16[384,1152]{1,0:T(8,128)(2,1)} %get-tuple-element.190), channel_id=1, source_target_pairs={{16,56},{17,57},{18,58},{19,59},{20,60},{21,61},{22,62},{23,63},{8... | collective-permute-start | bytes 2654216 | tf_op jit(solution)/shard_map/cond/branch_1_fun/ppermute | solution.py:21
  141.8 10.0 %copy-start.2 = (bf16[384,1152]{1,0:T(8,128)(2,1)}, bf16[384,1152]{1,0:T(8,128)(2,1)S(1)}, u32[]{:S(2)}) copy-start(bf16[384,1152]{1,0:T(8,128)(2,1)S(1)} %broadcast_select_fusion.9) | copy-start | bytes 2654212 | tf_op jit(solution)/shard_map/cond
  141.8 19.9 %collective-permute-start.18 = (bf16[384,1152]{1,0:T(8,128)(2,1)S(1)}, bf16[384,1152]{1,0:T(8,128)(2,1)}, u32[]{:S(2)}, u32[]{:S(2)}) collective-permute-start(bf16[384,1152]{1,0:T(8,128)(2,1)S(1)} %broadcast_select_fusion.9), channel_id=1, source_target_pairs={{8,0},{16,8},{24,16},{32,24},{40,32},{48,40},{56,48},{9,1},{17,9},... | collective-permute-start | bytes 2654216 | tf_op jit(solution)/shard_map/cond/branch_1_fun/ppermute | solution.py:21
  143.8 26.3 %collective-permute-start.19 = (bf16[384,1152]{1,0:T(8,128)(2,1)}, bf16[384,1152]{1,0:T(8,128)(2,1)}, u32[]{:S(2)}, u32[]{:S(2)}) collective-permute-start(bf16[384,1152]{1,0:T(8,128)(2,1)} %get-tuple-element.193), channel_id=1, source_target_pairs={{48,56},{49,57},{50,58},{51,59},{52,60},{53,61},{54,62},{55,63},{1... | collective-permute-start | bytes 2654216 | tf_op jit(solution)/shard_map/cond/branch_1_fun/ppermute | solution.py:21
  153.3 10.3 %copy-start.3 = (bf16[384,1152]{1,0:T(8,128)(2,1)S(1)}, bf16[384,1152]{1,0:T(8,128)(2,1)}, u32[]{:S(2)}) copy-start(bf16[384,1152]{1,0:T(8,128)(2,1)} %copy-done.2) | copy-start | bytes 2654212 | tf_op jit(solution)/shard_map/cond
  161.7 14.7 %collective-permute-start.20 = (bf16[384,1152]{1,0:T(8,128)(2,1)}, bf16[384,1152]{1,0:T(8,128)(2,1)}, u32[]{:S(2)}, u32[]{:S(2)}) collective-permute-start(bf16[384,1152]{1,0:T(8,128)(2,1)} %collective-permute-done.18), channel_id=1, source_target_pairs={{8,0},{16,8},{24,16},{32,24},{40,32},{48,40},{56,48},{9,1},{17,9},... | collective-permute-start | bytes 2654216 | tf_op jit(solution)/shard_map/cond/branch_1_fun/ppermute | solution.py:21
  178.6 80.1 %collective-permute-start.31 = (bf16[392,1152]{1,0:T(8,128)(2,1)}, bf16[392,1152]{1,0:T(8,128)(2,1)}, u32[]{:S(2)}, u32[]{:S(2)}) collective-permute-start(bf16[392,1152]{1,0:T(8,128)(2,1)} %pad_maximum_fusion.4), channel_id=1, source_target_pairs={{56,64},{40,104},{57,65},{41,105},{58,66},{42,106},{59,67},{43,107... | collective-permute-start | bytes 2709512 | tf_op jit(solution)/shard_map/ppermute | solution.py:21
  180.2 78.5 %collective-permute-start.32 = (bf16[392,1152]{1,0:T(8,128)(2,1)}, bf16[392,1152]{1,0:T(8,128)(2,1)}, u32[]{:S(2)}, u32[]{:S(2)}) collective-permute-start(bf16[392,1152]{1,0:T(8,128)(2,1)} %get-tuple-element.241), channel_id=1, source_target_pairs={{8,72},{9,73},{10,74},{11,75},{12,76},{13,77},{14,78},{15,79},{72,... | collective-permute-start | bytes 2709512 | tf_op jit(solution)/shard_map/ppermute | solution.py:21
  184.5 3.5 copy-start.9
  184.5 3.5 copy-start.1
  188.0 2.7 copy-start.11
  192.5 1.6 copy-start.5
  194.2 5.1 %collective-permute-start.23 = (bf16[8,72,1152]{2,1,0:T(8,128)(2,1)S(1)}, bf16[8,72,1152]{2,1,0:T(8,128)(2,1)}, u32[]{:S(2)}, u32[]{:S(2)}) collective-permute-start(bf16[8,72,1152]{2,1,0:T(8,128)(2,1)S(1)} %dynamic-slice_bitcast_fusion.1), channel_id=1, source_target_pairs={{0,8},{1,9},{2,10},{3,11},{4,12},{5,13},{6,14},{7,15},{8,0},{9,1},... | collective-permute-start | bytes 3981320 | tf_op jit(solution)/shard_map/cond/branch_1_fun/ppermute | solution.py:31
  202.5 23.3 %collective-permute-start.26 = (bf16[8,24,1152]{2,1,0:T(8,128)(2,1)}, bf16[8,24,1152]{2,1,0:T(8,128)(2,1)}, u32[]{:S(2)}, u32[]{:S(2)}) collective-permute-start(bf16[8,24,1152]{2,1,0:T(8,128)(2,1)} %get-tuple-element.267), channel_id=1, source_target_pairs={{0,384},{1,385},{2,386},{3,387},{4,388},{5,389},{6,390},{7,391},{8... | collective-permute-start | bytes 1327112 | tf_op jit(solution)/shard_map/cond/branch_1_fun/ppermute | solution.py:31
  206.7 19.1 %collective-permute-start.25 = (bf16[8,24,1152]{2,1,0:T(8,128)(2,1)}, bf16[8,24,1152]{2,1,0:T(8,128)(2,1)}, u32[]{:S(2)}, u32[]{:S(2)}) collective-permute-start(bf16[8,24,1152]{2,1,0:T(8,128)(2,1)} %get-tuple-element.268), channel_id=1, source_target_pairs={{0,256},{1,257},{2,258},{3,259},{4,260},{5,261},{6,262},{7,263},{8... | collective-permute-start | bytes 1327112 | tf_op jit(solution)/shard_map/cond/branch_1_fun/ppermute | solution.py:31
  208.6 32.9 %collective-permute-start.24 = (bf16[8,24,1152]{2,1,0:T(8,128)(2,1)}, bf16[8,24,1152]{2,1,0:T(8,128)(2,1)}, u32[]{:S(2)}, u32[]{:S(2)}) collective-permute-start(bf16[8,24,1152]{2,1,0:T(8,128)(2,1)} %get-tuple-element.266), channel_id=1, source_target_pairs={{0,128},{1,129},{2,130},{3,131},{4,132},{5,133},{6,134},{7,135},{8... | collective-permute-start | bytes 1327112 | tf_op jit(solution)/shard_map/cond/branch_1_fun/ppermute | solution.py:31
  243.0 1.0 copy-start.4
  244.0 7.3 %collective-permute-start.29 = (bf16[8,24,384]{2,1,0:T(8,128)(2,1)S(1)}, bf16[8,24,384]{2,1,0:T(8,128)(2,1)S(1)}, u32[]{:S(2)}, u32[]{:S(2)}) collective-permute-start(bf16[8,24,384]{2,1,0:T(8,128)(2,1)S(1)} %get-tuple-element.270), channel_id=1, source_target_pairs={{0,48},{1,49},{2,50},{3,51},{4,52},{5,53},{6,54},{7,55},{8,56},{9,... | collective-permute-start | bytes 442376 | tf_op jit(solution)/shard_map/cond/branch_1_fun/ppermute | solution.py:31
  245.9 8.3 %collective-permute-start.28 = (bf16[8,24,384]{2,1,0:T(8,128)(2,1)S(1)}, bf16[8,24,384]{2,1,0:T(8,128)(2,1)S(1)}, u32[]{:S(2)}, u32[]{:S(2)}) collective-permute-start(bf16[8,24,384]{2,1,0:T(8,128)(2,1)S(1)} %get-tuple-element.271), channel_id=1, source_target_pairs={{0,32},{1,33},{2,34},{3,35},{4,36},{5,37},{6,38},{7,39},{8,40},{9,... | collective-permute-start | bytes 442376 | tf_op jit(solution)/shard_map/cond/branch_1_fun/ppermute | solution.py:31
  247.9 9.6 %collective-permute-start.27 = (bf16[8,24,384]{2,1,0:T(8,128)(2,1)S(1)}, bf16[8,24,384]{2,1,0:T(8,128)(2,1)S(1)}, u32[]{:S(2)}, u32[]{:S(2)}) collective-permute-start(bf16[8,24,384]{2,1,0:T(8,128)(2,1)S(1)} %get-tuple-element.269), channel_id=1, source_target_pairs={{0,16},{1,17},{2,18},{3,19},{4,20},{5,21},{6,22},{7,23},{8,24},{9,... | collective-permute-start | bytes 442376 | tf_op jit(solution)/shard_map/cond/branch_1_fun/ppermute | solution.py:31
  258.7 1.6 copy-start.6
  258.7 43.3 %collective-permute-start.33 = (bf16[392,1152]{1,0:T(8,128)(2,1)}, bf16[392,1152]{1,0:T(8,128)(2,1)}, u32[]{:S(2)}, u32[]{:S(2)}) collective-permute-start(bf16[392,1152]{1,0:T(8,128)(2,1)} %collective-permute-done.31), channel_id=1, source_target_pairs={{40,0},{41,1},{42,2},{43,3},{44,4},{45,5},{46,6},{47,7},{104,64},{... | collective-permute-start | bytes 2709512 | tf_op jit(solution)/shard_map/ppermute | solution.py:21
  260.3 4.0 %copy-start.7 = (f32[8,24,384]{2,1,0:T(8,128)S(1)}, f32[8,24,384]{2,1,0:T(8,128)}, u32[]{:S(2)}) copy-start(f32[8,24,384]{2,1,0:T(8,128)} %copy-done.6) | copy-start | bytes 884740
  261.6 40.4 %collective-permute-start.34 = (bf16[392,1152]{1,0:T(8,128)(2,1)S(1)}, bf16[392,1152]{1,0:T(8,128)(2,1)S(1)}, u32[]{:S(2)}, u32[]{:S(2)}) collective-permute-start(bf16[392,1152]{1,0:T(8,128)(2,1)S(1)} %broadcast_select_fusion.13), channel_id=1, source_target_pairs={{0,8},{8,16},{16,24},{24,32},{32,40},{40,48},{48,56},{1,9},{9,17},... | collective-permute-start | bytes 2709512 | tf_op jit(solution)/shard_map/ppermute | solution.py:21
  264.3 78.9 %collective-permute-start.35 = (bf16[392,1152]{1,0:T(8,128)(2,1)}, bf16[392,1152]{1,0:T(8,128)(2,1)}, u32[]{:S(2)}, u32[]{:S(2)}) collective-permute-start(bf16[392,1152]{1,0:T(8,128)(2,1)} %collective-permute-done.32), channel_id=1, source_target_pairs={{8,0},{9,1},{10,2},{11,3},{12,4},{13,5},{14,6},{15,7},{72,64},{73,... | collective-permute-start | bytes 2709512 | tf_op jit(solution)/shard_map/ppermute | solution.py:21
  267.8 10.3 %collective-permute-start.13 = (bf16[4,24,384]{2,1,0:T(8,128)(2,1)S(1)}, bf16[4,24,384]{2,1,0:T(8,128)(2,1)S(1)}, u32[]{:S(2)}, u32[]{:S(2)}) collective-permute-start(bf16[4,24,384]{2,1,0:T(8,128)(2,1)S(1)} %fusion.34), channel_id=1, source_target_pairs={{0,4},{1,5},{2,6},{3,7},{4,0},{5,1},{6,2},{7,3},{8,12},{9,13},{10,... | collective-permute-start | bytes 221192 | tf_op jit(solution)/shard_map/cond/branch_1_fun/ppermute | solution.py:31
  278.2 5.9 %collective-permute-start.14 = (bf16[2,24,384]{2,1,0:T(8,128)(2,1)S(1)}, bf16[2,24,384]{2,1,0:T(8,128)(2,1)S(1)}, u32[]{:S(2)}, u32[]{:S(2)}) collective-permute-start(bf16[2,24,384]{2,1,0:T(8,128)(2,1)S(1)} %fusion.35), channel_id=1, source_target_pairs={{0,2},{1,3},{2,0},{3,1},{4,6},{5,7},{6,4},{7,5},{8,10},{9,11},{10,... | collective-permute-start | bytes 110600 | tf_op jit(solution)/shard_map/cond/branch_1_fun/ppermute | solution.py:31
  284.1 4.5 %collective-permute-start.15 = (bf16[1,24,384]{2,1,0:T(8,128)(2,1)S(1)}, bf16[1,24,384]{2,1,0:T(8,128)(2,1)S(1)}, u32[]{:S(2)}, u32[]{:S(2)}) collective-permute-start(bf16[1,24,384]{2,1,0:T(8,128)(2,1)S(1)} %dynamic-slice_convert_fusion.8), channel_id=1, source_target_pairs={{0,1},{1,0},{2,3},{3,2},{4,5},{5,4},{6,7},{7,6},{8,9},{9,8},{10,11... | collective-permute-start | bytes 55304 | tf_op jit(solution)/shard_map/cond/branch_1_fun/ppermute | solution.py:31
  288.6 13.4 %collective-permute-start.16 = (f32[24,384]{1,0:T(8,128)S(1)}, f32[24,384]{1,0:T(8,128)S(1)}, u32[]{:S(2)}, u32[]{:S(2)}) collective-permute-start(f32[24,384]{1,0:T(8,128)S(1)} %add_bitcast_fusion), channel_id=1, source_target_pairs={{0,64},{1,65},{2,66},{3,67},{4,68},{5,69},{6,70},{7,71},{8,72},{9,... | collective-permute-start | bytes 110600 | tf_op jit(solution)/shard_map/cond/branch_1_fun/ppermute | solution.py:31
  303.6 39.6 %collective-permute-start.36 = (bf16[392,1152]{1,0:T(8,128)(2,1)S(1)}, bf16[392,1152]{1,0:T(8,128)(2,1)S(1)}, u32[]{:S(2)}, u32[]{:S(2)}) collective-permute-start(bf16[392,1152]{1,0:T(8,128)(2,1)S(1)} %collective-permute-done.34), channel_id=1, source_target_pairs={{0,8},{8,16},{16,24},{24,32},{32,40},{40,48},{48,56},{1,9},{9,17},... | collective-permute-start | bytes 2709512 | tf_op jit(solution)/shard_map/ppermute | solution.py:21
  308.8 10.4 %collective-permute-start.37 = (bf16[1,24,384]{2,1,0:T(8,128)(2,1)S(1)}, bf16[1,24,384]{2,1,0:T(8,128)(2,1)S(1)}, u32[]{:S(2)}, u32[]{:S(2)}) collective-permute-start(bf16[1,24,384]{2,1,0:T(8,128)(2,1)S(1)} %bitcast.124), channel_id=1, source_target_pairs={{0,16},{1,17},{2,18},{3,19},{4,20},{5,21},{6,22},{7,23},{8,24},{9,... | collective-permute-start | bytes 55304 | tf_op jit(solution)/shard_map/ppermute | solution.py:31
  319.2 6.2 %collective-permute-start.38 = (bf16[2,24,384]{2,1,0:T(8,128)(2,1)S(1)}, bf16[2,24,384]{2,1,0:T(8,128)(2,1)S(1)}, u32[]{:S(2)}, u32[]{:S(2)}) collective-permute-start(bf16[2,24,384]{2,1,0:T(8,128)(2,1)S(1)} %pad_maximum_fusion.7), channel_id=1, source_target_pairs={{0,32},{1,33},{2,34},{3,35},{4,36},{5,37},{6,38},{7,39},{8,40},{9,... | collective-permute-start | bytes 110600 | tf_op jit(solution)/shard_map/ppermute | solution.py:31
  325.4 4.9 %collective-permute-start.39 = (bf16[1,24,1152]{2,1,0:T(8,128)(2,1)S(1)}, bf16[1,24,1152]{2,1,0:T(8,128)(2,1)S(1)}, u32[]{:S(2)}, u32[]{:S(2)}) collective-permute-start(bf16[1,24,1152]{2,1,0:T(8,128)(2,1)S(1)} %maximum_bitcast_fusion), channel_id=1, source_target_pairs={{0,128},{1,129},{2,130},{3,131},{4,132},{5,133},{6,134},{7,135},{8... | collective-permute-start | bytes 165896 | tf_op jit(solution)/shard_map/ppermute | solution.py:31
  330.4 8.2 %collective-permute-start.40 = (bf16[2,24,1152]{2,1,0:T(8,128)(2,1)S(1)}, bf16[2,24,1152]{2,1,0:T(8,128)(2,1)S(1)}, u32[]{:S(2)}, u32[]{:S(2)}) collective-permute-start(bf16[2,24,1152]{2,1,0:T(8,128)(2,1)S(1)} %pad_maximum_fusion.6), channel_id=1, source_target_pairs={{0,256},{1,257},{2,258},{3,259},{4,260},{5,261},{6,262},{7,263},{8... | collective-permute-start | bytes 331784 | tf_op jit(solution)/shard_map/ppermute | solution.py:31
  338.7 3.6 %collective-permute-start.41 = (bf16[72,1152]{1,0:T(8,128)(2,1)S(1)}, bf16[72,1152]{1,0:T(8,128)(2,1)S(1)}, u32[]{:S(2)}, u32[]{:S(2)}) collective-permute-start(bf16[72,1152]{1,0:T(8,128)(2,1)S(1)} %pad_maximum_fusion.5), channel_id=1, source_target_pairs={{0,8},{1,9},{2,10},{3,11},{4,12},{5,13},{6,14},{7,15},{8,0},{9,1},... | collective-permute-start | bytes 497672 | tf_op jit(solution)/shard_map/ppermute | solution.py:31
  344.6 1.2 copy-start

commit v3 on v2

--- a/solution.py
+++ b/solution.py
@@ -93,18 +93,22 @@
 
         return lax.cond(scale > 0.0, stage, unused, *blocks)
 
+    def z_shift(block, d):
+        def target(x, hi, y, c, q):
+            z = (hi * lanes + q + d) % (2 * lanes)
+            return x, z // lanes, y, c, z % lanes
+
+        return coords(block, target)
+
     def gather_z(mine):
         bit = 1
-        while bit < lanes:
+        while 2 * bit < lanes:
             mine = in_order(mine, z_flip(mine, bit), lane // bit % 2, 0)
             bit *= 2
-        return mine
-
-    def gather_rest(mine):
-        pieces = [mine] + [y_shift(mine, d) for d in range(1, SIDE)]
-        strip = jnp.zeros((lanes, window, cols), bf16)
-        for d, piece in enumerate(pieces):
-            strip = lax.dynamic_update_slice_in_dim(strip, piece, (at_y - d) % SIDE * step_y, 2)
+        theirs = jnp.concatenate([z_shift(mine[: bit // 2], bit), z_shift(mine[bit // 2 :], -bit)])
+        return in_order(mine, theirs, lane // bit % 2, 0)
+
+    def gather_x(strip):
         pieces = [strip] + [x_shift(strip, d) for d in range(1, SIDE)]
         ours = jnp.zeros((lanes, half, cols), bf16)
         for d, piece in enumerate(pieces):
@@ -136,22 +140,21 @@
     down = [(s, 0, s - 1) for s in range(1, GROUP)]
     up = [(s, 0, s + 1) for s in range(GROUP - 1)]
 
-    far = chain(unit_txt, [(0, -1, 7), (2, -1, 2)])
-    ready, _ = lax.optimization_barrier((head_weight, unit_txt))
-    mine = lax.dynamic_slice(
-        ready, (core * half + at_x * step, at_y * step_y), (window, window_y)
-    )[None]
-
-    def gather(mine):
-        mine, moved, near = one_step(
-            lambda m: (gather_z(m), chain(unit_txt, [(1, 0, 6)]), chain(unit_txt, down)), mine
-        )
-        far_1 = chain(moved, [(6, -1, 6)])
-        whole = one_step(gather_rest, mine)
-        return *lax.optimization_barrier((whole, far_1)), near
-
-    full_weight, far_1, near = one_step(gather, mine)
-    full_weight, far = lax.optimization_barrier((full_weight, far))
+    ready, unit_txt = lax.optimization_barrier((head_weight, unit_txt))
+    mine = lax.dynamic_slice_in_dim(ready, core * half + at_x * step, window, 0)[None]
+    mine, moved, near_1 = one_step(
+        lambda m: (gather_z(m), chain(unit_txt, [(1, 0, 6)]), chain(unit_txt, down)), mine
+    )
+    unit_far, mine = lax.optimization_barrier((unit_txt, mine))
+    far = chain(unit_far, [(0, -1, 7), (2, -1, 2)])
+    far_1 = chain(moved, [(6, -1, 6)])
+
+    def gather_and_chain(mine, near_1):
+        near_2 = chain(near_1, down)
+        return gather_x(mine), near_2, chain(near_2, down)
+
+    full_weight, near_2, near_3 = one_step(gather_and_chain, mine, near_1)
+    full_weight, far, far_1 = lax.optimization_barrier((full_weight, far, far_1))
 
     projected = jnp.dot(image_features, full_weight, preferred_element_type=f32)
     img_norm = jnp.sqrt(jnp.sum(projected * projected, axis=1, keepdims=True) + 1e-06)
@@ -165,8 +168,6 @@
     code = jnp.pad(code[None, :], ((0, 7), (0, 0)))
     parcel = jnp.concatenate([unit_img, code], axis=0)
 
-    back = chain(parcel, [(7, 1, 0), (5, 1, 5)])
-
     offsets = lax.iota(jnp.int32, rows)
 
     def pair_weight(logits, match):
@@ -180,28 +181,19 @@
         weights = pair_weight(scale * logits + bias, met[:, None] == offsets[None, :])
         return scale * jnp.dot(weights, text, preferred_element_type=f32)
 
-    def meet_texts(far, near, far_1):
-        far_2 = chain(far, [(2, 0, 7)])
-        text_1 = jnp.where(last, far, near)
-        text_2 = chain(text_1, down)
-        text_3 = chain(text_2, down)
-        far_3 = chain(far_1, [(6, 0, 7)])
-        text_2 = jnp.where(last, far_2, text_2)
-        text_3 = jnp.where(last, far_3, jnp.where(slot == GROUP - 2, far_1, text_3))
-        texts = [
-            (unit_txt, 0),
-            (text_1, 1),
-            (text_2, jnp.where(last, 3, 2)),
-            (text_3, jnp.where(last, 2, 3)),
-        ]
-        img_grad = 0.0
-        for text, k in texts[:-1]:
-            img_grad = img_grad + met_grad(text, k)
+    def meet_texts(far, far_1):
+        swapped = chain(jnp.where(last, far, far_1), [(7, 0, 6), (6, 0, 7)])
+        passed = chain(far, [(2, 0, 7), (7, 0, 5)])
         back_0 = chain(parcel, [(6, 0, 1)])
-        return img_grad, text_3, back_0, chain(parcel, up)
-
-    def head_terms(img_grad, text):
-        img_grad = img_grad + met_grad(text, jnp.where(last, 2, 3))
+        beside_1 = chain(parcel, up)
+        img_grad = met_grad(unit_txt, 0) + met_grad(jnp.where(last, far, near_1), 1)
+        return img_grad, swapped, passed, back_0, beside_1
+
+    def head_terms(img_grad, swapped, passed):
+        text_3 = jnp.where(slot >= GROUP - 3, passed, near_3)
+        text_3 = jnp.where(slot == GROUP - 2, far_1, text_3)
+        img_grad = img_grad + met_grad(jnp.where(slot >= GROUP - 2, swapped, near_2), 2)
+        img_grad = img_grad + met_grad(text_3, 3)
         proj_grad = (
             (img_grad - unit_f * jnp.sum(unit_f * img_grad, axis=1, keepdims=True)) / img_norm
         ).astype(bf16)
@@ -225,21 +217,29 @@
         total = total.reshape(window, window_y)
         return (total + hi_flip(total)).astype(bf16)
 
-    img_grad, text, back_0, beside = one_step(meet_texts, far, near, far_1)
+    img_grad, swapped, passed, back_0, beside_1 = one_step(meet_texts, far, far_1)
+    parcel_far, img_grad = lax.optimization_barrier((parcel, img_grad))
+    back = chain(parcel_far, [(7, 1, 0), (5, 1, 5)])
     back_1 = chain(back_0, [(1, 1, 1)])
-    total = one_step(lambda *blocks: sum_xy(head_terms(*blocks)), img_grad, text)
+
+    total = one_step(lambda *blocks: sum_xy(head_terms(*blocks)), img_grad, swapped, passed)
     total, back, back_1 = lax.optimization_barrier((total, back, back_1))
-    back_2 = chain(back, [(5, 0, 0)])
-    image_1 = jnp.where(first, back, beside)
-    image_2 = chain(image_1, up)
-    total_z = one_step(sum_z, total)
-    total_z, back_2, image_2, parcel, image_1 = lax.optimization_barrier(
-        (total_z, back_2, image_2, parcel, image_1)
-    )
-    image_3 = chain(image_2, up)
-    back_3 = chain(back_1, [(1, 0, 0)])
-    image_2 = jnp.where(first, back_2, image_2)
-    image_3 = jnp.where(first, back_3, jnp.where(slot == 1, back_1, image_3))
+
+    def sum_z_and_chain(total, back, back_1):
+        beside_2 = chain(beside_1, up)
+        swapped = chain(jnp.where(first, back, back_1), [(0, 0, 1), (1, 0, 0)])
+        passed = chain(back, [(5, 0, 0), (0, 0, 2)])
+        return sum_z(total), swapped, passed, beside_2, chain(beside_2, up)
+
+    total_z, swapped, passed, beside_2, beside_3 = one_step(sum_z_and_chain, total, back, back_1)
+    parcel, total_z = lax.optimization_barrier((parcel, total_z))
+    image_3 = jnp.where(slot <= 2, passed, beside_3)
+    images = [
+        parcel,
+        jnp.where(first, back, beside_1),
+        jnp.where(slot <= 1, swapped, beside_2),
+        jnp.where(slot == 1, back_1, image_3),
+    ]
 
     strips = total_z[None]
     for bit in (1, 2):
@@ -254,15 +254,8 @@
     )
     head_grad = in_order(ours, core_swap(ours), core, 0).astype(f32)
 
-    images = [
-        (parcel, 0),
-        (image_1, 1),
-        (image_2, jnp.where(first, 3, 2)),
-        (image_3, jnp.where(first, 2, 3)),
-    ]
-
     txt_grad = 0.0
-    for image, k in images:
+    for k, image in enumerate(images):
         unit, marks = image[:rows], image[rows].astype(f32).astype(jnp.int32)
         met = marks[rows : 2 * rows] * 128 + marks[2 * rows : 3 * rows]
         met = jnp.where(marks[:rows] == k, met, -1)

time: 350 us -> 334 us (0.954)
  waiting for transfers between devices: 134 us -> 102 us
  starting transfers between devices: 145 us -> 157 us
  other arithmetic: 23.9 us -> 27.5 us
    ppermute x26 -> x24, waiting for transfers between devices: 120 us -> 76.8 us  [by_coords(): return lax.ppermute(block, AXES, route)]
    ppermute x26 -> x24, starting transfers between devices: 89.1 us -> 107 us  [by_coords(): return lax.ppermute(block, AXES, route)]
    ppermute x16, waiting for transfers between devices: 14.1 us -> 25.2 us  [along_chain(): return lax.ppermute(block, AXES, route)]
    ppermute x16, starting transfers between devices: 55.7 us -> 50.5 us  [along_chain(): return lax.ppermute(block, AXES, route)]
    select_n x5 -> x7, other arithmetic: 6.27 us -> 7.05 us  [the longest x1 1.98 us: on_device(): jnp.where(slot == 1, back_1, image_3)]
  transfers between devices with their start and end apart: 42 -> 40, of which waited for: 24 -> 23; matrix products, arithmetic and copies ran while one was open for 14% -> 13% of each run, Pallas kernels for 0% -> 0%
where the time goes in v3:
time: 334 us; the launch traced here: 331 us
  starting transfers between devices  157 us (47%)
  waiting for transfers between devices  102 us (31%)
  matrix products  30.9 us (9%)
  other arithmetic  27.5 us (8%)
  local copies, waits for them, and re-layouts  9.51 us (3%)
    ppermute x24, starting transfers between devices, by_coords(): return lax.ppermute(block, AXES, route)  107 us
    ppermute x24, waiting for transfers between devices, by_coords(): return lax.ppermute(block, AXES, route)  76.8 us
    ppermute x16, starting transfers between devices, along_chain(): return lax.ppermute(block, AXES, route)  50.5 us
    ppermute x16, waiting for transfers between devices, along_chain(): return lax.ppermute(block, AXES, route)  25.2 us
    dot_general x4, matrix products, met_grad(): logits = jnp.einsum('ie,je->ij', unit_img, text, preferred_element_type=f32)  9.43 us
    dot_general x4, matrix products, met_grad(): return scale * jnp.dot(weights, text, preferred_element_type=f32)  7.45 us
  transfers between devices with their start and end apart: 40, of which 23 were waited for; matrix products, arithmetic and copies ran while one was open for 13% of the time, Pallas kernels for 0%

profile of v3, /device:TPU:1, one launch (start us, length us, event | category | flops | bytes accessed | tf_op | source)
XLA Modules:
  0.0 331.5 jit_solution(15244473145462884560)
XLA Ops:
  4.3 48.3 %conditional.5 = (bf16[8,24,1152]{2,1,0:T(8,128)(2,1)S(1)}, bf16[384,1152]{1,0:T(8,128)(2,1)}, bf16[384,1152]{1,0:T(8,128)(2,1)}) conditional(s32[]{:T(128)} %convert_element_type.171, () %tuple.59, (s32[]{:T(128)}, s32[]{:T(128)}, s32[]{:T(128)}, bf16[144,1152]{1,0:T(8,128)(2,1)}, bf16[384,1152]{1,0:T(8,128)(2,1)S(1)}) %tuple.60), branch_computations={%region_1.2_spmd, %region_2.3_spmd} | conditional | flops 829500 | bytes 11834224 | solution.py:94
  5.1 4.4 %collective-permute-start = (bf16[1,24,1152]{2,1,0:T(8,128)(2,1)S(1)}, bf16[1,24,1152]{2,1,0:T(8,128)(2,1)S(1)}, u32[]{:S(2)}, u32[]{:S(2)}) collective-permute-start(bf16[1,24,1152]{2,1,0:T(8,128)(2,1)S(1)} %dynamic-slice_bitcast_fusion), channel_id=1, source_target_pairs={{0,1},{1,0},{2,3},{3,2},{4,5},{5,4},{6,7},{7,6},{8,9},{9,8},{10,11... | collective-permute-start | bytes 165896 | tf_op jit(solution)/shard_map/cond/branch_1_fun/ppermute | solution.py:31
  11.9 4.9 %collective-permute-start.1 = (bf16[2,24,1152]{2,1,0:T(8,128)(2,1)S(1)}, bf16[2,24,1152]{2,1,0:T(8,128)(2,1)S(1)}, u32[]{:S(2)}, u32[]{:S(2)}) collective-permute-start(bf16[2,24,1152]{2,1,0:T(8,128)(2,1)S(1)} %pad_maximum_fusion.2), channel_id=1, source_target_pairs={{0,2},{1,3},{2,0},{3,1},{4,6},{5,7},{6,4},{7,5},{8,10},{9,11},{10,... | collective-permute-start | bytes 331784 | tf_op jit(solution)/shard_map/cond/branch_1_fun/ppermute | solution.py:31
  16.8 2.1 collective-permute-done.1
  19.0 8.8 %collective-permute-start.2 = (bf16[2,24,1152]{2,1,0:T(8,128)(2,1)S(1)}, bf16[2,24,1152]{2,1,0:T(8,128)(2,1)S(1)}, u32[]{:S(2)}, u32[]{:S(2)}) collective-permute-start(bf16[2,24,1152]{2,1,0:T(8,128)(2,1)S(1)} %get-tuple-element.236), channel_id=1, source_target_pairs={{0,4},{1,5},{2,6},{3,7},{4,64},{5,65},{6,66},{7,67},{8,12},{9,13},... | collective-permute-start | bytes 331784 | tf_op jit(solution)/shard_map/cond/branch_1_fun/ppermute | solution.py:31
  27.8 10.0 %collective-permute-start.4 = (bf16[384,1152]{1,0:T(8,128)(2,1)S(1)}, bf16[384,1152]{1,0:T(8,128)(2,1)}, u32[]{:S(2)}, u32[]{:S(2)}) collective-permute-start(bf16[384,1152]{1,0:T(8,128)(2,1)S(1)} %get-tuple-element.123), channel_id=1, source_target_pairs={{8,48},{9,49},{10,50},{11,51},{12,52},{13,53},{14,54},{15,55},{72,... | collective-permute-start | bytes 2654216 | tf_op jit(solution)/shard_map/cond/branch_1_fun/ppermute | solution.py:21
  39.7 4.5 %collective-permute-start.3 = (bf16[2,24,1152]{2,1,0:T(8,128)(2,1)S(1)}, bf16[2,24,1152]{2,1,0:T(8,128)(2,1)S(1)}, u32[]{:S(2)}, u32[]{:S(2)}) collective-permute-start(bf16[2,24,1152]{2,1,0:T(8,128)(2,1)S(1)} %get-tuple-element.235), channel_id=1, source_target_pairs={{0,68},{1,69},{2,70},{3,71},{4,0},{5,1},{6,2},{7,3},{8,76},{9,77},... | collective-permute-start | bytes 331784 | tf_op jit(solution)/shard_map/cond/branch_1_fun/ppermute | solution.py:31
  44.2 8.2 %collective-permute-done.3 = bf16[2,24,1152]{2,1,0:T(8,128)(2,1)S(1)} collective-permute-done((bf16[2,24,1152]{2,1,0:T(8,128)(2,1)S(1)}, bf16[2,24,1152]{2,1,0:T(8,128)(2,1)S(1)}, u32[]{:S(2)}, u32[]{:S(2)}) %collective-permute-start.3) | collective-permute-done | bytes 110624 | tf_op jit(solution)/shard_map/cond/branch_1_fun/ppermute | solution.py:31
  55.6 66.2 %conditional.6 = (bf16[1152,1152]{1,0:T(8,128)(2,1)}, bf16[384,1152]{1,0:T(8,128)(2,1)}, bf16[384,1152]{1,0:T(8,128)(2,1)}) conditional(s32[]{:T(128)} %convert_element_type.171, () %tuple.57, (s32[]{:T(128)}, s32[]{:T(128)}, bf16[8,24,1152]{2,1,0:T(8,128)(2,1)S(1)}, bf16[384,1152]{1,0:T(8,128)(2,1)}) %tuple.62), branch_computations={%region_3.4_spmd, %region_4.5_spmd} | conditional | flops 6635584 | bytes 33178548 | solution.py:94
  55.6 3.1 collective-permute-start.6
  58.7 4.4 %collective-permute-start.7 = (bf16[8,24,1152]{2,1,0:T(8,128)(2,1)S(1)}, bf16[8,24,1152]{2,1,0:T(8,128)(2,1)}, u32[]{:S(2)}, u32[]{:S(2)}) collective-permute-start(bf16[8,24,1152]{2,1,0:T(8,128)(2,1)S(1)} %get-tuple-element.125), channel_id=1, source_target_pairs={{0,256},{1,257},{2,258},{3,259},{4,260},{5,261},{6,262},{7,263},{8... | collective-permute-start | bytes 1327112 | tf_op jit(solution)/shard_map/cond/branch_1_fun/ppermute | solution.py:31
  63.1 3.1 collective-permute-start.8
  67.5 4.2 %collective-permute-done.7 = bf16[8,24,1152]{2,1,0:T(8,128)(2,1)} collective-permute-done((bf16[8,24,1152]{2,1,0:T(8,128)(2,1)S(1)}, bf16[8,24,1152]{2,1,0:T(8,128)(2,1)}, u32[]{:S(2)}, u32[]{:S(2)}) %collective-permute-start.7) | collective-permute-done | bytes 442400 | tf_op jit(solution)/shard_map/cond/branch_1_fun/ppermute | solution.py:31
  74.2 18.2 %collective-permute-start.9 = (bf16[8,72,1152]{2,1,0:T(8,128)(2,1)S(1)}, bf16[8,72,1152]{2,1,0:T(8,128)(2,1)}, u32[]{:S(2)}, u32[]{:S(2)}) collective-permute-start(bf16[8,72,1152]{2,1,0:T(8,128)(2,1)S(1)} %constant_dynamic-update-slice_fusion.2), channel_id=1, source_target_pairs={{0,8},{1,9},{2,10},{3,11},{4,12},{5,13},{6,14},{7,15},{8,0},{9,1},... | collective-permute-start | bytes 3981320 | tf_op jit(solution)/shard_map/cond/branch_1_fun/ppermute | solution.py:31
  92.4 1.9 collective-permute-start.10
  94.3 12.7 %collective-permute-done.10 = bf16[384,1152]{1,0:T(8,128)(2,1)} collective-permute-done((bf16[384,1152]{1,0:T(8,128)(2,1)}, bf16[384,1152]{1,0:T(8,128)(2,1)}, u32[]{:S(2)}, u32[]{:S(2)}) %collective-permute-start.10) | collective-permute-done | bytes 884768 | tf_op jit(solution)/shard_map/cond/branch_1_fun/ppermute | solution.py:21
  107.1 1.9 collective-permute-start.11
  112.3 9.5 %collective-permute-done.11 = bf16[384,1152]{1,0:T(8,128)(2,1)} collective-permute-done((bf16[384,1152]{1,0:T(8,128)(2,1)}, bf16[384,1152]{1,0:T(8,128)(2,1)}, u32[]{:S(2)}, u32[]{:S(2)}) %collective-permute-start.11) | collective-permute-done | bytes 884768 | tf_op jit(solution)/shard_map/cond/branch_1_fun/ppermute | solution.py:21
  122.5 3.9 %multiply_reduce_fusion.2 = (f32[384]{0:T(512)S(1)}, f32[1152,384]{0,1:T(8,128)S(1)}) fusion(bf16[384,1152]{1,0:T(8,128)(2,1)} %param.16, bf16[1152,1152]{1,0:T(8,128)(2,1)} %get-tuple-element.207), kind=kOutput, calls=%fused_computation.106 | convolution fusion | flops 1020100224 | bytes 5309952 | tf_op jit(solution)/shard_map/dot_general | solution.py:159
  128.9 16.1 %conditional.7 = (f32[384,1152]{1,0:T(8,128)S(1)}, bf16[384,1152]{1,0:T(8,128)(2,1)}, bf16[384,1152]{1,0:T(8,128)(2,1)}, bf16[392,1152]{1,0:T(8,128)(2,1)}, bf16[392,1152]{1,0:T(8,128)(2,1)}) conditional(s32[]{:T(128)} %convert_element_type.171, () %tuple.66, (f32[]{:T(128)}, s32[384]{0:T(512)S(1)}, s32[384]{0:T(512)S(1)}, s32[384]{0:T(512)S(1)}, ...), branch_computations={%region_6.7_spmd, %region_7.8_spmd} | conditional | flops 1364854272 | bytes 35263748 | solution.py:94
  130.1 2.0 collective-permute-start.23
  139.4 2.6 fusion.13
  146.6 12.8 %collective-permute-start.34 = (bf16[392,1152]{1,0:T(8,128)(2,1)}, bf16[392,1152]{1,0:T(8,128)(2,1)}, u32[]{:S(2)}, u32[]{:S(2)}) collective-permute-start(bf16[392,1152]{1,0:T(8,128)(2,1)} %get-tuple-element.217), channel_id=1, source_target_pairs={{8,72},{9,73},{10,74},{11,75},{12,76},{13,77},{14,78},{15,79},{72,... | collective-permute-start | bytes 2709512 | tf_op jit(solution)/shard_map/ppermute | solution.py:21
  160.2 81.7 %conditional.8 = (f32[8,24,384]{2,1,0:T(8,128)S(1)}) conditional(s32[]{:T(128)} %convert_element_type.171, () %tuple.65, (f32[]{:T(128)}, s32[384]{0:T(512)S(1)}, s32[384]{0:T(512)S(1)}, s32[384]{0:T(512)S(1)}, s32[384]{0:T(512)S(1)}, /*index=5*/s32[]{:T(128)}, bf16[384,1152]{1,0:T(8,128)(2,1)}, bf16[384,1152]{1,0:T(8,128)(2,1)}, ...), branch_computations={%region_8.9_spmd, %region_9.11_spmd} | conditional | flops 2392696320 | bytes 84084168 | solution.py:94
  161.1 3.3 %fusion.33 = bf16[384,384]{1,0:T(8,128)(2,1)} fusion(bf16[384,1152]{1,0:T(8,128)(2,1)S(1)} %get-tuple-element.149, bf16[384,1152]{1,0:T(8,128)(2,1)} %get-tuple-element.147, bf16[384,1152]{1,0:T(8,128)(2,1)} %get-tuple-element.148, pred[]{:T(512)S(6)} %ge.4, f32[]{:T(128)} %get-tuple-element.150, f32[]{:T(128)} %get-tuple-element.142, ...), kind=kOutput, calls=%fused_computation.70 | convolution fusion | flops 341803008 | bytes 2952201 | tf_op jit(solution)/shard_map/cond/branch_1_fun/ie,je->ij/dot_general | solution.py:179
  165.7 2.2 fusion.32
  167.9 2.5 fusion.15
  170.4 2.5 multiply_reduce_fusion
  176.4 1.9 collective-permute-start.24
  178.4 3.1 collective-permute-done.24
  181.5 2.0 convert_add_fusion
  184.6 2.9 collective-permute-start.27
  187.5 4.9 %collective-permute-start.26 = (bf16[8,24,1152]{2,1,0:T(8,128)(2,1)}, bf16[8,24,1152]{2,1,0:T(8,128)(2,1)}, u32[]{:S(2)}, u32[]{:S(2)}) collective-permute-start(bf16[8,24,1152]{2,1,0:T(8,128)(2,1)} %get-tuple-element.245), channel_id=1, source_target_pairs={{0,256},{1,257},{2,258},{3,259},{4,260},{5,261},{6,262},{7,263},{8... | collective-permute-start | bytes 1327112 | tf_op jit(solution)/shard_map/cond/branch_1_fun/ppermute | solution.py:31
  192.4 1.9 collective-permute-start.25
  194.4 5.0 %collective-permute-done.27 = bf16[8,24,1152]{2,1,0:T(8,128)(2,1)} collective-permute-done((bf16[8,24,1152]{2,1,0:T(8,128)(2,1)}, bf16[8,24,1152]{2,1,0:T(8,128)(2,1)}, u32[]{:S(2)}, u32[]{:S(2)}) %collective-permute-start.27) | collective-permute-done | bytes 442400 | tf_op jit(solution)/shard_map/cond/branch_1_fun/ppermute | solution.py:31
  199.4 8.1 %collective-permute-done.26 = bf16[8,24,1152]{2,1,0:T(8,128)(2,1)} collective-permute-done((bf16[8,24,1152]{2,1,0:T(8,128)(2,1)}, bf16[8,24,1152]{2,1,0:T(8,128)(2,1)}, u32[]{:S(2)}, u32[]{:S(2)}) %collective-permute-start.26) | collective-permute-done | bytes 442400 | tf_op jit(solution)/shard_map/cond/branch_1_fun/ppermute | solution.py:31
  207.5 9.0 %collective-permute-done.25 = bf16[8,24,1152]{2,1,0:T(8,128)(2,1)} collective-permute-done((bf16[8,24,1152]{2,1,0:T(8,128)(2,1)}, bf16[8,24,1152]{2,1,0:T(8,128)(2,1)}, u32[]{:S(2)}, u32[]{:S(2)}) %collective-permute-start.25) | collective-permute-done | bytes 442400 | tf_op jit(solution)/shard_map/cond/branch_1_fun/ppermute | solution.py:31
  216.5 2.4 convert_add_fusion.1
  220.1 8.3 %collective-permute-start.30 = (bf16[8,24,384]{2,1,0:T(8,128)(2,1)S(1)}, bf16[8,24,384]{2,1,0:T(8,128)(2,1)S(1)}, u32[]{:S(2)}, u32[]{:S(2)}) collective-permute-start(bf16[8,24,384]{2,1,0:T(8,128)(2,1)S(1)} %get-tuple-element.247), channel_id=1, source_target_pairs={{0,48},{1,49},{2,50},{3,51},{4,52},{5,53},{6,54},{7,55},{8,56},{9,... | collective-permute-start | bytes 442376 | tf_op jit(solution)/shard_map/cond/branch_1_fun/ppermute | solution.py:31
  228.5 2.9 collective-permute-start.29
  231.4 2.8 collective-permute-start.28
  234.2 2.3 collective-permute-done.29
  236.5 4.2 %collective-permute-done.28 = bf16[8,24,384]{2,1,0:T(8,128)(2,1)S(1)} collective-permute-done((bf16[8,24,384]{2,1,0:T(8,128)(2,1)S(1)}, bf16[8,24,384]{2,1,0:T(8,128)(2,1)S(1)}, u32[]{:S(2)}, u32[]{:S(2)}) %collective-permute-start.28) | collective-permute-done | bytes 147488 | tf_op jit(solution)/shard_map/cond/branch_1_fun/ppermute | solution.py:31
  241.9 44.7 %conditional.9 = (bf16[24,384]{1,0:T(8,128)(2,1)S(1)}, bf16[392,1152]{1,0:T(8,128)(2,1)}, bf16[392,1152]{1,0:T(8,128)(2,1)}, bf16[392,1152]{1,0:T(8,128)(2,1)}, bf16[392,1152]{1,0:T(8,128)(2,1)}) conditional(s32[]{:T(128)} %convert_element_type.171, () %tuple.64, (f32[8,24,384]{2,1,0:T(8,128)S(1)}, s32[]{:T(128)}, pred[]{:T(512)}, ...), branch_computations={%region_11.12_spmd, %region_12.13_spmd} | conditional | flops 599112 | bytes 21179556 | solution.py:94
  241.9 2.0 collective-permute-start.18
  244.0 1.9 collective-permute-start.12
  248.9 3.6 %collective-permute-start.16 = (bf16[392,1152]{1,0:T(8,128)(2,1)S(1)}, bf16[392,1152]{1,0:T(8,128)(2,1)}, u32[]{:S(2)}, u32[]{:S(2)}) collective-permute-start(bf16[392,1152]{1,0:T(8,128)(2,1)S(1)} %broadcast_select_fusion.15), channel_id=1, source_target_pairs={{0,8},{8,0},{1,9},{9,1},{2,10},{10,2},{3,11},{11,3},{4,12},{12,4},... | collective-permute-start | bytes 2709512 | tf_op jit(solution)/shard_map/cond/branch_1_fun/ppermute | solution.py:21
  252.5 3.5 %collective-permute-done.12 = bf16[4,24,384]{2,1,0:T(8,128)(2,1)S(1)} collective-permute-done((bf16[4,24,384]{2,1,0:T(8,128)(2,1)S(1)}, bf16[4,24,384]{2,1,0:T(8,128)(2,1)S(1)}, u32[]{:S(2)}, u32[]{:S(2)}) %collective-permute-start.12) | collective-permute-done | bytes 73760 | tf_op jit(solution)/shard_map/cond/branch_1_fun/ppermute | solution.py:31
  256.0 2.6 collective-permute-done.18
  258.6 4.4 %collective-permute-start.19 = (bf16[392,1152]{1,0:T(8,128)(2,1)}, bf16[392,1152]{1,0:T(8,128)(2,1)}, u32[]{:S(2)}, u32[]{:S(2)}) collective-permute-start(bf16[392,1152]{1,0:T(8,128)(2,1)} %collective-permute-done.18), channel_id=1, source_target_pairs={{0,8},{8,16},{16,24},{24,32},{32,40},{40,48},{48,56},{1,9},{9,17},... | collective-permute-start | bytes 2709512 | tf_op jit(solution)/shard_map/cond/branch_1_fun/ppermute | solution.py:21
  263.0 1.9 collective-permute-start.13
  264.9 3.7 %collective-permute-done.13 = bf16[2,24,384]{2,1,0:T(8,128)(2,1)S(1)} collective-permute-done((bf16[2,24,384]{2,1,0:T(8,128)(2,1)S(1)}, bf16[2,24,384]{2,1,0:T(8,128)(2,1)S(1)}, u32[]{:S(2)}, u32[]{:S(2)}) %collective-permute-start.13) | collective-permute-done | bytes 36896 | tf_op jit(solution)/shard_map/cond/branch_1_fun/ppermute | solution.py:31
  268.6 1.9 collective-permute-start.14
  270.6 2.6 collective-permute-done.14
  273.1 1.9 collective-permute-start.15
  275.1 11.5 %collective-permute-done.15 = f32[24,384]{1,0:T(8,128)S(1)} collective-permute-done((f32[24,384]{1,0:T(8,128)S(1)}, f32[24,384]{1,0:T(8,128)S(1)}, u32[]{:S(2)}, u32[]{:S(2)}) %collective-permute-start.15) | collective-permute-done | bytes 36896 | tf_op jit(solution)/shard_map/cond/branch_1_fun/ppermute | solution.py:31
  287.3 2.0 fusion.68
  291.1 2.0 select_select_fusion.1
  296.1 1.9 collective-permute-start.35
  300.7 1.9 collective-permute-start.36
  302.6 4.3 %collective-permute-done.36 = bf16[2,24,384]{2,1,0:T(8,128)(2,1)S(1)} collective-permute-done((bf16[2,24,384]{2,1,0:T(8,128)(2,1)S(1)}, bf16[2,24,384]{2,1,0:T(8,128)(2,1)S(1)}, u32[]{:S(2)}, u32[]{:S(2)}) %collective-permute-start.36) | collective-permute-done | bytes 36896 | tf_op jit(solution)/shard_map/ppermute | solution.py:31
  306.9 4.5 %collective-permute-start.37 = (bf16[1,24,1152]{2,1,0:T(8,128)(2,1)S(1)}, bf16[1,24,1152]{2,1,0:T(8,128)(2,1)S(1)}, u32[]{:S(2)}, u32[]{:S(2)}) collective-permute-start(bf16[1,24,1152]{2,1,0:T(8,128)(2,1)S(1)} %maximum_bitcast_fusion), channel_id=1, source_target_pairs={{0,128},{1,129},{2,130},{3,131},{4,132},{5,133},{6,134},{7,135},{8... | collective-permute-start | bytes 165896 | tf_op jit(solution)/shard_map/ppermute | solution.py:31
  313.0 5.9 %collective-permute-start.38 = (bf16[2,24,1152]{2,1,0:T(8,128)(2,1)S(1)}, bf16[2,24,1152]{2,1,0:T(8,128)(2,1)S(1)}, u32[]{:S(2)}, u32[]{:S(2)}) collective-permute-start(bf16[2,24,1152]{2,1,0:T(8,128)(2,1)S(1)} %pad_maximum_fusion.6), channel_id=1, source_target_pairs={{0,256},{1,257},{2,258},{3,259},{4,260},{5,261},{6,262},{7,263},{8... | collective-permute-start | bytes 331784 | tf_op jit(solution)/shard_map/ppermute | solution.py:31
  321.2 8.0 %collective-permute-start.39 = (bf16[72,1152]{1,0:T(8,128)(2,1)S(1)}, bf16[72,1152]{1,0:T(8,128)(2,1)S(1)}, u32[]{:S(2)}, u32[]{:S(2)}) collective-permute-start(bf16[72,1152]{1,0:T(8,128)(2,1)S(1)} %pad_maximum_fusion.5), channel_id=1, source_target_pairs={{0,8},{1,9},{2,10},{3,11},{4,12},{5,13},{6,14},{7,15},{8,0},{9,1},... | collective-permute-start | bytes 497672 | tf_op jit(solution)/shard_map/ppermute | solution.py:31
  (146 shorter events, 60.3 us)
Async XLA Ops:
  2.1 0.7 copy-start.7
  4.3 50.7 %copy-start.11 = (s32[384]{0:T(512)S(1)}, s32[384]{0:T(512)}, u32[]{:S(2)}) copy-start(s32[384]{0:T(512)} %param.19) | copy-start | bytes 4612
  5.1 5.9 %collective-permute-start = (bf16[1,24,1152]{2,1,0:T(8,128)(2,1)S(1)}, bf16[1,24,1152]{2,1,0:T(8,128)(2,1)S(1)}, u32[]{:S(2)}, u32[]{:S(2)}) collective-permute-start(bf16[1,24,1152]{2,1,0:T(8,128)(2,1)S(1)} %dynamic-slice_bitcast_fusion), channel_id=1, source_target_pairs={{0,1},{1,0},{2,3},{3,2},{4,5},{5,4},{6,7},{7,6},{8,9},{9,8},{10,11... | collective-permute-start | bytes 165896 | tf_op jit(solution)/shard_map/cond/branch_1_fun/ppermute | solution.py:31
  11.9 7.0 %collective-permute-start.1 = (bf16[2,24,1152]{2,1,0:T(8,128)(2,1)S(1)}, bf16[2,24,1152]{2,1,0:T(8,128)(2,1)S(1)}, u32[]{:S(2)}, u32[]{:S(2)}) collective-permute-start(bf16[2,24,1152]{2,1,0:T(8,128)(2,1)S(1)} %pad_maximum_fusion.2), channel_id=1, source_target_pairs={{0,2},{1,3},{2,0},{3,1},{4,6},{5,7},{6,4},{7,5},{8,10},{9,11},{10,... | collective-permute-start | bytes 331784 | tf_op jit(solution)/shard_map/cond/branch_1_fun/ppermute | solution.py:31
  19.0 25.2 %collective-permute-start.2 = (bf16[2,24,1152]{2,1,0:T(8,128)(2,1)S(1)}, bf16[2,24,1152]{2,1,0:T(8,128)(2,1)S(1)}, u32[]{:S(2)}, u32[]{:S(2)}) collective-permute-start(bf16[2,24,1152]{2,1,0:T(8,128)(2,1)S(1)} %get-tuple-element.236), channel_id=1, source_target_pairs={{0,4},{1,5},{2,6},{3,7},{4,64},{5,65},{6,66},{7,67},{8,12},{9,13},... | collective-permute-start | bytes 331784 | tf_op jit(solution)/shard_map/cond/branch_1_fun/ppermute | solution.py:31
  27.8 24.8 %collective-permute-start.4 = (bf16[384,1152]{1,0:T(8,128)(2,1)S(1)}, bf16[384,1152]{1,0:T(8,128)(2,1)}, u32[]{:S(2)}, u32[]{:S(2)}) collective-permute-start(bf16[384,1152]{1,0:T(8,128)(2,1)S(1)} %get-tuple-element.123), channel_id=1, source_target_pairs={{8,48},{9,49},{10,50},{11,51},{12,52},{13,53},{14,54},{15,55},{72,... | collective-permute-start | bytes 2654216 | tf_op jit(solution)/shard_map/cond/branch_1_fun/ppermute | solution.py:21
  37.8 14.8 %collective-permute-start.5 = (bf16[384,1152]{1,0:T(8,128)(2,1)S(1)}, bf16[384,1152]{1,0:T(8,128)(2,1)}, u32[]{:S(2)}, u32[]{:S(2)}) collective-permute-start(bf16[384,1152]{1,0:T(8,128)(2,1)S(1)} %get-tuple-element.123), channel_id=1, source_target_pairs={{8,0},{16,8},{24,16},{32,24},{40,32},{48,40},{56,48},{9,1},{17,9},... | collective-permute-start | bytes 2654216 | tf_op jit(solution)/shard_map/cond/branch_1_fun/ppermute | solution.py:21
  39.7 12.7 %collective-permute-start.3 = (bf16[2,24,1152]{2,1,0:T(8,128)(2,1)S(1)}, bf16[2,24,1152]{2,1,0:T(8,128)(2,1)S(1)}, u32[]{:S(2)}, u32[]{:S(2)}) collective-permute-start(bf16[2,24,1152]{2,1,0:T(8,128)(2,1)S(1)} %get-tuple-element.235), channel_id=1, source_target_pairs={{0,68},{1,69},{2,70},{3,71},{4,0},{5,1},{6,2},{7,3},{8,76},{9,77},... | collective-permute-start | bytes 331784 | tf_op jit(solution)/shard_map/cond/branch_1_fun/ppermute | solution.py:31
  52.6 69.8 %collective-permute-start.31 = (bf16[384,1152]{1,0:T(8,128)(2,1)S(1)}, bf16[384,1152]{1,0:T(8,128)(2,1)}, u32[]{:S(2)}, u32[]{:S(2)}) collective-permute-start(bf16[384,1152]{1,0:T(8,128)(2,1)S(1)} %fusion.98), channel_id=1, source_target_pairs={{0,504},{16,464},{1,505},{17,465},{2,506},{18,466},{3,507},{19,467... | collective-permute-start | bytes 2654216 | tf_op jit(solution)/shard_map/ppermute | solution.py:21
  54.2 68.2 %collective-permute-start.32 = (bf16[384,1152]{1,0:T(8,128)(2,1)}, bf16[384,1152]{1,0:T(8,128)(2,1)S(1)}, u32[]{:S(2)}, u32[]{:S(2)}) collective-permute-start(bf16[384,1152]{1,0:T(8,128)(2,1)} %get-tuple-element.206), channel_id=1, source_target_pairs={{48,496},{49,497},{50,498},{51,499},{52,500},{53,501},{54,502},{55... | collective-permute-start | bytes 2654216 | tf_op jit(solution)/shard_map/ppermute | solution.py:21
  55.6 10.8 %collective-permute-start.6 = (bf16[8,24,1152]{2,1,0:T(8,128)(2,1)S(1)}, bf16[8,24,1152]{2,1,0:T(8,128)(2,1)}, u32[]{:S(2)}, u32[]{:S(2)}) collective-permute-start(bf16[8,24,1152]{2,1,0:T(8,128)(2,1)S(1)} %get-tuple-element.125), channel_id=1, source_target_pairs={{0,128},{1,129},{2,130},{3,131},{4,132},{5,133},{6,134},{7,135},{8... | collective-permute-start | bytes 1327112 | tf_op jit(solution)/shard_map/cond/branch_1_fun/ppermute | solution.py:31
  58.7 13.0 %collective-permute-start.7 = (bf16[8,24,1152]{2,1,0:T(8,128)(2,1)S(1)}, bf16[8,24,1152]{2,1,0:T(8,128)(2,1)}, u32[]{:S(2)}, u32[]{:S(2)}) collective-permute-start(bf16[8,24,1152]{2,1,0:T(8,128)(2,1)S(1)} %get-tuple-element.125), channel_id=1, source_target_pairs={{0,256},{1,257},{2,258},{3,259},{4,260},{5,261},{6,262},{7,263},{8... | collective-permute-start | bytes 1327112 | tf_op jit(solution)/shard_map/cond/branch_1_fun/ppermute | solution.py:31
  63.1 10.1 %collective-permute-start.8 = (bf16[8,24,1152]{2,1,0:T(8,128)(2,1)S(1)}, bf16[8,24,1152]{2,1,0:T(8,128)(2,1)}, u32[]{:S(2)}, u32[]{:S(2)}) collective-permute-start(bf16[8,24,1152]{2,1,0:T(8,128)(2,1)S(1)} %get-tuple-element.125), channel_id=1, source_target_pairs={{0,384},{1,385},{2,386},{3,387},{4,388},{5,389},{6,390},{7,391},{8... | collective-permute-start | bytes 1327112 | tf_op jit(solution)/shard_map/cond/branch_1_fun/ppermute | solution.py:31
  74.2 34.8 %collective-permute-start.9 = (bf16[8,72,1152]{2,1,0:T(8,128)(2,1)S(1)}, bf16[8,72,1152]{2,1,0:T(8,128)(2,1)}, u32[]{:S(2)}, u32[]{:S(2)}) collective-permute-start(bf16[8,72,1152]{2,1,0:T(8,128)(2,1)S(1)} %constant_dynamic-update-slice_fusion.2), channel_id=1, source_target_pairs={{0,8},{1,9},{2,10},{3,11},{4,12},{5,13},{6,14},{7,15},{8,0},{9,1},... | collective-permute-start | bytes 3981320 | tf_op jit(solution)/shard_map/cond/branch_1_fun/ppermute | solution.py:31
  92.4 14.7 %collective-permute-start.10 = (bf16[384,1152]{1,0:T(8,128)(2,1)}, bf16[384,1152]{1,0:T(8,128)(2,1)}, u32[]{:S(2)}, u32[]{:S(2)}) collective-permute-start(bf16[384,1152]{1,0:T(8,128)(2,1)} %get-tuple-element.127), channel_id=1, source_target_pairs={{8,0},{16,8},{24,16},{32,24},{40,32},{48,40},{56,48},{9,1},{17,9},... | collective-permute-start | bytes 2654216 | tf_op jit(solution)/shard_map/cond/branch_1_fun/ppermute | solution.py:21
  107.1 14.7 %collective-permute-start.11 = (bf16[384,1152]{1,0:T(8,128)(2,1)}, bf16[384,1152]{1,0:T(8,128)(2,1)}, u32[]{:S(2)}, u32[]{:S(2)}) collective-permute-start(bf16[384,1152]{1,0:T(8,128)(2,1)} %collective-permute-done.10), channel_id=1, source_target_pairs={{8,0},{16,8},{24,16},{32,24},{40,32},{48,40},{56,48},{9,1},{17,9},... | collective-permute-start | bytes 2654216 | tf_op jit(solution)/shard_map/cond/branch_1_fun/ppermute | solution.py:21
  122.5 6.4 %copy-start.3 = (bf16[384,1152]{1,0:T(8,128)(2,1)}, bf16[384,1152]{1,0:T(8,128)(2,1)S(1)}, u32[]{:S(2)}) copy-start(bf16[384,1152]{1,0:T(8,128)(2,1)S(1)} %collective-permute-done.32) | copy-start | bytes 2654212
  126.3 1.5 copy-start.9
  128.9 16.1 %collective-permute-start.22 = (bf16[392,1152]{1,0:T(8,128)(2,1)}, bf16[392,1152]{1,0:T(8,128)(2,1)}, u32[]{:S(2)}, u32[]{:S(2)}) collective-permute-start(bf16[392,1152]{1,0:T(8,128)(2,1)} %get-tuple-element.140), channel_id=1, source_target_pairs={{48,8},{49,9},{50,10},{51,11},{52,12},{53,13},{54,14},{55,15},{112... | collective-permute-start | bytes 2709512 | tf_op jit(solution)/shard_map/cond/branch_1_fun/ppermute | solution.py:21
  130.1 14.8 %collective-permute-start.23 = (bf16[392,1152]{1,0:T(8,128)(2,1)}, bf16[392,1152]{1,0:T(8,128)(2,1)}, u32[]{:S(2)}, u32[]{:S(2)}) collective-permute-start(bf16[392,1152]{1,0:T(8,128)(2,1)} %get-tuple-element.140), channel_id=1, source_target_pairs={{0,8},{8,16},{16,24},{24,32},{32,40},{40,48},{48,56},{1,9},{9,17},... | collective-permute-start | bytes 2709512 | tf_op jit(solution)/shard_map/cond/branch_1_fun/ppermute | solution.py:21
  132.2 12.4 %collective-permute-start.21 = (bf16[384,1152]{1,0:T(8,128)(2,1)}, bf16[384,1152]{1,0:T(8,128)(2,1)}, u32[]{:S(2)}, u32[]{:S(2)}) collective-permute-start(bf16[384,1152]{1,0:T(8,128)(2,1)} %get-tuple-element.137), channel_id=1, source_target_pairs={{16,56},{56,40},{17,57},{57,41},{18,58},{58,42},{19,59},{59,43},{2... | collective-permute-start | bytes 2654216 | tf_op jit(solution)/shard_map/cond/branch_1_fun/ppermute | solution.py:21
  134.9 9.7 %collective-permute-start.20 = (bf16[384,1152]{1,0:T(8,128)(2,1)}, bf16[384,1152]{1,0:T(8,128)(2,1)}, u32[]{:S(2)}, u32[]{:S(2)}) collective-permute-start(bf16[384,1152]{1,0:T(8,128)(2,1)} %broadcast_select_fusion.8), channel_id=1, source_target_pairs={{56,48},{48,56},{57,49},{49,57},{58,50},{50,58},{59,51},{51,59},{6... | collective-permute-start | bytes 2654216 | tf_op jit(solution)/shard_map/cond/branch_1_fun/ppermute | solution.py:21
  138.7 0.7 copy-start.12
  144.9 96.9 %collective-permute-start.33 = (bf16[392,1152]{1,0:T(8,128)(2,1)}, bf16[392,1152]{1,0:T(8,128)(2,1)}, u32[]{:S(2)}, u32[]{:S(2)}) collective-permute-start(bf16[392,1152]{1,0:T(8,128)(2,1)} %pad_maximum_fusion.4), channel_id=1, source_target_pairs={{56,64},{40,104},{57,65},{41,105},{58,66},{42,106},{59,67},{43,107... | collective-permute-start | bytes 2709512 | tf_op jit(solution)/shard_map/ppermute | solution.py:21
  146.6 95.3 %collective-permute-start.34 = (bf16[392,1152]{1,0:T(8,128)(2,1)}, bf16[392,1152]{1,0:T(8,128)(2,1)}, u32[]{:S(2)}, u32[]{:S(2)}) collective-permute-start(bf16[392,1152]{1,0:T(8,128)(2,1)} %get-tuple-element.217), channel_id=1, source_target_pairs={{8,72},{9,73},{10,74},{11,75},{12,76},{13,77},{14,78},{15,79},{72,... | collective-permute-start | bytes 2709512 | tf_op jit(solution)/shard_map/ppermute | solution.py:21
  160.4 4.0 %copy-start.2 = (f32[384,1152]{1,0:T(8,128)}, f32[384,1152]{1,0:T(8,128)S(1)}, u32[]{:S(2)}) copy-start(f32[384,1152]{1,0:T(8,128)S(1)} %get-tuple-element.141) | copy-start | bytes 5308420 | tf_op jit(solution)/shard_map/cond
  164.4 1.3 copy-start.13
  165.7 2.2 copy-start.10
  170.4 2.5 copy-start.1
  170.4 2.5 copy-start.14
  174.8 1.5 copy-start.4
  176.4 5.1 %collective-permute-start.24 = (bf16[8,72,1152]{2,1,0:T(8,128)(2,1)S(1)}, bf16[8,72,1152]{2,1,0:T(8,128)(2,1)}, u32[]{:S(2)}, u32[]{:S(2)}) collective-permute-start(bf16[8,72,1152]{2,1,0:T(8,128)(2,1)S(1)} %dynamic-slice_bitcast_fusion.1), channel_id=1, source_target_pairs={{0,8},{1,9},{2,10},{3,11},{4,12},{5,13},{6,14},{7,15},{8,0},{9,1},... | collective-permute-start | bytes 3981320 | tf_op jit(solution)/shard_map/cond/branch_1_fun/ppermute | solution.py:31
  184.6 14.8 %collective-permute-start.27 = (bf16[8,24,1152]{2,1,0:T(8,128)(2,1)}, bf16[8,24,1152]{2,1,0:T(8,128)(2,1)}, u32[]{:S(2)}, u32[]{:S(2)}) collective-permute-start(bf16[8,24,1152]{2,1,0:T(8,128)(2,1)} %get-tuple-element.244), channel_id=1, source_target_pairs={{0,384},{1,385},{2,386},{3,387},{4,388},{5,389},{6,390},{7,391},{8... | collective-permute-start | bytes 1327112 | tf_op jit(solution)/shard_map/cond/branch_1_fun/ppermute | solution.py:31
  187.5 20.0 %collective-permute-start.26 = (bf16[8,24,1152]{2,1,0:T(8,128)(2,1)}, bf16[8,24,1152]{2,1,0:T(8,128)(2,1)}, u32[]{:S(2)}, u32[]{:S(2)}) collective-permute-start(bf16[8,24,1152]{2,1,0:T(8,128)(2,1)} %get-tuple-element.245), channel_id=1, source_target_pairs={{0,256},{1,257},{2,258},{3,259},{4,260},{5,261},{6,262},{7,263},{8... | collective-permute-start | bytes 1327112 | tf_op jit(solution)/shard_map/cond/branch_1_fun/ppermute | solution.py:31
  192.4 24.1 %collective-permute-start.25 = (bf16[8,24,1152]{2,1,0:T(8,128)(2,1)}, bf16[8,24,1152]{2,1,0:T(8,128)(2,1)}, u32[]{:S(2)}, u32[]{:S(2)}) collective-permute-start(bf16[8,24,1152]{2,1,0:T(8,128)(2,1)} %get-tuple-element.243), channel_id=1, source_target_pairs={{0,128},{1,129},{2,130},{3,131},{4,132},{5,133},{6,134},{7,135},{8... | collective-permute-start | bytes 1327112 | tf_op jit(solution)/shard_map/cond/branch_1_fun/ppermute | solution.py:31
  220.1 14.1 %collective-permute-start.30 = (bf16[8,24,384]{2,1,0:T(8,128)(2,1)S(1)}, bf16[8,24,384]{2,1,0:T(8,128)(2,1)S(1)}, u32[]{:S(2)}, u32[]{:S(2)}) collective-permute-start(bf16[8,24,384]{2,1,0:T(8,128)(2,1)S(1)} %get-tuple-element.247), channel_id=1, source_target_pairs={{0,48},{1,49},{2,50},{3,51},{4,52},{5,53},{6,54},{7,55},{8,56},{9,... | collective-permute-start | bytes 442376 | tf_op jit(solution)/shard_map/cond/branch_1_fun/ppermute | solution.py:31
  228.5 8.0 %collective-permute-start.29 = (bf16[8,24,384]{2,1,0:T(8,128)(2,1)S(1)}, bf16[8,24,384]{2,1,0:T(8,128)(2,1)S(1)}, u32[]{:S(2)}, u32[]{:S(2)}) collective-permute-start(bf16[8,24,384]{2,1,0:T(8,128)(2,1)S(1)} %get-tuple-element.248), channel_id=1, source_target_pairs={{0,32},{1,33},{2,34},{3,35},{4,36},{5,37},{6,38},{7,39},{8,40},{9,... | collective-permute-start | bytes 442376 | tf_op jit(solution)/shard_map/cond/branch_1_fun/ppermute | solution.py:31
  231.4 9.2 %collective-permute-start.28 = (bf16[8,24,384]{2,1,0:T(8,128)(2,1)S(1)}, bf16[8,24,384]{2,1,0:T(8,128)(2,1)S(1)}, u32[]{:S(2)}, u32[]{:S(2)}) collective-permute-start(bf16[8,24,384]{2,1,0:T(8,128)(2,1)S(1)} %get-tuple-element.246), channel_id=1, source_target_pairs={{0,16},{1,17},{2,18},{3,19},{4,20},{5,21},{6,22},{7,23},{8,24},{9,... | collective-permute-start | bytes 442376 | tf_op jit(solution)/shard_map/cond/branch_1_fun/ppermute | solution.py:31
  241.9 5.6 %copy-start.5 = (f32[8,24,384]{2,1,0:T(8,128)}, f32[8,24,384]{2,1,0:T(8,128)S(1)}, u32[]{:S(2)}) copy-start(f32[8,24,384]{2,1,0:T(8,128)S(1)} %get-tuple-element.161) | copy-start | bytes 884740 | tf_op jit(solution)/shard_map/cond
  241.9 16.7 %collective-permute-start.18 = (bf16[392,1152]{1,0:T(8,128)(2,1)}, bf16[392,1152]{1,0:T(8,128)(2,1)}, u32[]{:S(2)}, u32[]{:S(2)}) collective-permute-start(bf16[392,1152]{1,0:T(8,128)(2,1)} %get-tuple-element.166), channel_id=1, source_target_pairs={{0,8},{8,16},{16,24},{24,32},{32,40},{40,48},{48,56},{1,9},{9,17},... | collective-permute-start | bytes 2709512 | tf_op jit(solution)/shard_map/cond/branch_1_fun/ppermute | solution.py:21
  244.0 12.0 %collective-permute-start.12 = (bf16[4,24,384]{2,1,0:T(8,128)(2,1)S(1)}, bf16[4,24,384]{2,1,0:T(8,128)(2,1)S(1)}, u32[]{:S(2)}, u32[]{:S(2)}) collective-permute-start(bf16[4,24,384]{2,1,0:T(8,128)(2,1)S(1)} %fusion.36), channel_id=1, source_target_pairs={{0,4},{1,5},{2,6},{3,7},{4,0},{5,1},{6,2},{7,3},{8,12},{9,13},{10,... | collective-permute-start | bytes 221192 | tf_op jit(solution)/shard_map/cond/branch_1_fun/ppermute | solution.py:31
  245.9 40.7 %collective-permute-start.17 = (bf16[392,1152]{1,0:T(8,128)(2,1)}, bf16[392,1152]{1,0:T(8,128)(2,1)}, u32[]{:S(2)}, u32[]{:S(2)}) collective-permute-start(bf16[392,1152]{1,0:T(8,128)(2,1)} %get-tuple-element.164), channel_id=1, source_target_pairs={{40,0},{0,16},{41,1},{1,17},{42,2},{2,18},{43,3},{3,19},{44,4},{4,... | collective-permute-start | bytes 2709512 | tf_op jit(solution)/shard_map/cond/branch_1_fun/ppermute | solution.py:21
  247.5 8.4 %copy-start.6 = (f32[8,24,384]{2,1,0:T(8,128)S(1)}, f32[8,24,384]{2,1,0:T(8,128)}, u32[]{:S(2)}) copy-start(f32[8,24,384]{2,1,0:T(8,128)} %copy-done.5) | copy-start | bytes 884740 | tf_op jit(solution)/shard_map/cond
  248.9 37.7 %collective-permute-start.16 = (bf16[392,1152]{1,0:T(8,128)(2,1)S(1)}, bf16[392,1152]{1,0:T(8,128)(2,1)}, u32[]{:S(2)}, u32[]{:S(2)}) collective-permute-start(bf16[392,1152]{1,0:T(8,128)(2,1)S(1)} %broadcast_select_fusion.15), channel_id=1, source_target_pairs={{0,8},{8,0},{1,9},{9,1},{2,10},{10,2},{3,11},{11,3},{4,12},{12,4},... | collective-permute-start | bytes 2709512 | tf_op jit(solution)/shard_map/cond/branch_1_fun/ppermute | solution.py:21
  258.6 28.0 %collective-permute-start.19 = (bf16[392,1152]{1,0:T(8,128)(2,1)}, bf16[392,1152]{1,0:T(8,128)(2,1)}, u32[]{:S(2)}, u32[]{:S(2)}) collective-permute-start(bf16[392,1152]{1,0:T(8,128)(2,1)} %collective-permute-done.18), channel_id=1, source_target_pairs={{0,8},{8,16},{16,24},{24,32},{32,40},{40,48},{48,56},{1,9},{9,17},... | collective-permute-start | bytes 2709512 | tf_op jit(solution)/shard_map/cond/branch_1_fun/ppermute | solution.py:21
  263.0 5.6 %collective-permute-start.13 = (bf16[2,24,384]{2,1,0:T(8,128)(2,1)S(1)}, bf16[2,24,384]{2,1,0:T(8,128)(2,1)S(1)}, u32[]{:S(2)}, u32[]{:S(2)}) collective-permute-start(bf16[2,24,384]{2,1,0:T(8,128)(2,1)S(1)} %fusion.37), channel_id=1, source_target_pairs={{0,2},{1,3},{2,0},{3,1},{4,6},{5,7},{6,4},{7,5},{8,10},{9,11},{10,... | collective-permute-start | bytes 110600 | tf_op jit(solution)/shard_map/cond/branch_1_fun/ppermute | solution.py:31
  268.6 4.5 %collective-permute-start.14 = (bf16[1,24,384]{2,1,0:T(8,128)(2,1)S(1)}, bf16[1,24,384]{2,1,0:T(8,128)(2,1)S(1)}, u32[]{:S(2)}, u32[]{:S(2)}) collective-permute-start(bf16[1,24,384]{2,1,0:T(8,128)(2,1)S(1)} %dynamic-slice_convert_fusion.8), channel_id=1, source_target_pairs={{0,1},{1,0},{2,3},{3,2},{4,5},{5,4},{6,7},{7,6},{8,9},{9,8},{10,11... | collective-permute-start | bytes 55304 | tf_op jit(solution)/shard_map/cond/branch_1_fun/ppermute | solution.py:31
  273.1 13.4 %collective-permute-start.15 = (f32[24,384]{1,0:T(8,128)S(1)}, f32[24,384]{1,0:T(8,128)S(1)}, u32[]{:S(2)}, u32[]{:S(2)}) collective-permute-start(f32[24,384]{1,0:T(8,128)S(1)} %add_bitcast_fusion), channel_id=1, source_target_pairs={{0,64},{1,65},{2,66},{3,67},{4,68},{5,69},{6,70},{7,71},{8,72},{9,... | collective-permute-start | bytes 110600 | tf_op jit(solution)/shard_map/cond/branch_1_fun/ppermute | solution.py:31
  296.1 4.5 %collective-permute-start.35 = (bf16[1,24,384]{2,1,0:T(8,128)(2,1)S(1)}, bf16[1,24,384]{2,1,0:T(8,128)(2,1)S(1)}, u32[]{:S(2)}, u32[]{:S(2)}) collective-permute-start(bf16[1,24,384]{2,1,0:T(8,128)(2,1)S(1)} %bitcast.138), channel_id=1, source_target_pairs={{0,16},{1,17},{2,18},{3,19},{4,20},{5,21},{6,22},{7,23},{8,24},{9,... | collective-permute-start | bytes 55304 | tf_op jit(solution)/shard_map/ppermute | solution.py:31
  300.7 6.2 %collective-permute-start.36 = (bf16[2,24,384]{2,1,0:T(8,128)(2,1)S(1)}, bf16[2,24,384]{2,1,0:T(8,128)(2,1)S(1)}, u32[]{:S(2)}, u32[]{:S(2)}) collective-permute-start(bf16[2,24,384]{2,1,0:T(8,128)(2,1)S(1)} %pad_maximum_fusion.7), channel_id=1, source_target_pairs={{0,32},{1,33},{2,34},{3,35},{4,36},{5,37},{6,38},{7,39},{8,40},{9,... | collective-permute-start | bytes 110600 | tf_op jit(solution)/shard_map/ppermute | solution.py:31
  306.9 6.0 %collective-permute-start.37 = (bf16[1,24,1152]{2,1,0:T(8,128)(2,1)S(1)}, bf16[1,24,1152]{2,1,0:T(8,128)(2,1)S(1)}, u32[]{:S(2)}, u32[]{:S(2)}) collective-permute-start(bf16[1,24,1152]{2,1,0:T(8,128)(2,1)S(1)} %maximum_bitcast_fusion), channel_id=1, source_target_pairs={{0,128},{1,129},{2,130},{3,131},{4,132},{5,133},{6,134},{7,135},{8... | collective-permute-start | bytes 165896 | tf_op jit(solution)/shard_map/ppermute | solution.py:31
  311.4 7.5 %copy-start = (bf16[384,1152]{1,0:T(8,128)(2,1)S(1)}, bf16[384,1152]{1,0:T(8,128)(2,1)}, u32[]{:S(2)}) copy-start(bf16[384,1152]{1,0:T(8,128)(2,1)} %param.18) | copy-start | bytes 2654212
  311.5 7.5 %copy-start.8 = (f32[384]{0:T(512)S(1)}, f32[384]{0:T(512)}, u32[]{:S(2)}) copy-start(f32[384]{0:T(512)} %copy-done.7) | copy-start | bytes 4612
  313.0 8.1 %collective-permute-start.38 = (bf16[2,24,1152]{2,1,0:T(8,128)(2,1)S(1)}, bf16[2,24,1152]{2,1,0:T(8,128)(2,1)S(1)}, u32[]{:S(2)}, u32[]{:S(2)}) collective-permute-start(bf16[2,24,1152]{2,1,0:T(8,128)(2,1)S(1)} %pad_maximum_fusion.6), channel_id=1, source_target_pairs={{0,256},{1,257},{2,258},{3,259},{4,260},{5,261},{6,262},{7,263},{8... | collective-permute-start | bytes 331784 | tf_op jit(solution)/shard_map/ppermute | solution.py:31
  321.2 9.3 %collective-permute-start.39 = (bf16[72,1152]{1,0:T(8,128)(2,1)S(1)}, bf16[72,1152]{1,0:T(8,128)(2,1)S(1)}, u32[]{:S(2)}, u32[]{:S(2)}) collective-permute-start(bf16[72,1152]{1,0:T(8,128)(2,1)S(1)} %pad_maximum_fusion.5), channel_id=1, source_target_pairs={{0,8},{1,9},{2,10},{3,11},{4,12},{5,13},{6,14},{7,15},{8,0},{9,1},... | collective-permute-start | bytes 497672 | tf_op jit(solution)/shard_map/ppermute | solution.py:31

commit v4 on v3

--- a/solution.py
+++ b/solution.py
@@ -93,20 +93,42 @@
 
         return lax.cond(scale > 0.0, stage, unused, *blocks)
 
-    def z_shift(block, d):
-        def target(x, hi, y, c, q):
+    LINE = 2
+
+    def on_line(block, d_y, target):
+        route = []
+        for p in range(width_dp):
+            for q in range(lanes):
+                x, hi, y, core = p // 16, p // 8 % 2, p // 2 % 4, p % 2
+                if y == LINE:
+                    hi2, q2 = target(hi, q)
+                    p2 = ((x * 2 + hi2) * 4 + (y + d_y) % SIDE) * 2 + core
+                    route.append((p * lanes + q, p2 * lanes + q2))
+        return lax.ppermute(block, AXES, route)
+
+    def line_shift(block, d):
+        def target(hi, q):
             z = (hi * lanes + q + d) % (2 * lanes)
-            return x, z // lanes, y, c, z % lanes
-
-        return coords(block, target)
+            return z // lanes, z % lanes
+
+        return on_line(block, 0, target)
 
     def gather_z(mine):
         bit = 1
         while 2 * bit < lanes:
-            mine = in_order(mine, z_flip(mine, bit), lane // bit % 2, 0)
+            theirs = on_line(mine, 0, lambda hi, q, bit=bit: (hi, q ^ bit))
+            mine = in_order(mine, theirs, lane // bit % 2, 0)
             bit *= 2
-        theirs = jnp.concatenate([z_shift(mine[: bit // 2], bit), z_shift(mine[bit // 2 :], -bit)])
+        theirs = jnp.concatenate(
+            [line_shift(mine[: bit // 2], bit), line_shift(mine[bit // 2 :], -bit)]
+        )
         return in_order(mine, theirs, lane // bit % 2, 0)
+
+    def gather_y(strip):
+        came = [on_line(strip, d, lambda hi, q: (hi, q)) for d in range(1, SIDE)]
+        for d, piece in enumerate(came):
+            strip = jnp.where(at_y == (LINE + 1 + d) % SIDE, piece, strip)
+        return strip
 
     def gather_x(strip):
         pieces = [strip] + [x_shift(strip, d) for d in range(1, SIDE)]
@@ -142,18 +164,16 @@
 
     ready, unit_txt = lax.optimization_barrier((head_weight, unit_txt))
     mine = lax.dynamic_slice_in_dim(ready, core * half + at_x * step, window, 0)[None]
-    mine, moved, near_1 = one_step(
-        lambda m: (gather_z(m), chain(unit_txt, [(1, 0, 6)]), chain(unit_txt, down)), mine
-    )
-    unit_far, mine = lax.optimization_barrier((unit_txt, mine))
-    far = chain(unit_far, [(0, -1, 7), (2, -1, 2)])
+    far = chain(unit_txt, [(0, -1, 7), (2, -1, 2)])
+
+    def along_z(mine):
+        moved = chain(unit_txt, [(1, 0, 6)])
+        near_1 = chain(unit_txt, down)
+        return gather_z(mine), moved, near_1, chain(near_1, down)
+
+    mine, moved, near_1, near_2 = one_step(along_z, mine)
     far_1 = chain(moved, [(6, -1, 6)])
-
-    def gather_and_chain(mine, near_1):
-        near_2 = chain(near_1, down)
-        return gather_x(mine), near_2, chain(near_2, down)
-
-    full_weight, near_2, near_3 = one_step(gather_and_chain, mine, near_1)
+    full_weight = one_step(lambda m: gather_x(gather_y(m)), mine)
     full_weight, far, far_1 = lax.optimization_barrier((full_weight, far, far_1))
 
     projected = jnp.dot(image_features, full_weight, preferred_element_type=f32)
@@ -185,11 +205,10 @@
         swapped = chain(jnp.where(last, far, far_1), [(7, 0, 6), (6, 0, 7)])
         passed = chain(far, [(2, 0, 7), (7, 0, 5)])
         back_0 = chain(parcel, [(6, 0, 1)])
-        beside_1 = chain(parcel, up)
         img_grad = met_grad(unit_txt, 0) + met_grad(jnp.where(last, far, near_1), 1)
-        return img_grad, swapped, passed, back_0, beside_1
-
-    def head_terms(img_grad, swapped, passed):
+        return img_grad, swapped, passed, back_0, chain(near_2, down)
+
+    def head_terms(img_grad, swapped, passed, near_3):
         text_3 = jnp.where(slot >= GROUP - 3, passed, near_3)
         text_3 = jnp.where(slot == GROUP - 2, far_1, text_3)
         img_grad = img_grad + met_grad(jnp.where(slot >= GROUP - 2, swapped, near_2), 2)
@@ -205,33 +224,39 @@
         theirs = lax.dynamic_index_in_dim(term, 1 - core, 1, keepdims=False)
         return ours.astype(f32) + core_swap(theirs).astype(f32)
 
-    def sum_z(total):
-        bit = lanes // 2
-        while bit:
+    def sum_z(total, bits):
+        for bit in bits:
             halves = total.reshape(2, bit, window, window_y)
             side = lane // bit % 2
             keep = lax.dynamic_index_in_dim(halves, side, 0, keepdims=False)
             give = lax.dynamic_index_in_dim(halves, 1 - side, 0, keepdims=False)
             total = keep + z_flip(give.astype(bf16), bit).astype(f32)
-            bit //= 2
-        total = total.reshape(window, window_y)
-        return (total + hi_flip(total)).astype(bf16)
-
-    img_grad, swapped, passed, back_0, beside_1 = one_step(meet_texts, far, far_1)
+        return total
+
+    bits = [1 << j for j in reversed(range(lanes.bit_length() - 1))]
+
+    img_grad, swapped, passed, back_0, near_3 = one_step(meet_texts, far, far_1)
     parcel_far, img_grad = lax.optimization_barrier((parcel, img_grad))
     back = chain(parcel_far, [(7, 1, 0), (5, 1, 5)])
     back_1 = chain(back_0, [(1, 1, 1)])
 
-    total = one_step(lambda *blocks: sum_xy(head_terms(*blocks)), img_grad, swapped, passed)
-    total, back, back_1 = lax.optimization_barrier((total, back, back_1))
+    total = one_step(lambda *blocks: sum_xy(head_terms(*blocks)), img_grad, swapped, passed, near_3)
+    total, back, back_1, parcel_near = lax.optimization_barrier((total, back, back_1, parcel))
 
     def sum_z_and_chain(total, back, back_1):
-        beside_2 = chain(beside_1, up)
         swapped = chain(jnp.where(first, back, back_1), [(0, 0, 1), (1, 0, 0)])
         passed = chain(back, [(5, 0, 0), (0, 0, 2)])
-        return sum_z(total), swapped, passed, beside_2, chain(beside_2, up)
-
-    total_z, swapped, passed, beside_2, beside_3 = one_step(sum_z_and_chain, total, back, back_1)
+        return sum_z(total, bits[:-1]), swapped, passed
+
+    def sum_z_last(total, beside_1):
+        total = sum_z(total, bits[-1:]).reshape(window, window_y)
+        return (total + hi_flip(total)).astype(bf16), chain(beside_1, up)
+
+    beside_1 = chain(parcel_near, up)
+    total, swapped, passed = one_step(sum_z_and_chain, total, back, back_1)
+    total, beside_1 = lax.optimization_barrier((total, beside_1))
+    total_z, beside_2 = one_step(sum_z_last, total, beside_1)
+    beside_3 = chain(beside_2, up)
     parcel, total_z = lax.optimization_barrier((parcel, total_z))
     image_3 = jnp.where(slot <= 2, passed, beside_3)
     images = [

time: 334 us -> 340 us (1.018)
  waiting for transfers between devices: 102 us -> 124 us
  starting transfers between devices: 157 us -> 140 us
    ppermute x24 -> x20, starting transfers between devices: 107 us -> 71.6 us  [by_coords(): return lax.ppermute(block, AXES, route)]
    ppermute x0 -> x7, waiting for transfers between devices: none -> 12.4 us  [on_line(): return lax.ppermute(block, AXES, route)]
    ppermute x16, starting transfers between devices: 50.5 us -> 62.4 us  [along_chain(): return lax.ppermute(block, AXES, route)]
    ppermute x16, waiting for transfers between devices: 25.2 us -> 34 us  [along_chain(): return lax.ppermute(block, AXES, route)]
    ppermute x0 -> x7, starting transfers between devices: none -> 6.05 us  [on_line(): return lax.ppermute(block, AXES, route)]
    ppermute x24 -> x20, waiting for transfers between devices: 76.8 us -> 77.1 us  [by_coords(): return lax.ppermute(block, AXES, route)]
  transfers between devices with their start and end apart: 40 -> 43, of which waited for: 23 -> 20; matrix products, arithmetic and copies ran while one was open for 13% -> 15% of each run, Pallas kernels for 0% -> 0%
where the time goes in v4:
time: 340 us; the launch traced here: 338 us
  starting transfers between devices  140 us (41%)
  waiting for transfers between devices  124 us (36%)
  matrix products  31 us (9%)
  other arithmetic  29.2 us (9%)
  local copies, waits for them, and re-layouts  9.97 us (3%)
    ppermute x20, waiting for transfers between devices, by_coords(): return lax.ppermute(block, AXES, route)  77.1 us
    ppermute x20, starting transfers between devices, by_coords(): return lax.ppermute(block, AXES, route)  71.6 us
    ppermute x16, starting transfers between devices, along_chain(): return lax.ppermute(block, AXES, route)  62.4 us
    ppermute x16, waiting for transfers between devices, along_chain(): return lax.ppermute(block, AXES, route)  34 us
    ppermute x7, waiting for transfers between devices, on_line(): return lax.ppermute(block, AXES, route)  12.4 us
    dot_general x4, matrix products, met_grad(): logits = jnp.einsum('ie,je->ij', unit_img, text, preferred_element_type=f32)  9.44 us
    dot_general x4, matrix products, met_grad(): return scale * jnp.dot(weights, text, preferred_element_type=f32)  7.45 us
  transfers between devices with their start and end apart: 43, of which 20 were waited for; matrix products, arithmetic and copies ran while one was open for 15% of the time, Pallas kernels for 0%

profile of v4, /device:TPU:1, one launch (start us, length us, event | category | flops | bytes accessed | tf_op | source)
XLA Modules:
  0.0 337.7 jit_solution(3597592560445276110)
XLA Ops:
  6.4 49.5 %conditional.6 = (bf16[8,24,1152]{2,1,0:T(8,128)(2,1)S(1)}, bf16[384,1152]{1,0:T(8,128)(2,1)}, bf16[384,1152]{1,0:T(8,128)(2,1)}, bf16[384,1152]{1,0:T(8,128)(2,1)}) conditional(s32[]{:T(128)} %convert_element_type.172, () %tuple.64, (s32[]{:T(128)}, s32[]{:T(128)}, s32[]{:T(128)}, bf16[144,1152]{1,0:T(8,128)(2,1)}, ...), branch_computations={%region_1.2_spmd, %region_2.3_spmd} | conditional | flops 829500 | bytes 15373216 | solution.py:94
  9.5 22.6 %collective-permute-start.5 = (bf16[384,1152]{1,0:T(8,128)(2,1)S(1)}, bf16[384,1152]{1,0:T(8,128)(2,1)}, u32[]{:S(2)}, u32[]{:S(2)}) collective-permute-start(bf16[384,1152]{1,0:T(8,128)(2,1)S(1)} %get-tuple-element.132), channel_id=1, source_target_pairs={{8,0},{16,8},{24,16},{32,24},{40,32},{48,40},{56,48},{9,1},{17,9},... | collective-permute-start | bytes 2654216 | tf_op jit(solution)/shard_map/cond/branch_1_fun/ppermute | solution.py:21
  32.8 2.2 collective-permute-start.4
  35.7 5.5 %collective-permute-done.5 = bf16[384,1152]{1,0:T(8,128)(2,1)} collective-permute-done((bf16[384,1152]{1,0:T(8,128)(2,1)S(1)}, bf16[384,1152]{1,0:T(8,128)(2,1)}, u32[]{:S(2)}, u32[]{:S(2)}) %collective-permute-start.5) | collective-permute-done | bytes 884768 | tf_op jit(solution)/shard_map/cond/branch_1_fun/ppermute | solution.py:21
  41.2 1.9 collective-permute-start.6
  44.1 11.8 %collective-permute-done.6 = bf16[384,1152]{1,0:T(8,128)(2,1)} collective-permute-done((bf16[384,1152]{1,0:T(8,128)(2,1)}, bf16[384,1152]{1,0:T(8,128)(2,1)}, u32[]{:S(2)}, u32[]{:S(2)}) %collective-permute-start.6) | collective-permute-done | bytes 884768 | tf_op jit(solution)/shard_map/cond/branch_1_fun/ppermute | solution.py:21
  57.3 54.7 %conditional.7 = (bf16[1152,1152]{1,0:T(8,128)(2,1)}) conditional(s32[]{:T(128)} %convert_element_type.172, () %tuple.63, (s32[]{:T(128)}, s32[]{:T(128)}, bf16[8,24,1152]{2,1,0:T(8,128)(2,1)S(1)}, s32[]{:T(128)}) %tuple.67), branch_computations={%region_3.4_spmd, %region_4.5_spmd} | conditional | flops 7299139 | bytes 36717588 | solution.py:94
  60.7 12.4 %collective-permute-done.15 = bf16[8,24,1152]{2,1,0:T(8,128)(2,1)S(1)} collective-permute-done((bf16[8,24,1152]{2,1,0:T(8,128)(2,1)S(1)}, bf16[8,24,1152]{2,1,0:T(8,128)(2,1)S(1)}, u32[]{:S(2)}, u32[]{:S(2)}) %collective-permute-start.15) | collective-permute-done | bytes 442400 | tf_op jit(solution)/shard_map/cond/branch_1_fun/ppermute | solution.py:107
  74.0 2.0 constant_dynamic-update-slice_fusion.5
  76.1 2.7 collective-permute-start.17
  78.8 4.1 %collective-permute-start.18 = (bf16[8,24,1152]{2,1,0:T(8,128)(2,1)}, bf16[8,24,1152]{2,1,0:T(8,128)(2,1)S(1)}, u32[]{:S(2)}, u32[]{:S(2)}) collective-permute-start(bf16[8,24,1152]{2,1,0:T(8,128)(2,1)} %get-tuple-element.240), channel_id=1, source_target_pairs={{0,256},{1,257},{2,258},{3,259},{4,260},{5,261},{6,262},{7,263},{8... | collective-permute-start | bytes 1327112 | tf_op jit(solution)/shard_map/cond/branch_1_fun/ppermute | solution.py:31
  82.9 3.4 collective-permute-start.19
  86.3 14.6 %collective-permute-done.17 = bf16[8,24,1152]{2,1,0:T(8,128)(2,1)} collective-permute-done((bf16[8,24,1152]{2,1,0:T(8,128)(2,1)}, bf16[8,24,1152]{2,1,0:T(8,128)(2,1)}, u32[]{:S(2)}, u32[]{:S(2)}) %collective-permute-start.17) | collective-permute-done | bytes 442400 | tf_op jit(solution)/shard_map/cond/branch_1_fun/ppermute | solution.py:31
  103.2 2.7 collective-permute-start.20
  105.9 2.8 collective-permute-done.20
  112.7 3.9 %multiply_reduce_fusion.2 = (f32[384]{0:T(512)S(1)}, f32[1152,384]{0,1:T(8,128)S(1)}) fusion(bf16[384,1152]{1,0:T(8,128)(2,1)} %param.18, bf16[1152,1152]{1,0:T(8,128)(2,1)} %get-tuple-element.319), kind=kOutput, calls=%fused_computation.107 | convolution fusion | flops 1020100224 | bytes 5309952 | tf_op jit(solution)/shard_map/dot_general | solution.py:179
  119.1 32.1 %conditional.8 = (f32[384,1152]{1,0:T(8,128)S(1)}, bf16[384,1152]{1,0:T(8,128)(2,1)}, bf16[384,1152]{1,0:T(8,128)(2,1)}, bf16[392,1152]{1,0:T(8,128)(2,1)}, bf16[384,1152]{1,0:T(8,128)(2,1)}) conditional(s32[]{:T(128)} %convert_element_type.172, () %tuple.72, (f32[]{:T(128)}, s32[384]{0:T(512)S(1)}, s32[384]{0:T(512)S(1)}, s32[384]{0:T(512)S(1)}, ...), branch_computations={%region_6.7_spmd, %region_7.8_spmd} | conditional | flops 1364854272 | bytes 35190020 | solution.py:94
  124.6 2.6 collective-permute-start.24
  130.2 2.6 fusion.13
  133.4 1.8 fusion
  135.3 15.9 %collective-permute-done.24 = bf16[384,1152]{1,0:T(8,128)(2,1)} collective-permute-done((bf16[384,1152]{1,0:T(8,128)(2,1)}, bf16[384,1152]{1,0:T(8,128)(2,1)}, u32[]{:S(2)}, u32[]{:S(2)}) %collective-permute-start.24) | collective-permute-done | bytes 884768 | tf_op jit(solution)/shard_map/cond/branch_1_fun/ppermute | solution.py:21
  152.8 11.3 %collective-permute-start.35 = (bf16[392,1152]{1,0:T(8,128)(2,1)}, bf16[392,1152]{1,0:T(8,128)(2,1)}, u32[]{:S(2)}, u32[]{:S(2)}) collective-permute-start(bf16[392,1152]{1,0:T(8,128)(2,1)} %get-tuple-element.225), channel_id=1, source_target_pairs={{8,72},{9,73},{10,74},{11,75},{12,76},{13,77},{14,78},{15,79},{72,... | collective-permute-start | bytes 2709512 | tf_op jit(solution)/shard_map/ppermute | solution.py:21
  164.2 73.0 %conditional.9 = (f32[8,24,384]{2,1,0:T(8,128)S(1)}) conditional(s32[]{:T(128)} %convert_element_type.172, () %tuple.71, (f32[]{:T(128)}, s32[384]{0:T(512)S(1)}, s32[384]{0:T(512)S(1)}, s32[384]{0:T(512)S(1)}, s32[384]{0:T(512)S(1)}, /*index=5*/s32[]{:T(128)}, bf16[384,1152]{1,0:T(8,128)(2,1)}, bf16[384,1152]{1,0:T(8,128)(2,1)}, ...), branch_computations={%region_8.9_spmd, %region_9.11_spmd} | conditional | flops 2392696320 | bytes 84084168 | solution.py:94
  165.0 3.3 fusion.33
  169.7 2.2 fusion.32
  171.9 2.5 fusion.15
  174.4 2.5 multiply_reduce_fusion
  176.9 1.9 convolution_convert_fusion
  180.4 1.9 collective-permute-start.25
  182.4 3.1 collective-permute-done.25
  185.4 2.0 convert_add_fusion
  188.5 5.1 %collective-permute-start.28 = (bf16[8,24,1152]{2,1,0:T(8,128)(2,1)}, bf16[8,24,1152]{2,1,0:T(8,128)(2,1)}, u32[]{:S(2)}, u32[]{:S(2)}) collective-permute-start(bf16[8,24,1152]{2,1,0:T(8,128)(2,1)} %get-tuple-element.254), channel_id=1, source_target_pairs={{0,384},{1,385},{2,386},{3,387},{4,388},{5,389},{6,390},{7,391},{8... | collective-permute-start | bytes 1327112 | tf_op jit(solution)/shard_map/cond/branch_1_fun/ppermute | solution.py:31
  193.6 2.8 collective-permute-start.27
  196.5 1.9 collective-permute-start.26
  198.5 14.2 %collective-permute-done.28 = bf16[8,24,1152]{2,1,0:T(8,128)(2,1)} collective-permute-done((bf16[8,24,1152]{2,1,0:T(8,128)(2,1)}, bf16[8,24,1152]{2,1,0:T(8,128)(2,1)}, u32[]{:S(2)}, u32[]{:S(2)}) %collective-permute-start.28) | collective-permute-done | bytes 442400 | tf_op jit(solution)/shard_map/cond/branch_1_fun/ppermute | solution.py:31
  212.7 6.2 %collective-permute-done.26 = bf16[8,24,1152]{2,1,0:T(8,128)(2,1)} collective-permute-done((bf16[8,24,1152]{2,1,0:T(8,128)(2,1)}, bf16[8,24,1152]{2,1,0:T(8,128)(2,1)}, u32[]{:S(2)}, u32[]{:S(2)}) %collective-permute-start.26) | collective-permute-done | bytes 442400 | tf_op jit(solution)/shard_map/cond/branch_1_fun/ppermute | solution.py:31
  218.9 2.4 convert_add_fusion.1
  222.5 1.9 collective-permute-start.31
  224.4 1.9 collective-permute-start.30
  226.4 3.4 collective-permute-start.29
  229.8 3.0 collective-permute-done.30
  232.8 3.2 collective-permute-done.29
  237.9 1.9 collective-permute-start.36
  240.6 26.6 %conditional.10 = (f32[2,24,384]{2,1,0:T(8,128)S(1)}, bf16[392,1152]{1,0:T(8,128)(2,1)}, bf16[392,1152]{1,0:T(8,128)(2,1)}) conditional(s32[]{:T(128)} %convert_element_type.172, () %tuple.70, (f32[8,24,384]{2,1,0:T(8,128)}, s32[]{:T(128)}, pred[]{:T(512)}, bf16[392,1152]{1,0:T(8,128)(2,1)}, bf16[392,1152]{1,0:T(8,128)(2,1)}) %tuple.124), branch_computations={%region_11.12_spmd, %region_12.13_spmd} | conditional | flops 562237 | bytes 12331868 | solution.py:94
  242.0 2.6 collective-permute-start.9
  246.2 5.3 %collective-permute-start.7 = (bf16[4,24,384]{2,1,0:T(8,128)(2,1)S(1)}, bf16[4,24,384]{2,1,0:T(8,128)(2,1)S(1)}, u32[]{:S(2)}, u32[]{:S(2)}) collective-permute-start(bf16[4,24,384]{2,1,0:T(8,128)(2,1)S(1)} %fusion.36), channel_id=1, source_target_pairs={{0,4},{1,5},{2,6},{3,7},{4,0},{5,1},{6,2},{7,3},{8,12},{9,13},{10,... | collective-permute-start | bytes 221192 | tf_op jit(solution)/shard_map/cond/branch_1_fun/ppermute | solution.py:31
  251.6 3.7 %collective-permute-done.7 = bf16[4,24,384]{2,1,0:T(8,128)(2,1)S(1)} collective-permute-done((bf16[4,24,384]{2,1,0:T(8,128)(2,1)S(1)}, bf16[4,24,384]{2,1,0:T(8,128)(2,1)S(1)}, u32[]{:S(2)}, u32[]{:S(2)}) %collective-permute-start.7) | collective-permute-done | bytes 73760 | tf_op jit(solution)/shard_map/cond/branch_1_fun/ppermute | solution.py:31
  255.3 10.5 %collective-permute-start.8 = (bf16[2,24,384]{2,1,0:T(8,128)(2,1)S(1)}, bf16[2,24,384]{2,1,0:T(8,128)(2,1)S(1)}, u32[]{:S(2)}, u32[]{:S(2)}) collective-permute-start(bf16[2,24,384]{2,1,0:T(8,128)(2,1)S(1)} %fusion.37), channel_id=1, source_target_pairs={{0,2},{1,3},{2,0},{3,1},{4,6},{5,7},{6,4},{7,5},{8,10},{9,11},{10,... | collective-permute-start | bytes 110600 | tf_op jit(solution)/shard_map/cond/branch_1_fun/ppermute | solution.py:31
  267.2 22.3 %conditional.11 = (bf16[24,384]{1,0:T(8,128)(2,1)S(1)}, bf16[392,1152]{1,0:T(8,128)(2,1)}) conditional(s32[]{:T(128)} %convert_element_type.172, () %tuple.69, (s32[]{:T(128)}, f32[2,24,384]{2,1,0:T(8,128)S(1)}, bf16[392,1152]{1,0:T(8,128)(2,1)S(1)}) %tuple.79), branch_computations={%region_13.14_spmd, %region_14.15_spmd} | conditional | flops 36882 | bytes 4055373 | solution.py:94
  267.2 1.9 collective-permute-start.13
  269.2 5.7 %collective-permute-start.11 = (bf16[1,24,384]{2,1,0:T(8,128)(2,1)S(1)}, bf16[1,24,384]{2,1,0:T(8,128)(2,1)S(1)}, u32[]{:S(2)}, u32[]{:S(2)}) collective-permute-start(bf16[1,24,384]{2,1,0:T(8,128)(2,1)S(1)} %dynamic-slice_convert_fusion.8), channel_id=1, source_target_pairs={{0,1},{1,0},{2,3},{3,2},{4,5},{5,4},{6,7},{7,6},{8,9},{9,8},{10,11... | collective-permute-start | bytes 55304 | tf_op jit(solution)/shard_map/cond/branch_1_fun/ppermute | solution.py:31
  276.0 1.9 collective-permute-start.12
  278.0 11.5 %collective-permute-done.12 = f32[24,384]{1,0:T(8,128)S(1)} collective-permute-done((f32[24,384]{1,0:T(8,128)S(1)}, f32[24,384]{1,0:T(8,128)S(1)}, u32[]{:S(2)}, u32[]{:S(2)}) %collective-permute-start.12) | collective-permute-done | bytes 36896 | tf_op jit(solution)/shard_map/cond/branch_1_fun/ppermute | solution.py:31
  290.2 5.3 %collective-permute-start.37 = (bf16[392,1152]{1,0:T(8,128)(2,1)}, bf16[392,1152]{1,0:T(8,128)(2,1)S(1)}, u32[]{:S(2)}, u32[]{:S(2)}) collective-permute-start(bf16[392,1152]{1,0:T(8,128)(2,1)} %get-tuple-element.236), channel_id=1, source_target_pairs={{0,8},{8,16},{16,24},{24,32},{32,40},{40,48},{48,56},{1,9},{9,17},... | collective-permute-start | bytes 2709512 | tf_op jit(solution)/shard_map/ppermute | solution.py:21
  296.8 4.5 %collective-permute-start.38 = (bf16[1,24,384]{2,1,0:T(8,128)(2,1)S(1)}, bf16[1,24,384]{2,1,0:T(8,128)(2,1)S(1)}, u32[]{:S(2)}, u32[]{:S(2)}) collective-permute-start(bf16[1,24,384]{2,1,0:T(8,128)(2,1)S(1)} %bitcast.139), channel_id=1, source_target_pairs={{0,16},{1,17},{2,18},{3,19},{4,20},{5,21},{6,22},{7,23},{8,24},{9,... | collective-permute-start | bytes 55304 | tf_op jit(solution)/shard_map/ppermute | solution.py:31
  301.3 5.0 %collective-permute-done.38 = bf16[1,24,384]{2,1,0:T(8,128)(2,1)S(1)} collective-permute-done((bf16[1,24,384]{2,1,0:T(8,128)(2,1)S(1)}, bf16[1,24,384]{2,1,0:T(8,128)(2,1)S(1)}, u32[]{:S(2)}, u32[]{:S(2)}) %collective-permute-start.38) | collective-permute-done | bytes 18464 | tf_op jit(solution)/shard_map/ppermute | solution.py:31
  306.3 5.2 %collective-permute-start.39 = (bf16[2,24,384]{2,1,0:T(8,128)(2,1)S(1)}, bf16[2,24,384]{2,1,0:T(8,128)(2,1)S(1)}, u32[]{:S(2)}, u32[]{:S(2)}) collective-permute-start(bf16[2,24,384]{2,1,0:T(8,128)(2,1)S(1)} %pad_maximum_fusion.7), channel_id=1, source_target_pairs={{0,32},{1,33},{2,34},{3,35},{4,36},{5,37},{6,38},{7,39},{8,40},{9,... | collective-permute-start | bytes 110600 | tf_op jit(solution)/shard_map/ppermute | solution.py:31
  311.5 2.0 fusion.68
  313.5 1.9 collective-permute-start.40
  315.5 2.9 collective-permute-done.40
  318.5 2.7 collective-permute-start.41
  322.1 3.4 %collective-permute-done.41 = bf16[2,24,1152]{2,1,0:T(8,128)(2,1)S(1)} collective-permute-done((bf16[2,24,1152]{2,1,0:T(8,128)(2,1)S(1)}, bf16[2,24,1152]{2,1,0:T(8,128)(2,1)S(1)}, u32[]{:S(2)}, u32[]{:S(2)}) %collective-permute-start.41) | collective-permute-done | bytes 110624 | tf_op jit(solution)/shard_map/ppermute | solution.py:31
  325.6 1.9 collective-permute-start.42
  327.5 1.8 fusion.78
  (157 shorter events, 59.8 us)
Async XLA Ops:
  2.1 0.6 copy-start.9
  4.1 108.6 %collective-permute-start.32 = (bf16[384,1152]{1,0:T(8,128)(2,1)S(1)}, bf16[384,1152]{1,0:T(8,128)(2,1)}, u32[]{:S(2)}, u32[]{:S(2)}) collective-permute-start(bf16[384,1152]{1,0:T(8,128)(2,1)S(1)} %fusion.98), channel_id=1, source_target_pairs={{0,504},{16,464},{1,505},{17,465},{2,506},{18,466},{3,507},{19,467... | collective-permute-start | bytes 2654216 | tf_op jit(solution)/shard_map/ppermute | solution.py:21
  6.4 50.3 %copy-start.13 = (s32[384]{0:T(512)S(1)}, s32[384]{0:T(512)}, u32[]{:S(2)}) copy-start(s32[384]{0:T(512)} %param.21) | copy-start | bytes 4612
  7.3 0.7 collective-permute-start
  8.8 23.3 %collective-permute-start.1 = (bf16[2,24,1152]{2,1,0:T(8,128)(2,1)S(1)}, bf16[2,24,1152]{2,1,0:T(8,128)(2,1)S(1)}, u32[]{:S(2)}, u32[]{:S(2)}) collective-permute-start(bf16[2,24,1152]{2,1,0:T(8,128)(2,1)S(1)} %pad_maximum_fusion.2), channel_id=1, source_target_pairs={{32,34},{33,35},{34,32},{35,33},{36,38},{37,39},{38,36},{39,37},{4... | collective-permute-start | bytes 331784 | tf_op jit(solution)/shard_map/cond/branch_1_fun/ppermute | solution.py:107
  9.5 31.8 %collective-permute-start.5 = (bf16[384,1152]{1,0:T(8,128)(2,1)S(1)}, bf16[384,1152]{1,0:T(8,128)(2,1)}, u32[]{:S(2)}, u32[]{:S(2)}) collective-permute-start(bf16[384,1152]{1,0:T(8,128)(2,1)S(1)} %get-tuple-element.132), channel_id=1, source_target_pairs={{8,0},{16,8},{24,16},{32,24},{40,32},{48,40},{56,48},{9,1},{17,9},... | collective-permute-start | bytes 2654216 | tf_op jit(solution)/shard_map/cond/branch_1_fun/ppermute | solution.py:21
  32.1 3.6 %collective-permute-start.2 = (bf16[2,24,1152]{2,1,0:T(8,128)(2,1)S(1)}, bf16[2,24,1152]{2,1,0:T(8,128)(2,1)S(1)}, u32[]{:S(2)}, u32[]{:S(2)}) collective-permute-start(bf16[2,24,1152]{2,1,0:T(8,128)(2,1)S(1)} %get-tuple-element.248), channel_id=1, source_target_pairs={{32,36},{33,37},{34,38},{35,39},{36,96},{37,97},{38,98},{39,99},{4... | collective-permute-start | bytes 331784 | tf_op jit(solution)/shard_map/cond/branch_1_fun/ppermute | solution.py:107
  32.8 11.3 %collective-permute-start.4 = (bf16[384,1152]{1,0:T(8,128)(2,1)S(1)}, bf16[384,1152]{1,0:T(8,128)(2,1)}, u32[]{:S(2)}, u32[]{:S(2)}) collective-permute-start(bf16[384,1152]{1,0:T(8,128)(2,1)S(1)} %get-tuple-element.132), channel_id=1, source_target_pairs={{8,48},{9,49},{10,50},{11,51},{12,52},{13,53},{14,54},{15,55},{72,... | collective-permute-start | bytes 2654216 | tf_op jit(solution)/shard_map/cond/branch_1_fun/ppermute | solution.py:21
  35.0 8.1 %collective-permute-start.3 = (bf16[2,24,1152]{2,1,0:T(8,128)(2,1)S(1)}, bf16[2,24,1152]{2,1,0:T(8,128)(2,1)S(1)}, u32[]{:S(2)}, u32[]{:S(2)}) collective-permute-start(bf16[2,24,1152]{2,1,0:T(8,128)(2,1)S(1)} %get-tuple-element.247), channel_id=1, source_target_pairs={{32,100},{33,101},{34,102},{35,103},{36,32},{37,33},{38,34},{39,35... | collective-permute-start | bytes 331784 | tf_op jit(solution)/shard_map/cond/branch_1_fun/ppermute | solution.py:107
  41.2 14.7 %collective-permute-start.6 = (bf16[384,1152]{1,0:T(8,128)(2,1)}, bf16[384,1152]{1,0:T(8,128)(2,1)}, u32[]{:S(2)}, u32[]{:S(2)}) collective-permute-start(bf16[384,1152]{1,0:T(8,128)(2,1)} %collective-permute-done.5), channel_id=1, source_target_pairs={{8,0},{16,8},{24,16},{32,24},{40,32},{48,40},{56,48},{9,1},{17,9},... | collective-permute-start | bytes 2654216 | tf_op jit(solution)/shard_map/cond/branch_1_fun/ppermute | solution.py:21
  55.9 56.8 %collective-permute-start.33 = (bf16[384,1152]{1,0:T(8,128)(2,1)}, bf16[384,1152]{1,0:T(8,128)(2,1)S(1)}, u32[]{:S(2)}, u32[]{:S(2)}) collective-permute-start(bf16[384,1152]{1,0:T(8,128)(2,1)} %get-tuple-element.213), channel_id=1, source_target_pairs={{48,496},{49,497},{50,498},{51,499},{52,500},{53,501},{54,502},{55... | collective-permute-start | bytes 2654216 | tf_op jit(solution)/shard_map/ppermute | solution.py:21
  57.3 3.4 %collective-permute-start.14 = (bf16[8,24,1152]{2,1,0:T(8,128)(2,1)S(1)}, bf16[8,24,1152]{2,1,0:T(8,128)(2,1)S(1)}, u32[]{:S(2)}, u32[]{:S(2)}) collective-permute-start(bf16[8,24,1152]{2,1,0:T(8,128)(2,1)S(1)} %get-tuple-element.135), channel_id=1, source_target_pairs={{32,16},{33,17},{34,18},{35,19},{36,20},{37,21},{38,22},{39,23},{4... | collective-permute-start | bytes 1327112 | tf_op jit(solution)/shard_map/cond/branch_1_fun/ppermute | solution.py:107
  58.0 15.2 %collective-permute-start.15 = (bf16[8,24,1152]{2,1,0:T(8,128)(2,1)S(1)}, bf16[8,24,1152]{2,1,0:T(8,128)(2,1)S(1)}, u32[]{:S(2)}, u32[]{:S(2)}) collective-permute-start(bf16[8,24,1152]{2,1,0:T(8,128)(2,1)S(1)} %get-tuple-element.135), channel_id=1, source_target_pairs={{32,0},{33,1},{34,2},{35,3},{36,4},{37,5},{38,6},{39,7},{40,8},{41... | collective-permute-start | bytes 1327112 | tf_op jit(solution)/shard_map/cond/branch_1_fun/ppermute | solution.py:107
  59.3 14.6 %collective-permute-start.16 = (bf16[8,24,1152]{2,1,0:T(8,128)(2,1)S(1)}, bf16[8,24,1152]{2,1,0:T(8,128)(2,1)}, u32[]{:S(2)}, u32[]{:S(2)}) collective-permute-start(bf16[8,24,1152]{2,1,0:T(8,128)(2,1)S(1)} %get-tuple-element.135), channel_id=1, source_target_pairs={{32,48},{33,49},{34,50},{35,51},{36,52},{37,53},{38,54},{39,55},{4... | collective-permute-start | bytes 1327112 | tf_op jit(solution)/shard_map/cond/branch_1_fun/ppermute | solution.py:107
  60.7 12.4 %copy-start.7 = (bf16[8,24,1152]{2,1,0:T(8,128)(2,1)}, bf16[8,24,1152]{2,1,0:T(8,128)(2,1)S(1)}, u32[]{:S(2)}) copy-start(bf16[8,24,1152]{2,1,0:T(8,128)(2,1)S(1)} %collective-permute-done.14) | copy-start | bytes 1327108 | tf_op jit(solution)/shard_map/cond
  73.2 0.8 copy-start.8
  76.1 24.9 %collective-permute-start.17 = (bf16[8,24,1152]{2,1,0:T(8,128)(2,1)}, bf16[8,24,1152]{2,1,0:T(8,128)(2,1)}, u32[]{:S(2)}, u32[]{:S(2)}) collective-permute-start(bf16[8,24,1152]{2,1,0:T(8,128)(2,1)} %get-tuple-element.240), channel_id=1, source_target_pairs={{0,128},{1,129},{2,130},{3,131},{4,132},{5,133},{6,134},{7,135},{8... | collective-permute-start | bytes 1327112 | tf_op jit(solution)/shard_map/cond/branch_1_fun/ppermute | solution.py:31
  78.8 23.2 %collective-permute-start.18 = (bf16[8,24,1152]{2,1,0:T(8,128)(2,1)}, bf16[8,24,1152]{2,1,0:T(8,128)(2,1)S(1)}, u32[]{:S(2)}, u32[]{:S(2)}) collective-permute-start(bf16[8,24,1152]{2,1,0:T(8,128)(2,1)} %get-tuple-element.240), channel_id=1, source_target_pairs={{0,256},{1,257},{2,258},{3,259},{4,260},{5,261},{6,262},{7,263},{8... | collective-permute-start | bytes 1327112 | tf_op jit(solution)/shard_map/cond/branch_1_fun/ppermute | solution.py:31
  82.9 20.2 %collective-permute-start.19 = (bf16[8,24,1152]{2,1,0:T(8,128)(2,1)}, bf16[8,24,1152]{2,1,0:T(8,128)(2,1)S(1)}, u32[]{:S(2)}, u32[]{:S(2)}) collective-permute-start(bf16[8,24,1152]{2,1,0:T(8,128)(2,1)} %get-tuple-element.240), channel_id=1, source_target_pairs={{0,384},{1,385},{2,386},{3,387},{4,388},{5,389},{6,390},{7,391},{8... | collective-permute-start | bytes 1327112 | tf_op jit(solution)/shard_map/cond/branch_1_fun/ppermute | solution.py:31
  103.2 5.5 %collective-permute-start.20 = (bf16[8,72,1152]{2,1,0:T(8,128)(2,1)S(1)}, bf16[8,72,1152]{2,1,0:T(8,128)(2,1)}, u32[]{:S(2)}, u32[]{:S(2)}) collective-permute-start(bf16[8,72,1152]{2,1,0:T(8,128)(2,1)S(1)} %constant_dynamic-update-slice_fusion.2), channel_id=1, source_target_pairs={{0,8},{1,9},{2,10},{3,11},{4,12},{5,13},{6,14},{7,15},{8,0},{9,1},... | collective-permute-start | bytes 3981320 | tf_op jit(solution)/shard_map/cond/branch_1_fun/ppermute | solution.py:31
  112.7 6.4 %copy-start.3 = (bf16[384,1152]{1,0:T(8,128)(2,1)}, bf16[384,1152]{1,0:T(8,128)(2,1)S(1)}, u32[]{:S(2)}) copy-start(bf16[384,1152]{1,0:T(8,128)(2,1)S(1)} %collective-permute-done.33) | copy-start | bytes 2654212
  116.6 1.5 copy-start.11
  119.1 16.2 %collective-permute-start.22 = (bf16[384,1152]{1,0:T(8,128)(2,1)}, bf16[384,1152]{1,0:T(8,128)(2,1)}, u32[]{:S(2)}, u32[]{:S(2)}) collective-permute-start(bf16[384,1152]{1,0:T(8,128)(2,1)} %get-tuple-element.146), channel_id=1, source_target_pairs={{16,56},{56,40},{17,57},{57,41},{18,58},{58,42},{19,59},{59,43},{2... | collective-permute-start | bytes 2654216 | tf_op jit(solution)/shard_map/cond/branch_1_fun/ppermute | solution.py:21
  121.7 13.5 %collective-permute-start.21 = (bf16[384,1152]{1,0:T(8,128)(2,1)}, bf16[384,1152]{1,0:T(8,128)(2,1)}, u32[]{:S(2)}, u32[]{:S(2)}) collective-permute-start(bf16[384,1152]{1,0:T(8,128)(2,1)} %broadcast_select_fusion.8), channel_id=1, source_target_pairs={{56,48},{48,56},{57,49},{49,57},{58,50},{50,58},{59,51},{51,59},{6... | collective-permute-start | bytes 2654216 | tf_op jit(solution)/shard_map/cond/branch_1_fun/ppermute | solution.py:21
  123.3 27.8 %collective-permute-start.23 = (bf16[392,1152]{1,0:T(8,128)(2,1)}, bf16[392,1152]{1,0:T(8,128)(2,1)}, u32[]{:S(2)}, u32[]{:S(2)}) collective-permute-start(bf16[392,1152]{1,0:T(8,128)(2,1)} %get-tuple-element.149), channel_id=1, source_target_pairs={{48,8},{49,9},{50,10},{51,11},{52,12},{53,13},{54,14},{55,15},{112... | collective-permute-start | bytes 2709512 | tf_op jit(solution)/shard_map/cond/branch_1_fun/ppermute | solution.py:21
  124.6 26.5 %collective-permute-start.24 = (bf16[384,1152]{1,0:T(8,128)(2,1)}, bf16[384,1152]{1,0:T(8,128)(2,1)}, u32[]{:S(2)}, u32[]{:S(2)}) collective-permute-start(bf16[384,1152]{1,0:T(8,128)(2,1)} %get-tuple-element.150), channel_id=1, source_target_pairs={{8,0},{16,8},{24,16},{32,24},{40,32},{48,40},{56,48},{9,1},{17,9},... | collective-permute-start | bytes 2654216 | tf_op jit(solution)/shard_map/cond/branch_1_fun/ppermute | solution.py:21
  129.5 0.7 copy-start.14
  151.2 86.0 %collective-permute-start.34 = (bf16[392,1152]{1,0:T(8,128)(2,1)}, bf16[392,1152]{1,0:T(8,128)(2,1)}, u32[]{:S(2)}, u32[]{:S(2)}) collective-permute-start(bf16[392,1152]{1,0:T(8,128)(2,1)} %pad_maximum_fusion.4), channel_id=1, source_target_pairs={{56,64},{40,104},{57,65},{41,105},{58,66},{42,106},{59,67},{43,107... | collective-permute-start | bytes 2709512 | tf_op jit(solution)/shard_map/ppermute | solution.py:21
  152.8 85.1 %collective-permute-start.35 = (bf16[392,1152]{1,0:T(8,128)(2,1)}, bf16[392,1152]{1,0:T(8,128)(2,1)}, u32[]{:S(2)}, u32[]{:S(2)}) collective-permute-start(bf16[392,1152]{1,0:T(8,128)(2,1)} %get-tuple-element.225), channel_id=1, source_target_pairs={{8,72},{9,73},{10,74},{11,75},{12,76},{13,77},{14,78},{15,79},{72,... | collective-permute-start | bytes 2709512 | tf_op jit(solution)/shard_map/ppermute | solution.py:21
  164.4 4.0 %copy-start.2 = (f32[384,1152]{1,0:T(8,128)}, f32[384,1152]{1,0:T(8,128)S(1)}, u32[]{:S(2)}) copy-start(f32[384,1152]{1,0:T(8,128)S(1)} %get-tuple-element.151) | copy-start | bytes 5308420 | tf_op jit(solution)/shard_map/cond
  168.4 1.3 copy-start.15
  169.7 2.2 copy-start.12
  174.4 2.5 copy-start.1
  174.4 2.5 copy-start.16
  178.8 1.5 copy-start.4
  180.4 5.1 %collective-permute-start.25 = (bf16[8,72,1152]{2,1,0:T(8,128)(2,1)S(1)}, bf16[8,72,1152]{2,1,0:T(8,128)(2,1)}, u32[]{:S(2)}, u32[]{:S(2)}) collective-permute-start(bf16[8,72,1152]{2,1,0:T(8,128)(2,1)S(1)} %dynamic-slice_bitcast_fusion.1), channel_id=1, source_target_pairs={{0,8},{1,9},{2,10},{3,11},{4,12},{5,13},{6,14},{7,15},{8,0},{9,1},... | collective-permute-start | bytes 3981320 | tf_op jit(solution)/shard_map/cond/branch_1_fun/ppermute | solution.py:31
  188.5 24.2 %collective-permute-start.28 = (bf16[8,24,1152]{2,1,0:T(8,128)(2,1)}, bf16[8,24,1152]{2,1,0:T(8,128)(2,1)}, u32[]{:S(2)}, u32[]{:S(2)}) collective-permute-start(bf16[8,24,1152]{2,1,0:T(8,128)(2,1)} %get-tuple-element.254), channel_id=1, source_target_pairs={{0,384},{1,385},{2,386},{3,387},{4,388},{5,389},{6,390},{7,391},{8... | collective-permute-start | bytes 1327112 | tf_op jit(solution)/shard_map/cond/branch_1_fun/ppermute | solution.py:31
  193.6 19.1 %collective-permute-start.27 = (bf16[8,24,1152]{2,1,0:T(8,128)(2,1)}, bf16[8,24,1152]{2,1,0:T(8,128)(2,1)}, u32[]{:S(2)}, u32[]{:S(2)}) collective-permute-start(bf16[8,24,1152]{2,1,0:T(8,128)(2,1)} %get-tuple-element.255), channel_id=1, source_target_pairs={{0,256},{1,257},{2,258},{3,259},{4,260},{5,261},{6,262},{7,263},{8... | collective-permute-start | bytes 1327112 | tf_op jit(solution)/shard_map/cond/branch_1_fun/ppermute | solution.py:31
  196.5 22.4 %collective-permute-start.26 = (bf16[8,24,1152]{2,1,0:T(8,128)(2,1)}, bf16[8,24,1152]{2,1,0:T(8,128)(2,1)}, u32[]{:S(2)}, u32[]{:S(2)}) collective-permute-start(bf16[8,24,1152]{2,1,0:T(8,128)(2,1)} %get-tuple-element.253), channel_id=1, source_target_pairs={{0,128},{1,129},{2,130},{3,131},{4,132},{5,133},{6,134},{7,135},{8... | collective-permute-start | bytes 1327112 | tf_op jit(solution)/shard_map/cond/branch_1_fun/ppermute | solution.py:31
  222.5 7.3 %collective-permute-start.31 = (bf16[8,24,384]{2,1,0:T(8,128)(2,1)S(1)}, bf16[8,24,384]{2,1,0:T(8,128)(2,1)S(1)}, u32[]{:S(2)}, u32[]{:S(2)}) collective-permute-start(bf16[8,24,384]{2,1,0:T(8,128)(2,1)S(1)} %get-tuple-element.257), channel_id=1, source_target_pairs={{0,48},{1,49},{2,50},{3,51},{4,52},{5,53},{6,54},{7,55},{8,56},{9,... | collective-permute-start | bytes 442376 | tf_op jit(solution)/shard_map/cond/branch_1_fun/ppermute | solution.py:31
  224.4 8.3 %collective-permute-start.30 = (bf16[8,24,384]{2,1,0:T(8,128)(2,1)S(1)}, bf16[8,24,384]{2,1,0:T(8,128)(2,1)S(1)}, u32[]{:S(2)}, u32[]{:S(2)}) collective-permute-start(bf16[8,24,384]{2,1,0:T(8,128)(2,1)S(1)} %get-tuple-element.258), channel_id=1, source_target_pairs={{0,32},{1,33},{2,34},{3,35},{4,36},{5,37},{6,38},{7,39},{8,40},{9,... | collective-permute-start | bytes 442376 | tf_op jit(solution)/shard_map/cond/branch_1_fun/ppermute | solution.py:31
  226.4 9.6 %collective-permute-start.29 = (bf16[8,24,384]{2,1,0:T(8,128)(2,1)S(1)}, bf16[8,24,384]{2,1,0:T(8,128)(2,1)S(1)}, u32[]{:S(2)}, u32[]{:S(2)}) collective-permute-start(bf16[8,24,384]{2,1,0:T(8,128)(2,1)S(1)} %get-tuple-element.256), channel_id=1, source_target_pairs={{0,16},{1,17},{2,18},{3,19},{4,20},{5,21},{6,22},{7,23},{8,24},{9,... | collective-permute-start | bytes 442376 | tf_op jit(solution)/shard_map/cond/branch_1_fun/ppermute | solution.py:31
  237.2 0.7 copy-start.5
  237.9 29.3 %collective-permute-start.36 = (bf16[392,1152]{1,0:T(8,128)(2,1)}, bf16[392,1152]{1,0:T(8,128)(2,1)S(1)}, u32[]{:S(2)}, u32[]{:S(2)}) collective-permute-start(bf16[392,1152]{1,0:T(8,128)(2,1)} %pad_maximum_fusion.4), channel_id=1, source_target_pairs={{0,8},{8,16},{16,24},{24,32},{32,40},{40,48},{48,56},{1,9},{9,17},... | collective-permute-start | bytes 2709512 | tf_op jit(solution)/shard_map/ppermute | solution.py:21
  240.6 5.6 %copy-start.6 = (f32[8,24,384]{2,1,0:T(8,128)S(1)}, f32[8,24,384]{2,1,0:T(8,128)}, u32[]{:S(2)}) copy-start(f32[8,24,384]{2,1,0:T(8,128)} %get-tuple-element.171) | copy-start | bytes 884740 | tf_op jit(solution)/shard_map/cond
  242.0 25.2 %collective-permute-start.9 = (bf16[392,1152]{1,0:T(8,128)(2,1)S(1)}, bf16[392,1152]{1,0:T(8,128)(2,1)}, u32[]{:S(2)}, u32[]{:S(2)}) collective-permute-start(bf16[392,1152]{1,0:T(8,128)(2,1)S(1)} %broadcast_select_fusion.15), channel_id=1, source_target_pairs={{0,8},{8,0},{1,9},{9,1},{2,10},{10,2},{3,11},{11,3},{4,12},{12,4},... | collective-permute-start | bytes 2709512 | tf_op jit(solution)/shard_map/cond/branch_1_fun/ppermute | solution.py:21
  244.6 22.5 %collective-permute-start.10 = (bf16[392,1152]{1,0:T(8,128)(2,1)}, bf16[392,1152]{1,0:T(8,128)(2,1)}, u32[]{:S(2)}, u32[]{:S(2)}) collective-permute-start(bf16[392,1152]{1,0:T(8,128)(2,1)} %get-tuple-element.174), channel_id=1, source_target_pairs={{40,0},{0,16},{41,1},{1,17},{42,2},{2,18},{43,3},{3,19},{44,4},{4,... | collective-permute-start | bytes 2709512 | tf_op jit(solution)/shard_map/cond/branch_1_fun/ppermute | solution.py:21
  246.2 9.0 %collective-permute-start.7 = (bf16[4,24,384]{2,1,0:T(8,128)(2,1)S(1)}, bf16[4,24,384]{2,1,0:T(8,128)(2,1)S(1)}, u32[]{:S(2)}, u32[]{:S(2)}) collective-permute-start(bf16[4,24,384]{2,1,0:T(8,128)(2,1)S(1)} %fusion.36), channel_id=1, source_target_pairs={{0,4},{1,5},{2,6},{3,7},{4,0},{5,1},{6,2},{7,3},{8,12},{9,13},{10,... | collective-permute-start | bytes 221192 | tf_op jit(solution)/shard_map/cond/branch_1_fun/ppermute | solution.py:31
  255.3 11.8 %collective-permute-start.8 = (bf16[2,24,384]{2,1,0:T(8,128)(2,1)S(1)}, bf16[2,24,384]{2,1,0:T(8,128)(2,1)S(1)}, u32[]{:S(2)}, u32[]{:S(2)}) collective-permute-start(bf16[2,24,384]{2,1,0:T(8,128)(2,1)S(1)} %fusion.37), channel_id=1, source_target_pairs={{0,2},{1,3},{2,0},{3,1},{4,6},{5,7},{6,4},{7,5},{8,10},{9,11},{10,... | collective-permute-start | bytes 110600 | tf_op jit(solution)/shard_map/cond/branch_1_fun/ppermute | solution.py:31
  267.2 22.3 %collective-permute-start.13 = (bf16[392,1152]{1,0:T(8,128)(2,1)S(1)}, bf16[392,1152]{1,0:T(8,128)(2,1)}, u32[]{:S(2)}, u32[]{:S(2)}) collective-permute-start(bf16[392,1152]{1,0:T(8,128)(2,1)S(1)} %get-tuple-element.178), channel_id=1, source_target_pairs={{0,8},{8,16},{16,24},{24,32},{32,40},{40,48},{48,56},{1,9},{9,17},... | collective-permute-start | bytes 2709512 | tf_op jit(solution)/shard_map/cond/branch_1_fun/ppermute | solution.py:21
  269.2 6.9 %collective-permute-start.11 = (bf16[1,24,384]{2,1,0:T(8,128)(2,1)S(1)}, bf16[1,24,384]{2,1,0:T(8,128)(2,1)S(1)}, u32[]{:S(2)}, u32[]{:S(2)}) collective-permute-start(bf16[1,24,384]{2,1,0:T(8,128)(2,1)S(1)} %dynamic-slice_convert_fusion.8), channel_id=1, source_target_pairs={{0,1},{1,0},{2,3},{3,2},{4,5},{5,4},{6,7},{7,6},{8,9},{9,8},{10,11... | collective-permute-start | bytes 55304 | tf_op jit(solution)/shard_map/cond/branch_1_fun/ppermute | solution.py:31
  276.0 13.4 %collective-permute-start.12 = (f32[24,384]{1,0:T(8,128)S(1)}, f32[24,384]{1,0:T(8,128)S(1)}, u32[]{:S(2)}, u32[]{:S(2)}) collective-permute-start(f32[24,384]{1,0:T(8,128)S(1)} %add_bitcast_fusion), channel_id=1, source_target_pairs={{0,64},{1,65},{2,66},{3,67},{4,68},{5,69},{6,70},{7,71},{8,72},{9,... | collective-permute-start | bytes 110600 | tf_op jit(solution)/shard_map/cond/branch_1_fun/ppermute | solution.py:31
  290.2 40.1 %collective-permute-start.37 = (bf16[392,1152]{1,0:T(8,128)(2,1)}, bf16[392,1152]{1,0:T(8,128)(2,1)S(1)}, u32[]{:S(2)}, u32[]{:S(2)}) collective-permute-start(bf16[392,1152]{1,0:T(8,128)(2,1)} %get-tuple-element.236), channel_id=1, source_target_pairs={{0,8},{8,16},{16,24},{24,32},{32,40},{40,48},{48,56},{1,9},{9,17},... | collective-permute-start | bytes 2709512 | tf_op jit(solution)/shard_map/ppermute | solution.py:21
  296.8 9.5 %collective-permute-start.38 = (bf16[1,24,384]{2,1,0:T(8,128)(2,1)S(1)}, bf16[1,24,384]{2,1,0:T(8,128)(2,1)S(1)}, u32[]{:S(2)}, u32[]{:S(2)}) collective-permute-start(bf16[1,24,384]{2,1,0:T(8,128)(2,1)S(1)} %bitcast.139), channel_id=1, source_target_pairs={{0,16},{1,17},{2,18},{3,19},{4,20},{5,21},{6,22},{7,23},{8,24},{9,... | collective-permute-start | bytes 55304 | tf_op jit(solution)/shard_map/ppermute | solution.py:31
  306.3 7.2 %collective-permute-start.39 = (bf16[2,24,384]{2,1,0:T(8,128)(2,1)S(1)}, bf16[2,24,384]{2,1,0:T(8,128)(2,1)S(1)}, u32[]{:S(2)}, u32[]{:S(2)}) collective-permute-start(bf16[2,24,384]{2,1,0:T(8,128)(2,1)S(1)} %pad_maximum_fusion.7), channel_id=1, source_target_pairs={{0,32},{1,33},{2,34},{3,35},{4,36},{5,37},{6,38},{7,39},{8,40},{9,... | collective-permute-start | bytes 110600 | tf_op jit(solution)/shard_map/ppermute | solution.py:31
  313.5 4.9 %collective-permute-start.40 = (bf16[1,24,1152]{2,1,0:T(8,128)(2,1)S(1)}, bf16[1,24,1152]{2,1,0:T(8,128)(2,1)S(1)}, u32[]{:S(2)}, u32[]{:S(2)}) collective-permute-start(bf16[1,24,1152]{2,1,0:T(8,128)(2,1)S(1)} %maximum_bitcast_fusion), channel_id=1, source_target_pairs={{0,128},{1,129},{2,130},{3,131},{4,132},{5,133},{6,134},{7,135},{8... | collective-permute-start | bytes 165896 | tf_op jit(solution)/shard_map/ppermute | solution.py:31
  318.5 7.0 %collective-permute-start.41 = (bf16[2,24,1152]{2,1,0:T(8,128)(2,1)S(1)}, bf16[2,24,1152]{2,1,0:T(8,128)(2,1)S(1)}, u32[]{:S(2)}, u32[]{:S(2)}) collective-permute-start(bf16[2,24,1152]{2,1,0:T(8,128)(2,1)S(1)} %pad_maximum_fusion.6), channel_id=1, source_target_pairs={{0,256},{1,257},{2,258},{3,259},{4,260},{5,261},{6,262},{7,263},{8... | collective-permute-start | bytes 331784 | tf_op jit(solution)/shard_map/ppermute | solution.py:31
  325.6 3.7 %collective-permute-start.42 = (bf16[72,1152]{1,0:T(8,128)(2,1)S(1)}, bf16[72,1152]{1,0:T(8,128)(2,1)S(1)}, u32[]{:S(2)}, u32[]{:S(2)}) collective-permute-start(bf16[72,1152]{1,0:T(8,128)(2,1)S(1)} %pad_maximum_fusion.5), channel_id=1, source_target_pairs={{0,8},{1,9},{2,10},{3,11},{4,12},{5,13},{6,14},{7,15},{8,0},{9,1},... | collective-permute-start | bytes 497672 | tf_op jit(solution)/shard_map/ppermute | solution.py:31
  334.4 1.2 copy-start
  334.4 1.2 copy-start.10

commit v5 on v3

--- a/solution.py
+++ b/solution.py
@@ -184,10 +184,9 @@
     def meet_texts(far, far_1):
         swapped = chain(jnp.where(last, far, far_1), [(7, 0, 6), (6, 0, 7)])
         passed = chain(far, [(2, 0, 7), (7, 0, 5)])
-        back_0 = chain(parcel, [(6, 0, 1)])
-        beside_1 = chain(parcel, up)
+        swapped, passed = lax.optimization_barrier((swapped, passed))
         img_grad = met_grad(unit_txt, 0) + met_grad(jnp.where(last, far, near_1), 1)
-        return img_grad, swapped, passed, back_0, beside_1
+        return img_grad, swapped, passed
 
     def head_terms(img_grad, swapped, passed):
         text_3 = jnp.where(slot >= GROUP - 3, passed, near_3)
@@ -217,29 +216,19 @@
         total = total.reshape(window, window_y)
         return (total + hi_flip(total)).astype(bf16)
 
-    img_grad, swapped, passed, back_0, beside_1 = one_step(meet_texts, far, far_1)
-    parcel_far, img_grad = lax.optimization_barrier((parcel, img_grad))
-    back = chain(parcel_far, [(7, 1, 0), (5, 1, 5)])
-    back_1 = chain(back_0, [(1, 1, 1)])
-
-    total = one_step(lambda *blocks: sum_xy(head_terms(*blocks)), img_grad, swapped, passed)
-    total, back, back_1 = lax.optimization_barrier((total, back, back_1))
-
-    def sum_z_and_chain(total, back, back_1):
-        beside_2 = chain(beside_1, up)
-        swapped = chain(jnp.where(first, back, back_1), [(0, 0, 1), (1, 0, 0)])
-        passed = chain(back, [(5, 0, 0), (0, 0, 2)])
-        return sum_z(total), swapped, passed, beside_2, chain(beside_2, up)
-
-    total_z, swapped, passed, beside_2, beside_3 = one_step(sum_z_and_chain, total, back, back_1)
-    parcel, total_z = lax.optimization_barrier((parcel, total_z))
-    image_3 = jnp.where(slot <= 2, passed, beside_3)
-    images = [
-        parcel,
-        jnp.where(first, back, beside_1),
-        jnp.where(slot <= 1, swapped, beside_2),
-        jnp.where(slot == 1, back_1, image_3),
-    ]
+    back = chain(parcel, [(7, 1, 7), (5, 1, 5), (6, 0, 0)])
+    total = one_step(lambda *blocks: head_terms(*meet_texts(*blocks)), far, far_1)
+    total, back, parcel = lax.optimization_barrier((total, back, parcel))
+    back_2 = chain(back, [(0, 1, 0), (5, 0, 7)])
+    image_1 = chain(jnp.where(last, back, parcel), up + [(7, 0, 0)])
+    total = one_step(sum_xy, total)
+    total, back_2, image_1 = lax.optimization_barrier((total, back_2, image_1))
+    come_2 = chain(jnp.where(last, back_2, image_1), up + [(7, 0, 0)])
+    total_z = one_step(sum_z, total)
+    total_z, come_2, parcel = lax.optimization_barrier((total_z, come_2, parcel))
+    image_2 = jnp.where(first, back_2, come_2)
+    come_3 = chain(image_2, up)
+    images = [parcel, image_1, image_2, jnp.where(first, come_2, come_3)]
 
     strips = total_z[None]
     for bit in (1, 2):

time: 334 us -> 324 us (0.970)
  waiting for transfers between devices: 102 us -> 95.5 us
  starting transfers between devices: 157 us -> 152 us
  local copies, waits for them, and re-layouts: 9.51 us -> 13.2 us
    ppermute x16 -> x13, starting transfers between devices: 50.5 us -> 33.8 us  [along_chain(): return lax.ppermute(block, AXES, route)]
    ppermute x24, starting transfers between devices: 107 us -> 118 us  [by_coords(): return lax.ppermute(block, AXES, route)]
    ppermute x24, waiting for transfers between devices: 76.8 us -> 73.2 us  [by_coords(): return lax.ppermute(block, AXES, route)]
    ppermute x16 -> x13, waiting for transfers between devices: 25.2 us -> 22.3 us  [along_chain(): return lax.ppermute(block, AXES, route)]
  transfers between devices with their start and end apart: 40 -> 37, of which waited for: 23 -> 22; matrix products, arithmetic and copies ran while one was open for 13% -> 16% of each run, Pallas kernels for 0% -> 0%
where the time goes in v5:
time: 324 us; the launch traced here: 322 us
  starting transfers between devices  152 us (47%)
  waiting for transfers between devices  95.5 us (29%)
  matrix products  31.2 us (10%)
  other arithmetic  26.4 us (8%)
  local copies, waits for them, and re-layouts  13.2 us (4%)
    ppermute x24, starting transfers between devices, by_coords(): return lax.ppermute(block, AXES, route)  118 us
    ppermute x24, waiting for transfers between devices, by_coords(): return lax.ppermute(block, AXES, route)  73.2 us
    ppermute x13, starting transfers between devices, along_chain(): return lax.ppermute(block, AXES, route)  33.8 us
    ppermute x13, waiting for transfers between devices, along_chain(): return lax.ppermute(block, AXES, route)  22.3 us
    dot_general x4, matrix products, met_grad(): logits = jnp.einsum('ie,je->ij', unit_img, text, preferred_element_type=f32)  9.87 us
  transfers between devices with their start and end apart: 37, of which 22 were waited for; matrix products, arithmetic and copies ran while one was open for 16% of the time, Pallas kernels for 0%

profile of v5, /device:TPU:1, one launch (start us, length us, event | category | flops | bytes accessed | tf_op | source)
XLA Modules:
  0.0 321.8 jit_solution(13404666643392388101)
XLA Ops:
  4.3 48.3 %conditional.5 = (bf16[8,24,1152]{2,1,0:T(8,128)(2,1)S(1)}, bf16[384,1152]{1,0:T(8,128)(2,1)}, bf16[384,1152]{1,0:T(8,128)(2,1)}) conditional(s32[]{:T(128)} %convert_element_type.171, () %tuple.59, (s32[]{:T(128)}, s32[]{:T(128)}, s32[]{:T(128)}, bf16[144,1152]{1,0:T(8,128)(2,1)}, bf16[384,1152]{1,0:T(8,128)(2,1)S(1)}) %tuple.60), branch_computations={%region_1.2_spmd, %region_2.3_spmd} | conditional | flops 829500 | bytes 11834224 | solution.py:94
  5.1 4.4 %collective-permute-start = (bf16[1,24,1152]{2,1,0:T(8,128)(2,1)S(1)}, bf16[1,24,1152]{2,1,0:T(8,128)(2,1)S(1)}, u32[]{:S(2)}, u32[]{:S(2)}) collective-permute-start(bf16[1,24,1152]{2,1,0:T(8,128)(2,1)S(1)} %dynamic-slice_bitcast_fusion), channel_id=1, source_target_pairs={{0,1},{1,0},{2,3},{3,2},{4,5},{5,4},{6,7},{7,6},{8,9},{9,8},{10,11... | collective-permute-start | bytes 165896 | tf_op jit(solution)/shard_map/cond/branch_1_fun/ppermute | solution.py:31
  11.9 4.9 %collective-permute-start.1 = (bf16[2,24,1152]{2,1,0:T(8,128)(2,1)S(1)}, bf16[2,24,1152]{2,1,0:T(8,128)(2,1)S(1)}, u32[]{:S(2)}, u32[]{:S(2)}) collective-permute-start(bf16[2,24,1152]{2,1,0:T(8,128)(2,1)S(1)} %pad_maximum_fusion.2), channel_id=1, source_target_pairs={{0,2},{1,3},{2,0},{3,1},{4,6},{5,7},{6,4},{7,5},{8,10},{9,11},{10,... | collective-permute-start | bytes 331784 | tf_op jit(solution)/shard_map/cond/branch_1_fun/ppermute | solution.py:31
  16.8 2.1 collective-permute-done.1
  19.0 8.8 %collective-permute-start.2 = (bf16[2,24,1152]{2,1,0:T(8,128)(2,1)S(1)}, bf16[2,24,1152]{2,1,0:T(8,128)(2,1)S(1)}, u32[]{:S(2)}, u32[]{:S(2)}) collective-permute-start(bf16[2,24,1152]{2,1,0:T(8,128)(2,1)S(1)} %get-tuple-element.186), channel_id=1, source_target_pairs={{0,4},{1,5},{2,6},{3,7},{4,64},{5,65},{6,66},{7,67},{8,12},{9,13},... | collective-permute-start | bytes 331784 | tf_op jit(solution)/shard_map/cond/branch_1_fun/ppermute | solution.py:31
  27.8 10.0 %collective-permute-start.4 = (bf16[384,1152]{1,0:T(8,128)(2,1)S(1)}, bf16[384,1152]{1,0:T(8,128)(2,1)}, u32[]{:S(2)}, u32[]{:S(2)}) collective-permute-start(bf16[384,1152]{1,0:T(8,128)(2,1)S(1)} %get-tuple-element.100), channel_id=1, source_target_pairs={{8,48},{9,49},{10,50},{11,51},{12,52},{13,53},{14,54},{15,55},{72,... | collective-permute-start | bytes 2654216 | tf_op jit(solution)/shard_map/cond/branch_1_fun/ppermute | solution.py:21
  37.8 1.9 collective-permute-start.5
  39.7 4.5 %collective-permute-start.3 = (bf16[2,24,1152]{2,1,0:T(8,128)(2,1)S(1)}, bf16[2,24,1152]{2,1,0:T(8,128)(2,1)S(1)}, u32[]{:S(2)}, u32[]{:S(2)}) collective-permute-start(bf16[2,24,1152]{2,1,0:T(8,128)(2,1)S(1)} %get-tuple-element.185), channel_id=1, source_target_pairs={{0,68},{1,69},{2,70},{3,71},{4,0},{5,1},{6,2},{7,3},{8,76},{9,77},... | collective-permute-start | bytes 331784 | tf_op jit(solution)/shard_map/cond/branch_1_fun/ppermute | solution.py:31
  44.2 8.2 %collective-permute-done.3 = bf16[2,24,1152]{2,1,0:T(8,128)(2,1)S(1)} collective-permute-done((bf16[2,24,1152]{2,1,0:T(8,128)(2,1)S(1)}, bf16[2,24,1152]{2,1,0:T(8,128)(2,1)S(1)}, u32[]{:S(2)}, u32[]{:S(2)}) %collective-permute-start.3) | collective-permute-done | bytes 110624 | tf_op jit(solution)/shard_map/cond/branch_1_fun/ppermute | solution.py:31
  56.2 66.2 %conditional.6 = (bf16[1152,1152]{1,0:T(8,128)(2,1)}, bf16[384,1152]{1,0:T(8,128)(2,1)}, bf16[384,1152]{1,0:T(8,128)(2,1)}) conditional(s32[]{:T(128)} %convert_element_type.171, () %tuple.57, (s32[]{:T(128)}, s32[]{:T(128)}, bf16[8,24,1152]{2,1,0:T(8,128)(2,1)S(1)}, bf16[384,1152]{1,0:T(8,128)(2,1)}) %tuple.62), branch_computations={%region_3.4_spmd, %region_4.5_spmd} | conditional | flops 6635584 | bytes 33178548 | solution.py:94
  56.2 3.1 collective-permute-start.6
  59.3 4.4 %collective-permute-start.7 = (bf16[8,24,1152]{2,1,0:T(8,128)(2,1)S(1)}, bf16[8,24,1152]{2,1,0:T(8,128)(2,1)}, u32[]{:S(2)}, u32[]{:S(2)}) collective-permute-start(bf16[8,24,1152]{2,1,0:T(8,128)(2,1)S(1)} %get-tuple-element.102), channel_id=1, source_target_pairs={{0,256},{1,257},{2,258},{3,259},{4,260},{5,261},{6,262},{7,263},{8... | collective-permute-start | bytes 1327112 | tf_op jit(solution)/shard_map/cond/branch_1_fun/ppermute | solution.py:31
  63.7 3.1 collective-permute-start.8
  68.1 4.2 %collective-permute-done.7 = bf16[8,24,1152]{2,1,0:T(8,128)(2,1)} collective-permute-done((bf16[8,24,1152]{2,1,0:T(8,128)(2,1)S(1)}, bf16[8,24,1152]{2,1,0:T(8,128)(2,1)}, u32[]{:S(2)}, u32[]{:S(2)}) %collective-permute-start.7) | collective-permute-done | bytes 442400 | tf_op jit(solution)/shard_map/cond/branch_1_fun/ppermute | solution.py:31
  74.8 18.2 %collective-permute-start.9 = (bf16[8,72,1152]{2,1,0:T(8,128)(2,1)S(1)}, bf16[8,72,1152]{2,1,0:T(8,128)(2,1)}, u32[]{:S(2)}, u32[]{:S(2)}) collective-permute-start(bf16[8,72,1152]{2,1,0:T(8,128)(2,1)S(1)} %constant_dynamic-update-slice_fusion.2), channel_id=1, source_target_pairs={{0,8},{1,9},{2,10},{3,11},{4,12},{5,13},{6,14},{7,15},{8,0},{9,1},... | collective-permute-start | bytes 3981320 | tf_op jit(solution)/shard_map/cond/branch_1_fun/ppermute | solution.py:31
  93.0 1.9 collective-permute-start.10
  94.9 12.7 %collective-permute-done.10 = bf16[384,1152]{1,0:T(8,128)(2,1)} collective-permute-done((bf16[384,1152]{1,0:T(8,128)(2,1)}, bf16[384,1152]{1,0:T(8,128)(2,1)}, u32[]{:S(2)}, u32[]{:S(2)}) %collective-permute-start.10) | collective-permute-done | bytes 884768 | tf_op jit(solution)/shard_map/cond/branch_1_fun/ppermute | solution.py:21
  107.7 1.9 collective-permute-start.11
  112.9 9.5 %collective-permute-done.11 = bf16[384,1152]{1,0:T(8,128)(2,1)} collective-permute-done((bf16[384,1152]{1,0:T(8,128)(2,1)}, bf16[384,1152]{1,0:T(8,128)(2,1)}, u32[]{:S(2)}, u32[]{:S(2)}) %collective-permute-start.11) | collective-permute-done | bytes 884768 | tf_op jit(solution)/shard_map/cond/branch_1_fun/ppermute | solution.py:21
  123.1 3.6 %multiply_reduce_fusion.2 = (f32[384]{0:T(512)S(1)}, f32[1152,384]{0,1:T(8,128)S(1)}) fusion(bf16[384,1152]{1,0:T(8,128)(2,1)} %param.16, bf16[1152,1152]{1,0:T(8,128)(2,1)} %get-tuple-element.165), kind=kOutput, calls=%fused_computation.103 | convolution fusion | flops 1020100224 | bytes 5309952 | tf_op jit(solution)/shard_map/dot_general | solution.py:159
  131.7 35.4 %conditional.7 = (f32[8,72,1152]{2,1,0:T(8,128)S(1)}) conditional(s32[]{:T(128)} %convert_element_type.171, () %tuple.56, (f32[]{:T(128)}, s32[384]{0:T(512)}, s32[384]{0:T(512)S(1)}, s32[384]{0:T(512)S(1)}, s32[384]{0:T(512)S(1)}, /*index=5*/s32[384]{0:T(512)S(1)}, s32[384]{0:T(512)S(1)}, bf16[384,1152]{1,0:T(8,128)(2,1)}, ...), branch_computations={%region_6.7_spmd, %region_7.9_spmd} | conditional | flops 3754896384 | bytes 93851688 | solution.py:94
  137.9 3.2 fusion.7
  142.6 2.6 fusion.31
  145.9 1.8 convolution_add_fusion.2
  147.8 2.6 fusion.30
  153.2 2.0 convolution_add_fusion.1
  156.3 1.9 convolution_convert_fusion
  159.8 1.9 collective-permute-start.24
  161.7 3.1 collective-permute-done.24
  164.9 2.0 convert_add_fusion
  168.7 2.2 broadcast_select_fusion.18
  172.2 55.6 %conditional.8 = (f32[8,24,384]{2,1,0:T(8,128)S(1)}) conditional(s32[]{:T(128)} %convert_element_type.171, () %tuple.55, (s32[]{:T(128)}, f32[8,72,1152]{2,1,0:T(8,128)S(1)}, s32[]{:T(128)}) %tuple.66), branch_computations={%region_9.10_spmd, %region_10.11_spmd} | conditional | flops 1769598 | bytes 18286156 | solution.py:94
  173.4 4.2 %collective-permute-start.14 = (bf16[8,24,1152]{2,1,0:T(8,128)(2,1)}, bf16[8,24,1152]{2,1,0:T(8,128)(2,1)}, u32[]{:S(2)}, u32[]{:S(2)}) collective-permute-start(bf16[8,24,1152]{2,1,0:T(8,128)(2,1)} %get-tuple-element.198), channel_id=1, source_target_pairs={{0,384},{1,385},{2,386},{3,387},{4,388},{5,389},{6,390},{7,391},{8... | collective-permute-start | bytes 1327112 | tf_op jit(solution)/shard_map/cond/branch_1_fun/ppermute | solution.py:31
  177.6 2.1 collective-permute-start.13
  179.7 2.3 collective-permute-start.12
  182.1 5.8 %collective-permute-done.14 = bf16[8,24,1152]{2,1,0:T(8,128)(2,1)} collective-permute-done((bf16[8,24,1152]{2,1,0:T(8,128)(2,1)}, bf16[8,24,1152]{2,1,0:T(8,128)(2,1)}, u32[]{:S(2)}, u32[]{:S(2)}) %collective-permute-start.14) | collective-permute-done | bytes 442400 | tf_op jit(solution)/shard_map/cond/branch_1_fun/ppermute | solution.py:31
  187.9 3.0 collective-permute-done.13
  191.0 6.4 %collective-permute-done.12 = bf16[8,24,1152]{2,1,0:T(8,128)(2,1)} collective-permute-done((bf16[8,24,1152]{2,1,0:T(8,128)(2,1)}, bf16[8,24,1152]{2,1,0:T(8,128)(2,1)}, u32[]{:S(2)}, u32[]{:S(2)}) %collective-permute-start.12) | collective-permute-done | bytes 442400 | tf_op jit(solution)/shard_map/cond/branch_1_fun/ppermute | solution.py:31
  199.8 15.8 %collective-permute-start.17 = (bf16[8,24,384]{2,1,0:T(8,128)(2,1)S(1)}, bf16[8,24,384]{2,1,0:T(8,128)(2,1)S(1)}, u32[]{:S(2)}, u32[]{:S(2)}) collective-permute-start(bf16[8,24,384]{2,1,0:T(8,128)(2,1)S(1)} %get-tuple-element.201), channel_id=1, source_target_pairs={{0,48},{1,49},{2,50},{3,51},{4,52},{5,53},{6,54},{7,55},{8,56},{9,... | collective-permute-start | bytes 442376 | tf_op jit(solution)/shard_map/cond/branch_1_fun/ppermute | solution.py:31
  215.6 3.4 %collective-permute-start.16 = (bf16[8,24,384]{2,1,0:T(8,128)(2,1)S(1)}, bf16[8,24,384]{2,1,0:T(8,128)(2,1)S(1)}, u32[]{:S(2)}, u32[]{:S(2)}) collective-permute-start(bf16[8,24,384]{2,1,0:T(8,128)(2,1)S(1)} %get-tuple-element.202), channel_id=1, source_target_pairs={{0,32},{1,33},{2,34},{3,35},{4,36},{5,37},{6,38},{7,39},{8,40},{9,... | collective-permute-start | bytes 442376 | tf_op jit(solution)/shard_map/cond/branch_1_fun/ppermute | solution.py:31
  219.0 2.8 collective-permute-start.15
  221.8 2.5 collective-permute-done.16
  224.3 2.4 collective-permute-done.15
  232.1 2.0 fusion.67
  234.1 41.6 %conditional.9 = (bf16[24,384]{1,0:T(8,128)(2,1)S(1)}) conditional(s32[]{:T(128)} %convert_element_type.171, () %tuple.54, (f32[8,24,384]{2,1,0:T(8,128)S(1)}, s32[]{:T(128)}) %tuple.110), branch_computations={%region_11.12_spmd, %region_12.13_spmd} | conditional | flops 147528 | bytes 1659820 | solution.py:94
  234.2 10.2 %collective-permute-start.18 = (bf16[4,24,384]{2,1,0:T(8,128)(2,1)S(1)}, bf16[4,24,384]{2,1,0:T(8,128)(2,1)S(1)}, u32[]{:S(2)}, u32[]{:S(2)}) collective-permute-start(bf16[4,24,384]{2,1,0:T(8,128)(2,1)S(1)} %fusion.34), channel_id=1, source_target_pairs={{0,4},{1,5},{2,6},{3,7},{4,0},{5,1},{6,2},{7,3},{8,12},{9,13},{10,... | collective-permute-start | bytes 221192 | tf_op jit(solution)/shard_map/cond/branch_1_fun/ppermute | solution.py:31
  244.5 3.1 collective-permute-done.18
  247.6 8.8 %collective-permute-start.19 = (bf16[2,24,384]{2,1,0:T(8,128)(2,1)S(1)}, bf16[2,24,384]{2,1,0:T(8,128)(2,1)S(1)}, u32[]{:S(2)}, u32[]{:S(2)}) collective-permute-start(bf16[2,24,384]{2,1,0:T(8,128)(2,1)S(1)} %fusion.35), channel_id=1, source_target_pairs={{0,2},{1,3},{2,0},{3,1},{4,6},{5,7},{6,4},{7,5},{8,10},{9,11},{10,... | collective-permute-start | bytes 110600 | tf_op jit(solution)/shard_map/cond/branch_1_fun/ppermute | solution.py:31
  257.8 1.9 collective-permute-start.20
  259.7 2.6 collective-permute-done.20
  262.3 2.1 collective-permute-start.21
  264.3 11.4 %collective-permute-done.21 = f32[24,384]{1,0:T(8,128)S(1)} collective-permute-done((f32[24,384]{1,0:T(8,128)S(1)}, f32[24,384]{1,0:T(8,128)S(1)}, u32[]{:S(2)}, u32[]{:S(2)}) %collective-permute-start.21) | collective-permute-done | bytes 36896 | tf_op jit(solution)/shard_map/cond/branch_1_fun/ppermute | solution.py:31
  275.8 1.8 fusion.74
  277.7 7.1 %collective-permute-start.31 = (bf16[392,1152]{1,0:T(8,128)(2,1)S(1)}, bf16[392,1152]{1,0:T(8,128)(2,1)S(1)}, u32[]{:S(2)}, u32[]{:S(2)}) collective-permute-start(bf16[392,1152]{1,0:T(8,128)(2,1)S(1)} %broadcast_select_fusion.16), channel_id=1, source_target_pairs={{0,8},{8,16},{16,24},{24,32},{32,40},{40,48},{48,56},{1,9},{9,17},... | collective-permute-start | bytes 2709512 | tf_op jit(solution)/shard_map/ppermute | solution.py:21
  285.6 2.0 collective-permute-start.32
  287.6 2.0 fusion.66
  289.6 6.2 %collective-permute-done.32 = bf16[1,24,384]{2,1,0:T(8,128)(2,1)S(1)} collective-permute-done((bf16[1,24,384]{2,1,0:T(8,128)(2,1)S(1)}, bf16[1,24,384]{2,1,0:T(8,128)(2,1)S(1)}, u32[]{:S(2)}, u32[]{:S(2)}) %collective-permute-start.32) | collective-permute-done | bytes 18464 | tf_op jit(solution)/shard_map/ppermute | solution.py:31
  295.8 1.9 collective-permute-start.33
  299.5 2.5 collective-permute-done.33
  302.1 1.9 collective-permute-start.34
  304.0 2.9 collective-permute-done.34
  307.0 3.4 %collective-permute-start.35 = (bf16[2,24,1152]{2,1,0:T(8,128)(2,1)S(1)}, bf16[2,24,1152]{2,1,0:T(8,128)(2,1)S(1)}, u32[]{:S(2)}, u32[]{:S(2)}) collective-permute-start(bf16[2,24,1152]{2,1,0:T(8,128)(2,1)S(1)} %pad_maximum_fusion.6), channel_id=1, source_target_pairs={{0,256},{1,257},{2,258},{3,259},{4,260},{5,261},{6,262},{7,263},{8... | collective-permute-start | bytes 331784 | tf_op jit(solution)/shard_map/ppermute | solution.py:31
  311.2 2.8 collective-permute-done.35
  314.1 1.9 collective-permute-start.36
  (141 shorter events, 58.2 us)
Async XLA Ops:
  4.3 50.7 %copy-start.11 = (s32[384]{0:T(512)S(1)}, s32[384]{0:T(512)}, u32[]{:S(2)}) copy-start(s32[384]{0:T(512)} %param.19) | copy-start | bytes 4612
  5.1 5.9 %collective-permute-start = (bf16[1,24,1152]{2,1,0:T(8,128)(2,1)S(1)}, bf16[1,24,1152]{2,1,0:T(8,128)(2,1)S(1)}, u32[]{:S(2)}, u32[]{:S(2)}) collective-permute-start(bf16[1,24,1152]{2,1,0:T(8,128)(2,1)S(1)} %dynamic-slice_bitcast_fusion), channel_id=1, source_target_pairs={{0,1},{1,0},{2,3},{3,2},{4,5},{5,4},{6,7},{7,6},{8,9},{9,8},{10,11... | collective-permute-start | bytes 165896 | tf_op jit(solution)/shard_map/cond/branch_1_fun/ppermute | solution.py:31
  11.9 7.0 %collective-permute-start.1 = (bf16[2,24,1152]{2,1,0:T(8,128)(2,1)S(1)}, bf16[2,24,1152]{2,1,0:T(8,128)(2,1)S(1)}, u32[]{:S(2)}, u32[]{:S(2)}) collective-permute-start(bf16[2,24,1152]{2,1,0:T(8,128)(2,1)S(1)} %pad_maximum_fusion.2), channel_id=1, source_target_pairs={{0,2},{1,3},{2,0},{3,1},{4,6},{5,7},{6,4},{7,5},{8,10},{9,11},{10,... | collective-permute-start | bytes 331784 | tf_op jit(solution)/shard_map/cond/branch_1_fun/ppermute | solution.py:31
  19.0 25.2 %collective-permute-start.2 = (bf16[2,24,1152]{2,1,0:T(8,128)(2,1)S(1)}, bf16[2,24,1152]{2,1,0:T(8,128)(2,1)S(1)}, u32[]{:S(2)}, u32[]{:S(2)}) collective-permute-start(bf16[2,24,1152]{2,1,0:T(8,128)(2,1)S(1)} %get-tuple-element.186), channel_id=1, source_target_pairs={{0,4},{1,5},{2,6},{3,7},{4,64},{5,65},{6,66},{7,67},{8,12},{9,13},... | collective-permute-start | bytes 331784 | tf_op jit(solution)/shard_map/cond/branch_1_fun/ppermute | solution.py:31
  27.8 24.8 %collective-permute-start.4 = (bf16[384,1152]{1,0:T(8,128)(2,1)S(1)}, bf16[384,1152]{1,0:T(8,128)(2,1)}, u32[]{:S(2)}, u32[]{:S(2)}) collective-permute-start(bf16[384,1152]{1,0:T(8,128)(2,1)S(1)} %get-tuple-element.100), channel_id=1, source_target_pairs={{8,48},{9,49},{10,50},{11,51},{12,52},{13,53},{14,54},{15,55},{72,... | collective-permute-start | bytes 2654216 | tf_op jit(solution)/shard_map/cond/branch_1_fun/ppermute | solution.py:21
  37.8 14.8 %collective-permute-start.5 = (bf16[384,1152]{1,0:T(8,128)(2,1)S(1)}, bf16[384,1152]{1,0:T(8,128)(2,1)}, u32[]{:S(2)}, u32[]{:S(2)}) collective-permute-start(bf16[384,1152]{1,0:T(8,128)(2,1)S(1)} %get-tuple-element.100), channel_id=1, source_target_pairs={{8,0},{16,8},{24,16},{32,24},{40,32},{48,40},{56,48},{9,1},{17,9},... | collective-permute-start | bytes 2654216 | tf_op jit(solution)/shard_map/cond/branch_1_fun/ppermute | solution.py:21
  39.7 12.7 %collective-permute-start.3 = (bf16[2,24,1152]{2,1,0:T(8,128)(2,1)S(1)}, bf16[2,24,1152]{2,1,0:T(8,128)(2,1)S(1)}, u32[]{:S(2)}, u32[]{:S(2)}) collective-permute-start(bf16[2,24,1152]{2,1,0:T(8,128)(2,1)S(1)} %get-tuple-element.185), channel_id=1, source_target_pairs={{0,68},{1,69},{2,70},{3,71},{4,0},{5,1},{6,2},{7,3},{8,76},{9,77},... | collective-permute-start | bytes 331784 | tf_op jit(solution)/shard_map/cond/branch_1_fun/ppermute | solution.py:31
  52.6 70.5 %collective-permute-start.25 = (bf16[384,1152]{1,0:T(8,128)(2,1)S(1)}, bf16[384,1152]{1,0:T(8,128)(2,1)}, u32[]{:S(2)}, u32[]{:S(2)}) collective-permute-start(bf16[384,1152]{1,0:T(8,128)(2,1)S(1)} %fusion.95), channel_id=1, source_target_pairs={{0,504},{16,464},{1,505},{17,465},{2,506},{18,466},{3,507},{19,467... | collective-permute-start | bytes 2654216 | tf_op jit(solution)/shard_map/ppermute | solution.py:21
  54.3 68.8 %collective-permute-start.26 = (bf16[384,1152]{1,0:T(8,128)(2,1)}, bf16[384,1152]{1,0:T(8,128)(2,1)S(1)}, u32[]{:S(2)}, u32[]{:S(2)}) collective-permute-start(bf16[384,1152]{1,0:T(8,128)(2,1)} %get-tuple-element.164), channel_id=1, source_target_pairs={{48,496},{49,497},{50,498},{51,499},{52,500},{53,501},{54,502},{55... | collective-permute-start | bytes 2654216 | tf_op jit(solution)/shard_map/ppermute | solution.py:21
  56.2 10.8 %collective-permute-start.6 = (bf16[8,24,1152]{2,1,0:T(8,128)(2,1)S(1)}, bf16[8,24,1152]{2,1,0:T(8,128)(2,1)}, u32[]{:S(2)}, u32[]{:S(2)}) collective-permute-start(bf16[8,24,1152]{2,1,0:T(8,128)(2,1)S(1)} %get-tuple-element.102), channel_id=1, source_target_pairs={{0,128},{1,129},{2,130},{3,131},{4,132},{5,133},{6,134},{7,135},{8... | collective-permute-start | bytes 1327112 | tf_op jit(solution)/shard_map/cond/branch_1_fun/ppermute | solution.py:31
  59.3 13.0 %collective-permute-start.7 = (bf16[8,24,1152]{2,1,0:T(8,128)(2,1)S(1)}, bf16[8,24,1152]{2,1,0:T(8,128)(2,1)}, u32[]{:S(2)}, u32[]{:S(2)}) collective-permute-start(bf16[8,24,1152]{2,1,0:T(8,128)(2,1)S(1)} %get-tuple-element.102), channel_id=1, source_target_pairs={{0,256},{1,257},{2,258},{3,259},{4,260},{5,261},{6,262},{7,263},{8... | collective-permute-start | bytes 1327112 | tf_op jit(solution)/shard_map/cond/branch_1_fun/ppermute | solution.py:31
  63.7 10.1 %collective-permute-start.8 = (bf16[8,24,1152]{2,1,0:T(8,128)(2,1)S(1)}, bf16[8,24,1152]{2,1,0:T(8,128)(2,1)}, u32[]{:S(2)}, u32[]{:S(2)}) collective-permute-start(bf16[8,24,1152]{2,1,0:T(8,128)(2,1)S(1)} %get-tuple-element.102), channel_id=1, source_target_pairs={{0,384},{1,385},{2,386},{3,387},{4,388},{5,389},{6,390},{7,391},{8... | collective-permute-start | bytes 1327112 | tf_op jit(solution)/shard_map/cond/branch_1_fun/ppermute | solution.py:31
  74.8 34.8 %collective-permute-start.9 = (bf16[8,72,1152]{2,1,0:T(8,128)(2,1)S(1)}, bf16[8,72,1152]{2,1,0:T(8,128)(2,1)}, u32[]{:S(2)}, u32[]{:S(2)}) collective-permute-start(bf16[8,72,1152]{2,1,0:T(8,128)(2,1)S(1)} %constant_dynamic-update-slice_fusion.2), channel_id=1, source_target_pairs={{0,8},{1,9},{2,10},{3,11},{4,12},{5,13},{6,14},{7,15},{8,0},{9,1},... | collective-permute-start | bytes 3981320 | tf_op jit(solution)/shard_map/cond/branch_1_fun/ppermute | solution.py:31
  93.0 14.7 %collective-permute-start.10 = (bf16[384,1152]{1,0:T(8,128)(2,1)}, bf16[384,1152]{1,0:T(8,128)(2,1)}, u32[]{:S(2)}, u32[]{:S(2)}) collective-permute-start(bf16[384,1152]{1,0:T(8,128)(2,1)} %get-tuple-element.104), channel_id=1, source_target_pairs={{8,0},{16,8},{24,16},{32,24},{40,32},{48,40},{56,48},{9,1},{17,9},... | collective-permute-start | bytes 2654216 | tf_op jit(solution)/shard_map/cond/branch_1_fun/ppermute | solution.py:21
  107.7 14.7 %collective-permute-start.11 = (bf16[384,1152]{1,0:T(8,128)(2,1)}, bf16[384,1152]{1,0:T(8,128)(2,1)}, u32[]{:S(2)}, u32[]{:S(2)}) collective-permute-start(bf16[384,1152]{1,0:T(8,128)(2,1)} %collective-permute-done.10), channel_id=1, source_target_pairs={{8,0},{16,8},{24,16},{32,24},{40,32},{48,40},{56,48},{9,1},{17,9},... | collective-permute-start | bytes 2654216 | tf_op jit(solution)/shard_map/cond/branch_1_fun/ppermute | solution.py:21
  128.1 0.9 copy-start.1
  130.0 37.0 %collective-permute-start.27 = (bf16[392,1152]{1,0:T(8,128)(2,1)}, bf16[392,1152]{1,0:T(8,128)(2,1)}, u32[]{:S(2)}, u32[]{:S(2)}) collective-permute-start(bf16[392,1152]{1,0:T(8,128)(2,1)} %pad_maximum_fusion.4), channel_id=1, source_target_pairs={{56,120},{40,104},{48,0},{57,121},{41,105},{49,1},{58,122},{42,106... | collective-permute-start | bytes 2709512 | tf_op jit(solution)/shard_map/ppermute | solution.py:21
  131.7 1.8 copy-start.9
  131.7 4.4 %copy-start.8 = (s32[384]{0:T(512)S(1)}, s32[384]{0:T(512)}, u32[]{:S(2)}) copy-start(s32[384]{0:T(512)} %get-tuple-element.106) | copy-start | bytes 4612 | tf_op jit(solution)/shard_map/cond
  131.7 16.1 %collective-permute-start.23 = (bf16[384,1152]{1,0:T(8,128)(2,1)}, bf16[384,1152]{1,0:T(8,128)(2,1)}, u32[]{:S(2)}, u32[]{:S(2)}) collective-permute-start(bf16[384,1152]{1,0:T(8,128)(2,1)} %get-tuple-element.114), channel_id=1, source_target_pairs={{16,56},{56,40},{17,57},{57,41},{18,58},{58,42},{19,59},{59,43},{2... | collective-permute-start | bytes 2654216 | tf_op jit(solution)/shard_map/cond/branch_1_fun/ppermute | solution.py:21
  133.4 4.4 %copy-start.2 = (bf16[384,1152]{1,0:T(8,128)(2,1)S(1)}, bf16[384,1152]{1,0:T(8,128)(2,1)}, u32[]{:S(2)}) copy-start(bf16[384,1152]{1,0:T(8,128)(2,1)} %get-tuple-element.109) | copy-start | bytes 2654212 | tf_op jit(solution)/shard_map/cond
  134.5 13.3 %collective-permute-start.22 = (bf16[384,1152]{1,0:T(8,128)(2,1)}, bf16[384,1152]{1,0:T(8,128)(2,1)}, u32[]{:S(2)}, u32[]{:S(2)}) collective-permute-start(bf16[384,1152]{1,0:T(8,128)(2,1)} %broadcast_select_fusion.9), channel_id=1, source_target_pairs={{56,48},{48,56},{57,49},{49,57},{58,50},{50,58},{59,51},{51,59},{6... | collective-permute-start | bytes 2654216 | tf_op jit(solution)/shard_map/cond/branch_1_fun/ppermute | solution.py:21
  141.1 1.5 copy-start.14
  142.6 2.6 copy-start.10
  145.9 1.9 copy-start.13
  150.4 1.3 copy-start.12
  153.2 2.0 copy-start.3
  155.2 1.2 copy-start.15
  158.2 1.5 copy-start.5
  159.8 5.1 %collective-permute-start.24 = (bf16[8,72,1152]{2,1,0:T(8,128)(2,1)S(1)}, bf16[8,72,1152]{2,1,0:T(8,128)(2,1)}, u32[]{:S(2)}, u32[]{:S(2)}) collective-permute-start(bf16[8,72,1152]{2,1,0:T(8,128)(2,1)S(1)} %dynamic-slice_bitcast_fusion.1), channel_id=1, source_target_pairs={{0,8},{1,9},{2,10},{3,11},{4,12},{5,13},{6,14},{7,15},{8,0},{9,1},... | collective-permute-start | bytes 3981320 | tf_op jit(solution)/shard_map/cond/branch_1_fun/ppermute | solution.py:31
  167.1 60.6 %collective-permute-start.28 = (bf16[392,1152]{1,0:T(8,128)(2,1)}, bf16[392,1152]{1,0:T(8,128)(2,1)}, u32[]{:S(2)}, u32[]{:S(2)}) collective-permute-start(bf16[392,1152]{1,0:T(8,128)(2,1)} %collective-permute-done.27), channel_id=1, source_target_pairs={{0,64},{40,56},{1,65},{41,57},{2,66},{42,58},{3,67},{43,59},{4,68}... | collective-permute-start | bytes 2709512 | tf_op jit(solution)/shard_map/ppermute | solution.py:21
  170.9 56.8 %collective-permute-start.29 = (bf16[392,1152]{1,0:T(8,128)(2,1)}, bf16[392,1152]{1,0:T(8,128)(2,1)}, u32[]{:S(2)}, u32[]{:S(2)}) collective-permute-start(bf16[392,1152]{1,0:T(8,128)(2,1)} %broadcast_select_fusion.18), channel_id=1, source_target_pairs={{0,8},{8,16},{16,24},{24,32},{32,40},{40,48},{48,56},{56,0},{1,9},... | collective-permute-start | bytes 2709512 | tf_op jit(solution)/shard_map/ppermute | solution.py:21
  173.4 14.6 %collective-permute-start.14 = (bf16[8,24,1152]{2,1,0:T(8,128)(2,1)}, bf16[8,24,1152]{2,1,0:T(8,128)(2,1)}, u32[]{:S(2)}, u32[]{:S(2)}) collective-permute-start(bf16[8,24,1152]{2,1,0:T(8,128)(2,1)} %get-tuple-element.198), channel_id=1, source_target_pairs={{0,384},{1,385},{2,386},{3,387},{4,388},{5,389},{6,390},{7,391},{8... | collective-permute-start | bytes 1327112 | tf_op jit(solution)/shard_map/cond/branch_1_fun/ppermute | solution.py:31
  177.6 13.4 %collective-permute-start.13 = (bf16[8,24,1152]{2,1,0:T(8,128)(2,1)}, bf16[8,24,1152]{2,1,0:T(8,128)(2,1)}, u32[]{:S(2)}, u32[]{:S(2)}) collective-permute-start(bf16[8,24,1152]{2,1,0:T(8,128)(2,1)} %get-tuple-element.199), channel_id=1, source_target_pairs={{0,256},{1,257},{2,258},{3,259},{4,260},{5,261},{6,262},{7,263},{8... | collective-permute-start | bytes 1327112 | tf_op jit(solution)/shard_map/cond/branch_1_fun/ppermute | solution.py:31
  179.7 17.6 %collective-permute-start.12 = (bf16[8,24,1152]{2,1,0:T(8,128)(2,1)}, bf16[8,24,1152]{2,1,0:T(8,128)(2,1)}, u32[]{:S(2)}, u32[]{:S(2)}) collective-permute-start(bf16[8,24,1152]{2,1,0:T(8,128)(2,1)} %get-tuple-element.197), channel_id=1, source_target_pairs={{0,128},{1,129},{2,130},{3,131},{4,132},{5,133},{6,134},{7,135},{8... | collective-permute-start | bytes 1327112 | tf_op jit(solution)/shard_map/cond/branch_1_fun/ppermute | solution.py:31
  198.8 0.9 copy-start.4
  199.8 22.0 %collective-permute-start.17 = (bf16[8,24,384]{2,1,0:T(8,128)(2,1)S(1)}, bf16[8,24,384]{2,1,0:T(8,128)(2,1)S(1)}, u32[]{:S(2)}, u32[]{:S(2)}) collective-permute-start(bf16[8,24,384]{2,1,0:T(8,128)(2,1)S(1)} %get-tuple-element.201), channel_id=1, source_target_pairs={{0,48},{1,49},{2,50},{3,51},{4,52},{5,53},{6,54},{7,55},{8,56},{9,... | collective-permute-start | bytes 442376 | tf_op jit(solution)/shard_map/cond/branch_1_fun/ppermute | solution.py:31
  215.6 8.8 %collective-permute-start.16 = (bf16[8,24,384]{2,1,0:T(8,128)(2,1)S(1)}, bf16[8,24,384]{2,1,0:T(8,128)(2,1)S(1)}, u32[]{:S(2)}, u32[]{:S(2)}) collective-permute-start(bf16[8,24,384]{2,1,0:T(8,128)(2,1)S(1)} %get-tuple-element.202), channel_id=1, source_target_pairs={{0,32},{1,33},{2,34},{3,35},{4,36},{5,37},{6,38},{7,39},{8,40},{9,... | collective-permute-start | bytes 442376 | tf_op jit(solution)/shard_map/cond/branch_1_fun/ppermute | solution.py:31
  219.0 7.7 %collective-permute-start.15 = (bf16[8,24,384]{2,1,0:T(8,128)(2,1)S(1)}, bf16[8,24,384]{2,1,0:T(8,128)(2,1)S(1)}, u32[]{:S(2)}, u32[]{:S(2)}) collective-permute-start(bf16[8,24,384]{2,1,0:T(8,128)(2,1)S(1)} %get-tuple-element.200), channel_id=1, source_target_pairs={{0,16},{1,17},{2,18},{3,19},{4,20},{5,21},{6,22},{7,23},{8,24},{9,... | collective-permute-start | bytes 442376 | tf_op jit(solution)/shard_map/cond/branch_1_fun/ppermute | solution.py:31
  227.7 0.7 copy-start.6
  229.7 47.8 %collective-permute-start.30 = (bf16[392,1152]{1,0:T(8,128)(2,1)S(1)}, bf16[392,1152]{1,0:T(8,128)(2,1)S(1)}, u32[]{:S(2)}, u32[]{:S(2)}) collective-permute-start(bf16[392,1152]{1,0:T(8,128)(2,1)S(1)} %broadcast_select_fusion.17), channel_id=1, source_target_pairs={{0,8},{8,16},{16,24},{24,32},{32,40},{40,48},{48,56},{56,0},{1,9},... | collective-permute-start | bytes 2709512 | tf_op jit(solution)/shard_map/ppermute | solution.py:21
  232.1 2.0 copy-start.7
  234.2 13.3 %collective-permute-start.18 = (bf16[4,24,384]{2,1,0:T(8,128)(2,1)S(1)}, bf16[4,24,384]{2,1,0:T(8,128)(2,1)S(1)}, u32[]{:S(2)}, u32[]{:S(2)}) collective-permute-start(bf16[4,24,384]{2,1,0:T(8,128)(2,1)S(1)} %fusion.34), channel_id=1, source_target_pairs={{0,4},{1,5},{2,6},{3,7},{4,0},{5,1},{6,2},{7,3},{8,12},{9,13},{10,... | collective-permute-start | bytes 221192 | tf_op jit(solution)/shard_map/cond/branch_1_fun/ppermute | solution.py:31
  247.6 10.1 %collective-permute-start.19 = (bf16[2,24,384]{2,1,0:T(8,128)(2,1)S(1)}, bf16[2,24,384]{2,1,0:T(8,128)(2,1)S(1)}, u32[]{:S(2)}, u32[]{:S(2)}) collective-permute-start(bf16[2,24,384]{2,1,0:T(8,128)(2,1)S(1)} %fusion.35), channel_id=1, source_target_pairs={{0,2},{1,3},{2,0},{3,1},{4,6},{5,7},{6,4},{7,5},{8,10},{9,11},{10,... | collective-permute-start | bytes 110600 | tf_op jit(solution)/shard_map/cond/branch_1_fun/ppermute | solution.py:31
  257.8 4.5 %collective-permute-start.20 = (bf16[1,24,384]{2,1,0:T(8,128)(2,1)S(1)}, bf16[1,24,384]{2,1,0:T(8,128)(2,1)S(1)}, u32[]{:S(2)}, u32[]{:S(2)}) collective-permute-start(bf16[1,24,384]{2,1,0:T(8,128)(2,1)S(1)} %dynamic-slice_convert_fusion.8), channel_id=1, source_target_pairs={{0,1},{1,0},{2,3},{3,2},{4,5},{5,4},{6,7},{7,6},{8,9},{9,8},{10,11... | collective-permute-start | bytes 55304 | tf_op jit(solution)/shard_map/cond/branch_1_fun/ppermute | solution.py:31
  262.3 13.5 %collective-permute-start.21 = (f32[24,384]{1,0:T(8,128)S(1)}, f32[24,384]{1,0:T(8,128)S(1)}, u32[]{:S(2)}, u32[]{:S(2)}) collective-permute-start(f32[24,384]{1,0:T(8,128)S(1)} %add_bitcast_fusion), channel_id=1, source_target_pairs={{0,64},{1,65},{2,66},{3,67},{4,68},{5,69},{6,70},{7,71},{8,72},{9,... | collective-permute-start | bytes 110600 | tf_op jit(solution)/shard_map/cond/branch_1_fun/ppermute | solution.py:31
  277.7 40.6 %collective-permute-start.31 = (bf16[392,1152]{1,0:T(8,128)(2,1)S(1)}, bf16[392,1152]{1,0:T(8,128)(2,1)S(1)}, u32[]{:S(2)}, u32[]{:S(2)}) collective-permute-start(bf16[392,1152]{1,0:T(8,128)(2,1)S(1)} %broadcast_select_fusion.16), channel_id=1, source_target_pairs={{0,8},{8,16},{16,24},{24,32},{32,40},{40,48},{48,56},{1,9},{9,17},... | collective-permute-start | bytes 2709512 | tf_op jit(solution)/shard_map/ppermute | solution.py:21
  285.6 10.2 %collective-permute-start.32 = (bf16[1,24,384]{2,1,0:T(8,128)(2,1)S(1)}, bf16[1,24,384]{2,1,0:T(8,128)(2,1)S(1)}, u32[]{:S(2)}, u32[]{:S(2)}) collective-permute-start(bf16[1,24,384]{2,1,0:T(8,128)(2,1)S(1)} %bitcast.138), channel_id=1, source_target_pairs={{0,16},{1,17},{2,18},{3,19},{4,20},{5,21},{6,22},{7,23},{8,24},{9,... | collective-permute-start | bytes 55304 | tf_op jit(solution)/shard_map/ppermute | solution.py:31
  295.8 6.2 %collective-permute-start.33 = (bf16[2,24,384]{2,1,0:T(8,128)(2,1)S(1)}, bf16[2,24,384]{2,1,0:T(8,128)(2,1)S(1)}, u32[]{:S(2)}, u32[]{:S(2)}) collective-permute-start(bf16[2,24,384]{2,1,0:T(8,128)(2,1)S(1)} %pad_maximum_fusion.7), channel_id=1, source_target_pairs={{0,32},{1,33},{2,34},{3,35},{4,36},{5,37},{6,38},{7,39},{8,40},{9,... | collective-permute-start | bytes 110600 | tf_op jit(solution)/shard_map/ppermute | solution.py:31
  302.1 4.9 %collective-permute-start.34 = (bf16[1,24,1152]{2,1,0:T(8,128)(2,1)S(1)}, bf16[1,24,1152]{2,1,0:T(8,128)(2,1)S(1)}, u32[]{:S(2)}, u32[]{:S(2)}) collective-permute-start(bf16[1,24,1152]{2,1,0:T(8,128)(2,1)S(1)} %maximum_bitcast_fusion), channel_id=1, source_target_pairs={{0,128},{1,129},{2,130},{3,131},{4,132},{5,133},{6,134},{7,135},{8... | collective-permute-start | bytes 165896 | tf_op jit(solution)/shard_map/ppermute | solution.py:31
  307.0 7.0 %collective-permute-start.35 = (bf16[2,24,1152]{2,1,0:T(8,128)(2,1)S(1)}, bf16[2,24,1152]{2,1,0:T(8,128)(2,1)S(1)}, u32[]{:S(2)}, u32[]{:S(2)}) collective-permute-start(bf16[2,24,1152]{2,1,0:T(8,128)(2,1)S(1)} %pad_maximum_fusion.6), channel_id=1, source_target_pairs={{0,256},{1,257},{2,258},{3,259},{4,260},{5,261},{6,262},{7,263},{8... | collective-permute-start | bytes 331784 | tf_op jit(solution)/shard_map/ppermute | solution.py:31
  314.1 3.3 %collective-permute-start.36 = (bf16[72,1152]{1,0:T(8,128)(2,1)S(1)}, bf16[72,1152]{1,0:T(8,128)(2,1)S(1)}, u32[]{:S(2)}, u32[]{:S(2)}) collective-permute-start(bf16[72,1152]{1,0:T(8,128)(2,1)S(1)} %pad_maximum_fusion.5), channel_id=1, source_target_pairs={{0,8},{1,9},{2,10},{3,11},{4,12},{5,13},{6,14},{7,15},{8,0},{9,1},... | collective-permute-start | bytes 497672 | tf_op jit(solution)/shard_map/ppermute | solution.py:31
  318.5 1.2 copy-start
